TPU v7x, 32 devices: a whole 2x2x4 slice. The times are simulated.
32 devices in a mesh: groups: 2 (over x), replica: 8 (over z, y), tensor: 2 (over core).
Axes of the slice: x: 2, y: 2, z: 4, core: 2. Of those that a mesh axis runs over, the one named last changes fastest.
Arguments:
- tokens: bfloat16 [2048, 5120], P(('groups', 'replica'), 'tensor'), parts along dimension 0, may hold values from -6 to 6
- cotangent: bfloat16 [2048, 512], P(('groups', 'replica'), 'tensor'), parts along dimension 0, may hold values from -6 to 6
- key_weight: bfloat16 [512, 5120], P('tensor'), may hold values from -0.078125 to 0.078125
- momentum: bfloat16 [16, 512, 5120], P(('groups', 'replica'), 'tensor'), parts along dimension 0, may hold values from -60 to 60
- indices: int32 [8, 80, 8], P('tensor'), may hold values from 0 to 4095, as said below
Outputs:
- keys: bfloat16 [2048, 512], P(('groups', 'replica'), 'tensor'), parts along dimension 0
- input_grad: bfloat16 [2048, 5120], P(('groups', 'replica'), 'tensor'), parts along dimension 0
- new_momentum: bfloat16 [16, 512, 5120], P(('groups', 'replica'), 'tensor'), parts along dimension 0
- update: bfloat16 [1024, 5120], P(('groups', 'tensor')), parts along dimension 0
- pooled: float32 [16, 80, 8], P(('groups', 'tensor')), parts along dimension 0
There are 2 independent parts, one for each index of `groups`. A program takes and returns all parts, laid end to end along the dimension named above; an argument that names none is the same for every part. Nothing has to cross between parts.
Inputs may be any that keep to these rules, and one draw needn't show every extreme that they name: `indices`: within a span the 8 positions are distinct.
All inputs are finite; a program needn't handle non-finite values.
Results may differ from a plain program's by a relative error of at most 0.001.
Values may be sent and summed in bfloat16 or wider, within the bound.
No kernel may reach another device: no remote copies, remote signals or barrier semaphores. Data moves between devices by JAX's collectives and lax.ppermute only.
A program may use at most 128 MiB of HBM per device.

v0:
```python
import jax
import jax.numpy as jnp
from jax import lax
from jax.sharding import PartitionSpec as P

SPAN = 64


decay_rate = 0.9


def dct_table(order):
    freq = jnp.arange(order, dtype=jnp.float32)[:, None]
    place = jnp.arange(order, dtype=jnp.float32)[None, :]
    scale = jnp.where(freq == 0, jnp.sqrt(1.0 / order), jnp.sqrt(2.0 / order))
    return scale * jnp.cos(jnp.pi * (2.0 * place + 1.0) * freq / (2.0 * order))


def table_rows(indices, table, side):
    first = jnp.take(table, indices // side, axis=0)
    second = jnp.take(table, indices % side, axis=0)
    return (first, second)


def select_coefs(field, first, second, side):
    rows, cols = field.shape
    blocks = field.reshape(rows // side, side, cols // side, side)
    partial_rows = jnp.einsum("ijta,iajb->ijtb", first, blocks, precision=lax.Precision.HIGHEST)
    return jnp.sum(partial_rows * second, axis=3)


def decode(coefs, first, second):
    blocks = jnp.einsum(
        "ijta,ijt,ijtb->iajb", first, coefs, second, precision=lax.Precision.HIGHEST
    )
    nrow, side, ncol, other = blocks.shape
    return blocks.reshape(nrow * side, ncol * other)


def shards(tokens, cotangent, key_weight, momentum, indices):
    table = dct_table(SPAN)
    first, second = table_rows(indices, table, SPAN)
    whole = lax.all_gather(tokens, "tensor", axis=1, tiled=True)
    keys = jnp.einsum("td,kd->tk", whole, key_weight, preferred_element_type=jnp.float32).astype(
        jnp.bfloat16
    )
    grad = jnp.einsum("tk,td->kd", cotangent, whole, preferred_element_type=jnp.float32)
    moved = decay_rate * momentum[0].astype(jnp.float32) + grad
    coefs = select_coefs(moved, first, second, SPAN)
    total = jnp.sum(lax.all_gather(coefs[None], "replica", axis=0, tiled=True), axis=0)
    partial_in = jnp.dot(cotangent, key_weight, preferred_element_type=jnp.float32)
    input_grad = lax.psum_scatter(partial_in, "tensor", scatter_dimension=1, tiled=True).astype(
        jnp.bfloat16
    )
    remain = (moved - decode(coefs, first, second)).astype(jnp.bfloat16)
    pooled = total / lax.axis_size("replica")
    update = decode(pooled, first, second).astype(jnp.bfloat16)
    return (keys, input_grad, remain[None], update, pooled)


def solution(mesh):
    placed = (
        P(("groups", "replica"), "tensor"),
        P(("groups", "replica"), "tensor"),
        P("tensor", None),
        P(("groups", "replica"), "tensor", None),
        P("tensor", None, None),
    )
    return jax.shard_map(
        shards,
        mesh=mesh,
        in_specs=placed,
        out_specs=(
            P(("groups", "replica"), "tensor"),
            P(("groups", "replica"), "tensor"),
            P(("groups", "replica"), "tensor", None),
            P(("groups", "tensor"), None),
            P(("groups", "tensor"), None, None),
        ),
        check_vma=False,
    )
```

profile of v0, /device:TPU:0, one launch (start us, length us, event | category | flops | bytes accessed | tf_op | source)
XLA Modules:
  0.0 184.7 jit_solution(4620052398755299848)
XLA Ops:
  7.2 0.0 copy-start
  7.2 0.0 all-gather.3.cloned.1.call-start
  7.2 0.7 all-gather.3.cloned.1.call-update
  7.9 0.0 reduce-scatter.2.cloned.1.call-start
  8.0 0.9 copy-done
  8.9 2.8 %fusion.31 = f32[128,5120]{1,0:T(8,128)} fusion(bf16[128,256]{1,0:T(8,128)(2,1)} %param.8, bf16[256,5120]{1,0:T(8,128)(2,1)S(1)} %copy-done), kind=kOutput, calls=%fused_computation.50 | convolution fusion | flops 335544320 | bytes 5308416 | tf_op jit(solution)/shard_map/dot_general | solution.py:51
  11.7 0.0 copy-start.2
  11.7 0.0 reduce-scatter.2.cloned.1.call-update
  11.8 0.7 copy-done.2
  12.5 0.1 copy.33
  12.6 0.1 copy.36
  12.8 0.1 copy.34
  12.9 0.1 reshape.65
  13.0 0.1 copy.37
  13.1 0.1 reshape.69
  13.3 0.1 cosine_multiply_fusion
  13.4 5.6 %gather_fusion.1 = f32[2560,64]{1,0:T(8,128)} fusion(f32[64,64]{1,0:T(8,128)S(1)} %cosine_multiply_fusion, s32[3072]{0:T(1024)S(1)} %pad_clamp_fusion), kind=kCustom, calls=%fused_computation.1.clone | custom fusion | bytes 1320960 | tf_op jit(solution)/shard_map/jit(_take)/gather | solution.py:21
  19.1 0.0 copy-start.1
  19.1 5.6 %gather_fusion = f32[2560,64]{1,0:T(8,128)} fusion(f32[64,64]{1,0:T(8,128)S(1)} %cosine_multiply_fusion, s32[3072]{0:T(1024)S(1)} %pad_clamp_fusion.1), kind=kCustom, calls=%fused_computation.clone | custom fusion | bytes 1320960 | tf_op jit(solution)/shard_map/jit(_take)/gather | solution.py:20
  24.7 0.0 all-gather.3.cloned.1.call-done
  24.7 0.0 copy-done.1
  24.7 5.3 %convolution_add_fusion = f32[256,5120]{1,0:T(8,128)} fusion(bf16[128,256]{1,0:T(8,128)(2,1)S(1)} %copy-done.1, bf16[128,5120]{1,0:T(8,128)(2,1)} %all-gather.3.cloned.1.call-done, bf16[1,256,5120]{2,1,0:T(8,128)(2,1)} %param.10), kind=kOutput, calls=%fused_computation.4 | convolution fusion | flops 339476480 | bytes 9240576 | tf_op jit(solution)/shard_map/tk,td->kd/dot_general | solution.py:47
  30.1 8.6 %reshape.42 = f32[4,64,80,64]{3,2,1,0:T(8,128)} reshape(f32[256,5120]{1,0:T(8,128)} %convolution_add_fusion) | data formatting | bytes 10485760 | tf_op jit(solution)/shard_map/reshape | solution.py:27
  38.7 15.6 %fusion.8 = f32[4,80,8]{2,1,0:T(8,128)S(1)} fusion(f32[4,64,80,64]{3,2,1,0:T(8,128)} %reshape.42, f32[4,80,8,64]{3,2,1,0:T(8,128)} %bitcast.21, f32[4,80,8,64]{3,2,1,0:T(8,128)} %bitcast.24, pred[4,80,8]{2,1,0:T(8,128)(4,1)S(1)} %copy.36, pred[4,80,8]{2,1,0:T(8,128)(4,1)S(1)} %copy.33), kind=kOutput, calls=%fused_computation.12 | convolution fusion | flops 126481920 | bytes 6568960 | tf_op jit(solution)/shard_map/ijta,iajb->ijtb/dot_general | solution.py:28
  54.3 0.1 copy.39
  54.4 32.6 %all-gather = f32[32,80,8]{1,2,0:T(8,128)S(1)} all-gather(f32[4,80,8]{1,2,0:T(8,128)S(1)} %copy.39), channel_id=2, replica_groups=mesh['groups'=2,'replica'=8,'tensor'=2] {'replica'}, dimensions={0}, use_global_device_ids=true | all-gather | bytes 92160 | tf_op jit(solution)/shard_map/all_gather | solution.py:50
  87.0 0.1 copy.43
  87.1 0.7 copy.42
  87.8 20.8 %convert_bitcast_fusion = bf16[4,64,80,64]{1,3,2,0:T(8,128)(2,1)} fusion(f32[4,80,8,64]{3,2,1,0:T(8,128)} %bitcast.22, f32[4,80,8,64]{3,2,1,0:T(8,128)} %bitcast.25, f32[4,80,8]{2,1,0:T(8,128)S(1)} %broadcast_multiply_fusion, pred[4,80,8]{2,1,0:T(8,128)(4,1)S(1)} %copy.36, pred[4,80,8]{2,1,0:T(8,128)(4,1)S(1)} %copy.33), kind=kOutput, calls=%fused_computation.5 | convolution fusion | flops 127631360 | bytes 3947520 | tf_op jit(solution)/shard_map/ijta,ijt,ijtb->iajb/dot_general | solution.py:33
  108.6 8.2 %copy.41 = bf16[4,64,80,64]{3,2,1,0:T(8,128)(2,1)} copy(bf16[4,64,80,64]{1,3,2,0:T(8,128)(2,1)} %convert_bitcast_fusion) | data formatting | bytes 5242880 | tf_op jit(solution)/shard_map/convert_element_type | solution.py:57
  116.8 7.7 %convert_element_type.28 = bf16[256,5120]{1,0:T(8,128)(2,1)} reshape(bf16[4,64,80,64]{3,2,1,0:T(8,128)(2,1)} %copy.41) | data formatting | bytes 5242880 | tf_op jit(solution)/shard_map/convert_element_type | solution.py:57
  124.5 21.4 %convolution_bitcast_fusion = f32[4,64,80,64]{1,3,2,0:T(8,128)} fusion(f32[4,80,8,64]{3,2,1,0:T(8,128)} %bitcast.23, f32[4,80,8,64]{3,2,1,0:T(8,128)} %bitcast.26, f32[4,80,8]{2,1,0:T(8,128)S(1)} %fusion.8, pred[4,80,8]{2,1,0:T(8,128)(4,1)S(1)} %copy.36, pred[4,80,8]{2,1,0:T(8,128)(4,1)S(1)} %copy.33), kind=kOutput, calls=%fused_computation.7 | convolution fusion | flops 126320640 | bytes 6568960 | tf_op jit(solution)/shard_map/ijta,ijt,ijtb->iajb/dot_general | solution.py:33
  145.8 11.3 %copy.38 = f32[4,64,80,64]{3,2,1,0:T(8,128)} copy(f32[4,64,80,64]{1,3,2,0:T(8,128)} %convolution_bitcast_fusion) | data formatting | bytes 10485760 | tf_op jit(solution)/shard_map/ijta,ijt,ijtb->iajb/transpose | solution.py:33
  157.2 9.3 %reshape.43 = f32[256,5120]{1,0:T(8,128)} reshape(f32[4,64,80,64]{3,2,1,0:T(8,128)} %copy.38) | data formatting | bytes 10485760 | tf_op jit(solution)/shard_map/reshape | solution.py:37
  166.5 2.9 %convolution_convert_fusion = bf16[128,256]{1,0:T(8,128)(2,1)} fusion(bf16[128,5120]{1,0:T(8,128)(2,1)} %all-gather.3.cloned.1.call-done, bf16[256,5120]{1,0:T(8,128)(2,1)S(1)} %copy-done), kind=kOutput, calls=%fused_computation.18 | convolution fusion | flops 335577088 | bytes 3997696 | tf_op jit(solution)/shard_map/td,kd->tk/dot_general | solution.py:44
  169.4 6.2 %fusion.2 = bf16[1,256,5120]{2,1,0:T(8,128)(2,1)} fusion(f32[256,5120]{1,0:T(8,128)} %convolution_add_fusion, f32[256,5120]{1,0:T(8,128)} %reshape.43), kind=kLoop, calls=%fused_computation.8 | loop fusion | flops 2621440 | bytes 13107200 | tf_op jit(solution)/shard_map/broadcast_in_dim | solution.py:58
  175.6 0.0 reduce-scatter.2.cloned.1.call-done
  175.6 2.2 %convert_element_type.23 = bf16[128,2560]{1,0:T(8,128)(2,1)} convert(f32[128,2560]{1,0:T(8,128)} %reduce-scatter.2.cloned.1.call-done) | non-fusion elementwise | flops 327680 | bytes 1966080 | tf_op jit(solution)/shard_map/convert_element_type | solution.py:52
  (6 shorter events, 0.1 us)
Async XLA Ops:
  7.2 1.7 copy-start
  7.2 17.5 %all-gather.3.cloned.1.call-start = ((), (), s32[]{:S(2)}) async-start(), calls=%async_computation.1 | async-start | bytes 1966080 | tf_op jit(solution)/shard_map/all_gather | solution.py:43
  7.9 167.7 %reduce-scatter.2.cloned.1.call-start = ((), (), s32[]{:S(2)}) async-start(), calls=%async_computation.2 | async-start | bytes 3932160 | tf_op jit(solution)/shard_map/reduce_scatter | solution.py:52
  11.7 0.7 copy-start.2
  19.1 5.7 %copy-start.1 = (bf16[128,256]{1,0:T(8,128)(2,1)S(1)}, bf16[128,256]{1,0:T(8,128)(2,1)}, u32[]{:S(2)}) copy-start(bf16[128,256]{1,0:T(8,128)(2,1)} %param.8) | copy-start | bytes 196612
Sparse Core Ops, SparseCore 0:
  9.6 12.1 all-gather.2
  24.0 11.3 reduce-scatter.1
where the time goes:
time: 186 us; the launch traced here: 185 us
  matrix products  68.9 us (37%)
  local copies, waits for them, and re-layouts  59.6 us (32%)
  blocking collectives  32.6 us (18%)
  between operations  14.1 us (8%)
  other arithmetic  8.65 us (5%)
    dot_general x2, matrix products, decode(): jnp.einsum('ijta,ijt,ijtb->iajb', first, coefs, second, precision=lax.Pre...  42.1 us
    all_gather x1, blocking collectives, shards(): lax.all_gather(coefs[None], 'replica', axis=0, tiled=True)  32.6 us
    convert_element_type x2, local copies, waits for them, and re-layouts, shards(): update = decode(pooled, first, second).astype(jnp.bfloat16)  15.9 us
    dot_general x1, matrix products, select_coefs(): jnp.einsum('ijta,iajb->ijtb', first, blocks, precision=lax.Precision.HIGH...  15.6 us
    transpose x1, local copies, waits for them, and re-layouts, decode(): jnp.einsum('ijta,ijt,ijtb->iajb', first, coefs, second, precision=lax.Pre...  11.3 us
    reshape x1, local copies, waits for them, and re-layouts, decode(): return blocks.reshape(nrow * side, ncol * other)  9.27 us
    reshape x1, local copies, waits for them, and re-layouts, select_coefs(): blocks = field.reshape(rows // side, side, cols // side, side)  8.62 us
    broadcast_in_dim x1, other arithmetic, shards(): return (keys, input_grad, remain[None], update, pooled)  6.21 us
  transfers between devices with their start and end apart: 2, of which 0 were waited for; matrix products, arithmetic and copies ran while one was open for 72% of the time, Pallas kernels for 0%

commit v1 on v0

v1 whole, which is shorter than its diff:
```python
import functools

import jax
import jax.numpy as jnp
import numpy as np
from jax import lax
from jax.experimental import pallas as pl
from jax.experimental.pallas import tpu as pltpu
from jax.sharding import PartitionSpec as P

SPAN = 64
GROUP = 4
SIDE = SPAN * GROUP
decay_rate = 0.9
bf16 = jnp.bfloat16
f32 = jnp.float32
VMEM = pltpu.VMEM


def split(x):
    hi = x.astype(bf16)
    return hi, (x - hi.astype(f32)).astype(bf16)


def tables():
    freq = np.arange(SPAN, dtype=np.float64)[:, None]
    place = np.arange(SPAN, dtype=np.float64)[None, :]
    scale = np.where(freq == 0, np.sqrt(1.0 / SPAN), np.sqrt(2.0 / SPAN))
    table = scale * np.cos(np.pi * (2.0 * place + 1.0) * freq / (2.0 * SPAN))
    block = np.kron(np.eye(GROUP), table)

    def parts(x):
        x = x.astype(np.float32)
        hi = x.astype(jnp.bfloat16)
        return hi, (x - hi.astype(np.float32)).astype(jnp.bfloat16)

    decayed = np.concatenate(parts(np.float32(decay_rate).astype(np.float64) * block), axis=1)
    plain = np.concatenate(parts(block), axis=1)
    back = np.concatenate(parts(block.T), axis=0)
    return decayed, plain, back


def mm(a, b):
    return jnp.dot(a, b, preferred_element_type=f32)


def mm_t(a, b):
    return lax.dot_general(a, b, (((1,), (1,)), ((), ())), preferred_element_type=f32)


def params(mib=16):
    return pltpu.CompilerParams(vmem_limit_bytes=mib * 2**20)


def vmem(x):
    return pltpu.with_memory_space_constraint(x, VMEM)


def whole(n):
    return [pl.BlockSpec(memory_space=VMEM)] * n


def plan_kernel(idx_ref, g_ref, decayed_ref, plain_ref, back_ref, sel_ref, selg_ref, lt_ref, sec_ref, gt_ref, tmp):
    blocks, kept = idx_ref.shape
    keep = kept // (GROUP * GROUP)
    tmp[...] = jnp.zeros(tmp.shape, jnp.int32)
    tmp[0:blocks, :] = idx_ref[...]
    idx = tmp[...]
    lane = lax.broadcasted_iota(jnp.int32, idx.shape, 1)
    a_row = (idx >> 6) + SPAN * (lane // (GROUP * keep))
    b_row = (idx & (SPAN - 1)) + SPAN * ((lane // keep) & (GROUP - 1))
    a_col, b_col = a_row.T, b_row.T
    gt = g_ref[...].astype(f32).T.astype(bf16)
    gt_ref[...] = gt
    plain = plain_ref[...]
    row_g = mm_t(plain[:, :SIDE], gt.T) + mm_t(plain[:, SIDE:], gt.T)
    row_hi, row_lo = split(row_g)
    row_tab = jnp.concatenate([decayed_ref[...], row_hi, row_lo], axis=1)
    lanes = lax.broadcasted_iota(jnp.int32, (kept, SIDE), 1)
    subs = lax.broadcasted_iota(jnp.int32, (SIDE, kept), 0)
    for j in range(blocks):
        one_a = jnp.where(lanes == a_col[:, j : j + 1], 1.0, 0.0).astype(bf16)
        one_b = jnp.where(lanes == b_col[:, j : j + 1], 1.0, 0.0).astype(bf16)
        one_t = jnp.where(subs == a_row[j : j + 1, :], 1.0, 0.0).astype(bf16)
        rows = mm(one_a, row_tab)
        sel_ref[j, 0:kept, :] = rows[:, :SIDE].astype(bf16)
        sel_ref[j, kept:, :] = rows[:, SIDE : 2 * SIDE].astype(bf16)
        tok = row_g.shape[1]
        selg_ref[j, 0:kept, :] = rows[:, 2 * SIDE : 2 * SIDE + tok].astype(bf16)
        selg_ref[j, kept:, :] = rows[:, 2 * SIDE + tok :].astype(bf16)
        cols = mm(one_b, plain)
        sec_ref[j] = cols[:, :SIDE] + cols[:, SIDE:]
        rev = mm(back_ref[...], one_t)
        lt_ref[j, :, 0:kept] = rev[:SIDE].astype(bf16)
        lt_ref[j, :, kept:] = rev[SIDE:].astype(bf16)


def plan(idx, g, tabs):
    blocks, kept = idx.shape
    tok, rows = g.shape
    return pl.pallas_call(
        plan_kernel,
        in_specs=whole(5),
        out_specs=whole(5),
        out_shape=[
            VMEM((blocks, 2 * kept, SIDE), bf16),
            VMEM((blocks, 2 * kept, tok), bf16),
            VMEM((blocks, SIDE, 2 * kept), bf16),
            VMEM((blocks, kept, SIDE), f32),
            VMEM((rows, tok), bf16),
        ],
        scratch_shapes=[pltpu.VMEM((kept, kept), jnp.int32)],
        compiler_params=params(),
        name="plan",
    )(idx, g, *tabs)


def pick(t_ref, own_ref, peer_ref, j, half):
    h, at = divmod(j, half)
    cols = slice(at * SIDE, (at + 1) * SIDE)
    return jnp.where(t_ref[0] == h, own_ref[:, cols], peer_ref[:, cols])


def select_kernel(t_ref, sel_ref, selg_ref, sec_ref, m_ref, own_ref, peer_ref, row_ref, col_ref):
    blocks, kept = sel_ref.shape[0], sel_ref.shape[1] // 2
    half = blocks // 2
    lane = lax.broadcasted_iota(jnp.int32, (kept, kept), 1)
    acc = jnp.zeros((kept, kept), f32)
    for j in range(blocks):
        x = pick(t_ref, own_ref, peer_ref, j, half)
        m = m_ref[:, j * SIDE : (j + 1) * SIDE]
        r = mm(sel_ref[j], m) + mm(selg_ref[j], x)
        r = (r[:kept] + r[kept:]) * sec_ref[j]
        acc = jnp.where(lane == j, jnp.sum(r, axis=1, keepdims=True), acc)
    col_ref[...] = acc
    row_ref[...] = acc.T[:blocks]


def select(t, sel, selg, sec, m, own, peer):
    blocks, kept = sel.shape[0], sel.shape[1] // 2
    return pl.pallas_call(
        select_kernel,
        in_specs=[pl.BlockSpec(memory_space=pltpu.SMEM)] + whole(6),
        out_specs=whole(2),
        out_shape=[VMEM((blocks, kept), f32), VMEM((kept, kept), f32)],
        compiler_params=params(),
        name="select",
    )(t, vmem(sel), vmem(selg), vmem(sec), vmem(m), vmem(own), vmem(peer))


def spread(lt, sec, c):
    hi, lo = split(sec * c)
    kept = hi.shape[0]
    return mm(lt, jnp.concatenate([hi, hi], axis=0)) + mm(lt[:, :kept], lo)


CHUNKS = 4


def remain_kernel(t_ref, lt_ref, sec_ref, gt_ref, m_ref, own_ref, peer_ref, col_ref, out_ref, buf, sems):
    blocks = lt_ref.shape[0]
    per = blocks // CHUNKS
    copies = []
    for j in range(blocks):
        x = pick(t_ref, own_ref, peer_ref, j, blocks // 2)
        cols = slice(j * SIDE, (j + 1) * SIDE)
        lt = lt_ref[j]
        kept = lt.shape[1] // 2
        hi, lo = split(sec_ref[j] * -col_ref[:, j : j + 1])
        moved = decay_rate * m_ref[:, cols].astype(f32)
        moved += mm(jnp.concatenate([lt[:, :kept], gt_ref[...]], axis=1), jnp.concatenate([lo, x], axis=0))
        moved += mm(lt, jnp.concatenate([hi, hi], axis=0))
        buf[:, cols] = moved.astype(bf16)
        if (j + 1) % per == 0:
            at = pl.ds((j + 1 - per) * SIDE, per * SIDE)
            copies.append(pltpu.make_async_copy(buf.at[:, at], out_ref.at[:, at], sems.at[j // per]))
            copies[-1].start()
    for copy in copies:
        copy.wait()


def remain(t, lt, sec, gt, m, own, peer, col):
    return pl.pallas_call(
        remain_kernel,
        in_specs=[pl.BlockSpec(memory_space=pltpu.SMEM)] + whole(7),
        out_specs=pl.BlockSpec(memory_space=pl.ANY),
        out_shape=jax.ShapeDtypeStruct(m.shape, bf16),
        scratch_shapes=[pltpu.VMEM(m.shape, bf16), pltpu.SemaphoreType.DMA((CHUNKS,))],
        compiler_params=params(),
        name="remain",
    )(t, vmem(lt), vmem(sec), vmem(gt), vmem(m), vmem(own), vmem(peer), vmem(col))


def update_kernel(scale, lt_ref, sec_ref, sum_ref, out_ref, mean_ref, buf, tmp, sems):
    blocks, kept = sum_ref.shape
    per = blocks // CHUNKS
    mean = sum_ref[...] * scale
    mean_ref[...] = mean
    tmp[...] = jnp.zeros(tmp.shape, f32)
    tmp[0:blocks, :] = mean
    col = tmp[...].T
    copies = []
    for j in range(blocks):
        cols = slice(j * SIDE, (j + 1) * SIDE)
        buf[:, cols] = spread(lt_ref[j], sec_ref[j], col[:, j : j + 1]).astype(bf16)
        if (j + 1) % per == 0:
            at = pl.ds((j + 1 - per) * SIDE, per * SIDE)
            copies.append(pltpu.make_async_copy(buf.at[:, at], out_ref.at[:, at], sems.at[j // per]))
            copies[-1].start()
    for copy in copies:
        copy.wait()


def update(lt, sec, total, replicas, shape):
    blocks, kept = total.shape
    return pl.pallas_call(
        functools.partial(update_kernel, 1.0 / replicas),
        in_specs=whole(3),
        out_specs=[pl.BlockSpec(memory_space=pl.ANY)] + whole(1),
        out_shape=[jax.ShapeDtypeStruct(shape, bf16), jax.ShapeDtypeStruct(total.shape, f32)],
        scratch_shapes=[
            pltpu.VMEM(shape, bf16),
            pltpu.VMEM((kept, kept), f32),
            pltpu.SemaphoreType.DMA((CHUNKS,)),
        ],
        compiler_params=params(),
        name="update",
    )(vmem(lt), vmem(sec), vmem(total))


def keys_kernel(t_ref, own_ref, peer_ref, w_ref, out_ref):
    width = own_ref.shape[1]
    t = t_ref[0]
    mine = pl.ds(pl.multiple_of(t * width, width), width)
    theirs = pl.ds(pl.multiple_of((1 - t) * width, width), width)
    out_ref[...] = (mm_t(own_ref[...], w_ref[:, mine]) + mm_t(peer_ref[...], w_ref[:, theirs])).astype(bf16)


def keys_of(t, own, peer, w):
    return pl.pallas_call(
        keys_kernel,
        in_specs=[pl.BlockSpec(memory_space=pltpu.SMEM)] + whole(3),
        out_specs=pl.BlockSpec(memory_space=VMEM),
        out_shape=jax.ShapeDtypeStruct((own.shape[0], w.shape[0]), bf16),
        compiler_params=params(),
        name="keys",
    )(t, vmem(own), vmem(peer), vmem(w))


def input_kernel(t_ref, own_ref, peer_ref, w_ref, wp_ref, out_ref):
    width = out_ref.shape[1]
    at = pl.ds(pl.multiple_of(t_ref[0] * width, width), width)
    out_ref[...] = (mm(own_ref[...], w_ref[:, at]) + mm(peer_ref[...], wp_ref[:, at])).astype(bf16)


def input_of(t, own, peer, w, wp):
    return pl.pallas_call(
        input_kernel,
        in_specs=[pl.BlockSpec(memory_space=pltpu.SMEM)] + whole(4),
        out_specs=pl.BlockSpec(memory_space=VMEM),
        out_shape=jax.ShapeDtypeStruct((own.shape[0], w.shape[1] // 2), bf16),
        compiler_params=params(),
        name="input_grad",
    )(t, vmem(own), vmem(peer), vmem(w), vmem(wp))


def replica_sum(x, n):
    if n & (n - 1):
        return lax.psum(x, "replica")
    step = 1
    while step < n:
        x = x + lax.ppermute(x, "replica", [(i, i ^ step) for i in range(n)])
        step *= 2
    return x


def shards(tokens, cotangent, key_weight, momentum, indices):
    replicas = lax.axis_size("replica")
    swap = [(0, 1), (1, 0)]
    t = lax.axis_index("tensor").astype(jnp.int32).reshape(1)
    peer = lax.ppermute(tokens, "tensor", swap)
    cot_peer = lax.ppermute(cotangent, "tensor", swap)
    w_peer = lax.ppermute(key_weight, "tensor", swap)
    m = momentum[0]
    nrow, ncol, keep = indices.shape
    blocks = ncol // GROUP
    idx = indices.reshape(nrow, blocks, GROUP, keep).transpose(1, 0, 2, 3).reshape(blocks, nrow * GROUP * keep)
    sel, selg, lt, sec, gt = plan(idx, cotangent, tables())
    row, col = select(t, sel, selg, sec, m, tokens, peer)
    total = replica_sum(row, replicas)
    remaining = remain(t, lt, sec, gt, m, tokens, peer, col)
    keys = keys_of(t, tokens, peer, key_weight)
    input_grad = input_of(t, cotangent, cot_peer, key_weight, w_peer)
    new_update, mean = update(lt, sec, total, replicas, m.shape)
    pooled = mean.reshape(blocks, nrow, GROUP, keep).transpose(1, 0, 2, 3).reshape(nrow, ncol, keep)
    return (keys, input_grad, remaining[None], new_update, pooled)


def solution(mesh):
    placed = (
        P(("groups", "replica"), "tensor"),
        P(("groups", "replica"), "tensor"),
        P("tensor", None),
        P(("groups", "replica"), "tensor", None),
        P("tensor", None, None),
    )
    return jax.shard_map(
        shards,
        mesh=mesh,
        in_specs=placed,
        out_specs=(
            P(("groups", "replica"), "tensor"),
            P(("groups", "replica"), "tensor"),
            P(("groups", "replica"), "tensor", None),
            P(("groups", "tensor"), None),
            P(("groups", "tensor"), None, None),
        ),
        check_vma=False,
    )
```

time: 186 us -> 37.4 us (0.20)
  matrix products: 68.9 us -> 0 us
  local copies, waits for them, and re-layouts: 59.6 us -> 8.57 us
  blocking collectives: 32.6 us -> 0 us
  Pallas kernels: 0 us -> 15.5 us
  between operations: 14.1 us -> 0.72 us
  starting transfers between devices: 0.08 us -> 8.78 us
  other arithmetic: 8.65 us -> 0.01 us
  waiting for transfers between devices: 0.7 us -> 3.36 us
    dot_general x6 -> x0, matrix products: 68.9 us -> none  [the longest x2 42.1 us: decode(): jnp.einsum('ijta,ijt,ijtb->iajb', first, coefs, second, precision=lax.Pre...]
    all_gather x1 -> x0, blocking collectives: 32.6 us -> none  [shards(): lax.all_gather(coefs[None], 'replica', axis=0, tiled=True)]
    reshape x2 -> x1, local copies, waits for them, and re-layouts: 17.9 us -> 0.06 us  [shards(): indices.reshape(nrow, blocks, GROUP, keep).transpose(1, 0, 2, 3)]
    convert_element_type x2 -> x0, local copies, waits for them, and re-layouts: 15.9 us -> none  [shards(): update = decode(pooled, first, second).astype(jnp.bfloat16)]
    pallas_call x0 -> x6, Pallas kernels: none -> 15.5 us  [the longest x1 3.55 us: plan(): pl.pallas_call(plan_kernel, in_specs=whole(5), out_specs=whole(5), out_sh...]
    gather x2 -> x0, local copies, waits for them, and re-layouts: 11.3 us -> none  [the longest x1 5.64 us: table_rows(): first = jnp.take(table, indices // side, axis=0)]
    transpose x1 -> x2, local copies, waits for them, and re-layouts: 11.3 us -> 0.33 us  [the longest x1 0.17 us: shards(): indices.reshape(nrow, blocks, GROUP, keep).transpose(1, 0, 2, 3)]
    ppermute x0 -> x6, starting transfers between devices: none -> 8.78 us  [the longest x3 7.75 us: replica_sum(): x = x + lax.ppermute(x, 'replica', [(i, i ^ step) for i in range(n)])]
  transfers between devices with their start and end apart: 2 -> 6, of which waited for: 0 -> 2; matrix products, arithmetic and copies ran while one was open for 72% -> 6% of each run, Pallas kernels for 0% -> 34%
where the time goes in v1:
time: 37.4 us; the launch traced here: 36.9 us
  Pallas kernels  15.5 us (41%)
  starting transfers between devices  8.78 us (23%)
  local copies, waits for them, and re-layouts  8.57 us (23%)
  waiting for transfers between devices  3.36 us (9%)
  between operations  0.72 us (2%)
    unnamed x20, local copies, waits for them, and re-layouts  8.07 us
    ppermute x3, starting transfers between devices, replica_sum(): x = x + lax.ppermute(x, 'replica', [(i, i ^ step) for i in range(n)])  7.75 us
    pallas_call x1, Pallas kernels, plan(): pl.pallas_call(plan_kernel, in_specs=whole(5), out_specs=whole(5), out_sh...  3.55 us
    ppermute x3, waiting for transfers between devices, replica_sum(): x = x + lax.ppermute(x, 'replica', [(i, i ^ step) for i in range(n)])  3.35 us
    pallas_call x1, Pallas kernels, input_of(): pl.pallas_call(input_kernel, in_specs=[pl.BlockSpec(memory_space=pltpu.SM...  3.1 us
    pallas_call x1, Pallas kernels, remain(): pl.pallas_call(remain_kernel, in_specs=[pl.BlockSpec(memory_space=pltpu.S...  2.83 us
    pallas_call x1, Pallas kernels, update(): pl.pallas_call(functools.partial(update_kernel, 1.0 / replicas), in_specs...  2.65 us
    pallas_call x1, Pallas kernels, select(): pl.pallas_call(select_kernel, in_specs=[pl.BlockSpec(memory_space=pltpu.S...  1.74 us
  transfers between devices with their start and end apart: 6, of which 2 were waited for; matrix products, arithmetic and copies ran while one was open for 6% of the time, Pallas kernels for 34%

profile of v1, /device:TPU:0, one launch (start us, length us, event | category | flops | bytes accessed | tf_op | source)
XLA Modules:
  0.0 36.9 jit_solution(6292948707454277576)
XLA Ops:
  0.6 0.5 %collective-permute-start.2 = (bf16[256,5120]{1,0:T(8,128)(2,1)}, bf16[256,5120]{1,0:T(8,128)(2,1)}, u32[]{:S(2)}, u32[]{:S(2)}) collective-permute-start(bf16[256,5120]{1,0:T(8,128)(2,1)} %w_ref.3), channel_id=1, source_target_pairs={{0,1},{1,0},{2,3},{3,2},{4,5},{5,4},{6,7},{7,6},{8,9},{9,8},{10,11... | collective-permute-start | bytes 7864328 | tf_op jit(solution)/shard_map/ppermute | solution.py:283
  1.1 0.1 collective-permute-start
  1.2 0.4 %collective-permute-start.1 = (bf16[128,256]{1,0:T(8,128)(2,1)}, bf16[128,256]{1,0:T(8,128)(2,1)S(1)}, u32[]{:S(2)}, u32[]{:S(2)}) collective-permute-start(bf16[128,256]{1,0:T(8,128)(2,1)} %g_ref.1), channel_id=1, source_target_pairs={{0,1},{1,0},{2,3},{3,2},{4,5},{5,4},{6,7},{7,6},{8,9},{9,8},{10,11... | collective-permute-start | bytes 196616 | tf_op jit(solution)/shard_map/ppermute | solution.py:282
  1.7 0.8 %copy.15 = s32[4,80,8]{2,1,0:T(8,128)S(1)} copy(s32[4,80,8]{1,2,0:T(8,128)} %param.12) | data formatting | bytes 20480 | tf_op args[4]
  2.5 0.2 copy.16
  2.6 0.1 copy.17.idx_ref
  2.7 0.0 copy-start.4
  2.7 0.9 %copy-done.4 = bf16[128,256]{1,0:T(8,128)(2,1)S(1)} copy-done((bf16[128,256]{1,0:T(8,128)(2,1)S(1)}, bf16[128,256]{1,0:T(8,128)(2,1)}, u32[]{:S(2)}) %copy-start.4) | copy-done | bytes 65560
  3.6 0.0 copy-start.6
  3.6 0.9 %copy-done.6 = bf16[512,256]{1,0:T(8,128)(2,1)S(1)} copy-done((bf16[512,256]{1,0:T(8,128)(2,1)S(1)}, bf16[512,256]{1,0:T(8,128)(2,1)}, u32[]{:S(2)}) %copy-start.6) | copy-done | bytes 262168
  4.5 0.0 copy-start.7
  4.5 0.9 %copy-done.7 = bf16[256,512]{1,0:T(8,128)(2,1)S(1)} copy-done((bf16[256,512]{1,0:T(8,128)(2,1)S(1)}, bf16[256,512]{1,0:T(8,128)(2,1)}, u32[]{:S(2)}) %copy-start.7) | copy-done | bytes 262168
  5.5 0.0 copy-start.8
  5.5 0.9 %copy-done.8 = bf16[256,512]{1,0:T(8,128)(2,1)S(1)} copy-done((bf16[256,512]{1,0:T(8,128)(2,1)S(1)}, bf16[256,512]{1,0:T(8,128)(2,1)}, u32[]{:S(2)}) %copy-start.8) | copy-done | bytes 262168
  6.4 3.6 %plan.1 = (bf16[20,256,256]{2,1,0:T(8,128)(2,1)S(1)}, bf16[20,256,128]{2,1,0:T(8,128)(2,1)S(1)}, bf16[20,256,256]{2,1,0:T(8,128)(2,1)S(1)}, f32[20,128,256]{2,1,0:T(8,128)S(1)}, bf16[256,128]{1,0:T(8,128)(2,1)S(1)}) custom-call(s32[20,128]{1,0:T(8,128)S(1)} %copy.17.idx_ref, bf16[128,256]{1,0:T(8,128)(2,1)S(1)} %copy-done.4, bf16[256,512]{1,0:T(8,128)(2,1)S(1)} %copy-done.8, ...), custom_call_target="tpu_custom_call" | custom-call | tf_op jit(solution)/shard_map/plan/pallas_call | solution.py:101
  10.0 0.0 collective-permute-done.peer_ref
  10.0 0.0 copy-start.1
  10.0 1.7 %copy-done.1 = bf16[1,256,5120]{2,1,0:T(8,128)(2,1)S(1)} copy-done((bf16[1,256,5120]{2,1,0:T(8,128)(2,1)S(1)}, bf16[1,256,5120]{2,1,0:T(8,128)(2,1)}, u32[]{:S(2)}) %copy-start.1) | copy-done | bytes 2621464
  11.7 0.0 copy-start.3
  11.7 1.1 %copy-done.3 = bf16[128,2560]{1,0:T(8,128)(2,1)S(1)} copy-done((bf16[128,2560]{1,0:T(8,128)(2,1)S(1)}, bf16[128,2560]{1,0:T(8,128)(2,1)}, u32[]{:S(2)}) %copy-start.3) | copy-done | bytes 655384
  12.8 0.0 copy-start
  12.8 1.7 %select.1 = (f32[20,128]{1,0:T(8,128)S(1)}, f32[128,128]{1,0:T(8,128)S(1)}) custom-call(s32[1]{0:T(128)} %bitcast.t_ref, bf16[20,256,256]{2,1,0:T(8,128)(2,1)S(1)} %get-tuple-element.17.sel_ref, bf16[20,256,128]{2,1,0:T(8,128)(2,1)S(1)} %get-tuple-element.18.selg_ref, f32[20,128,256]{2,1,0:T(8,128)S(1)} %get-tuple-element.15.sec_ref, ...), custom_call_target="tpu_custom_call" | custom-call | tf_op jit(solution)/shard_map/select/pallas_call | solution.py:141
  14.6 0.0 copy-start.2
  14.6 2.6 %collective-permute-start.3 = (f32[20,128]{1,0:T(8,128)S(1)}, f32[20,128]{1,0:T(8,128)S(1)}, u32[]{:S(2)}, u32[]{:S(2)}) collective-permute-start(f32[20,128]{1,0:T(8,128)S(1)} %get-tuple-element.20), channel_id=1, source_target_pairs={{0,2},{2,0},{4,6},{6,4},{8,10},{10,8},{12,14},{14,12},{1,3},{3,1},... | collective-permute-start | bytes 30728 | tf_op jit(solution)/shard_map/ppermute | solution.py:272
  17.2 1.7 %collective-permute-done.3 = f32[20,128]{1,0:T(8,128)S(1)} collective-permute-done((f32[20,128]{1,0:T(8,128)S(1)}, f32[20,128]{1,0:T(8,128)S(1)}, u32[]{:S(2)}, u32[]{:S(2)}) %collective-permute-start.3) | collective-permute-done | bytes 10272 | tf_op jit(solution)/shard_map/ppermute | solution.py:272
  18.9 2.1 %collective-permute-start.4 = (f32[20,128]{1,0:T(8,128)S(1)}, f32[20,128]{1,0:T(8,128)S(1)}, u32[]{:S(2)}, u32[]{:S(2)}) collective-permute-start(f32[20,128]{1,0:T(8,128)S(1)} %add.9), channel_id=1, source_target_pairs={{0,4},{2,6},{4,0},{6,2},{8,12},{10,14},{12,8},{14,10},{1,5},{3,7},... | collective-permute-start | bytes 30728 | tf_op jit(solution)/shard_map/ppermute | solution.py:272
  21.0 1.7 %collective-permute-done.4 = f32[20,128]{1,0:T(8,128)S(1)} collective-permute-done((f32[20,128]{1,0:T(8,128)S(1)}, f32[20,128]{1,0:T(8,128)S(1)}, u32[]{:S(2)}, u32[]{:S(2)}) %collective-permute-start.4) | collective-permute-done | bytes 10272 | tf_op jit(solution)/shard_map/ppermute | solution.py:272
  22.6 3.0 %collective-permute-start.5 = (f32[20,128]{1,0:T(8,128)S(1)}, f32[20,128]{1,0:T(8,128)S(1)}, u32[]{:S(2)}, u32[]{:S(2)}) collective-permute-start(f32[20,128]{1,0:T(8,128)S(1)} %add.10), channel_id=1, source_target_pairs={{0,8},{2,10},{4,12},{6,14},{8,0},{10,2},{12,4},{14,6},{1,9},{3,11}... | collective-permute-start | bytes 30728 | tf_op jit(solution)/shard_map/ppermute | solution.py:272
  25.7 0.0 copy-done
  25.7 1.6 %keys.1 = bf16[128,256]{1,0:T(8,128)(2,1)} custom-call(s32[1]{0:T(128)} %bitcast.t_ref, bf16[128,2560]{1,0:T(8,128)(2,1)S(1)} %copy-done.3, bf16[128,2560]{1,0:T(8,128)(2,1)S(1)} %collective-permute-done.peer_ref, bf16[256,5120]{1,0:T(8,128)(2,1)S(1)} %copy-done), custom_call_target="tpu_custom_call" | custom-call | tf_op jit(solution)/shard_map/keys/pallas_call | solution.py:240
  27.3 0.0 copy-done.2
  27.3 2.8 %remain.1 = bf16[256,5120]{1,0:T(8,128)(2,1)} custom-call(s32[1]{0:T(128)} %bitcast.t_ref, bf16[20,256,256]{2,1,0:T(8,128)(2,1)S(1)} %get-tuple-element.14.lt_ref, f32[20,128,256]{2,1,0:T(8,128)S(1)} %get-tuple-element.15.sec_ref, bf16[256,128]{1,0:T(8,128)(2,1)S(1)} %get-tuple-element.16.gt_ref, bf16[256,5120]{1,0:T(8,128)(2,1)S(1)} %bitcast.12, ...), custom_call_target="tpu_custom_call" | custom-call | tf_op jit(solution)/shard_map/remain/pallas_call | solution.py:183
  30.2 0.0 collective-permute-done.5
  30.2 0.0 copy-start.5
  30.2 2.7 %update.1 = (bf16[256,5120]{1,0:T(8,128)(2,1)}, f32[20,128]{1,0:T(8,128)S(1)}) custom-call(bf16[20,256,256]{2,1,0:T(8,128)(2,1)S(1)} %get-tuple-element.14.lt_ref, f32[20,128,256]{2,1,0:T(8,128)S(1)} %get-tuple-element.15.sec_ref, f32[20,128]{1,0:T(8,128)S(1)} %add.11.sum_ref), custom_call_target="tpu_custom_call" | custom-call | tf_op jit(solution)/shard_map/update/pallas_call | solution.py:216
  32.8 0.1 copy.18
  33.0 0.2 copy.19
  33.1 0.7 %copy.20 = f32[4,80,8]{1,2,0:T(8,128)} copy(f32[4,80,8]{2,1,0:T(8,128)S(1)} %bitcast.14) | data formatting | bytes 20480
  33.8 0.0 collective-permute-done.1.peer_ref
  33.8 0.0 collective-permute-done.2.wp_ref
  33.8 0.0 copy-done.5
  33.8 3.1 %input_grad.1 = bf16[128,2560]{1,0:T(8,128)(2,1)} custom-call(s32[1]{0:T(128)} %bitcast.t_ref, bf16[128,256]{1,0:T(8,128)(2,1)S(1)} %copy-done.5, bf16[128,256]{1,0:T(8,128)(2,1)S(1)} %collective-permute-done.1.peer_ref, bf16[256,5120]{1,0:T(8,128)(2,1)S(1)} %copy-done, bf16[256,5120]{1,0:T(8,128)(2,1)} %collective-permute-done.2.wp_ref), custom_call_target="tpu_custom_call" | custom-call | tf_op jit(solution)/shard_map/input_grad/pallas_call | solution.py:257
  (3 shorter events, 0.0 us)
Async XLA Ops:
  0.6 33.2 %collective-permute-start.2 = (bf16[256,5120]{1,0:T(8,128)(2,1)}, bf16[256,5120]{1,0:T(8,128)(2,1)}, u32[]{:S(2)}, u32[]{:S(2)}) collective-permute-start(bf16[256,5120]{1,0:T(8,128)(2,1)} %w_ref.3), channel_id=1, source_target_pairs={{0,1},{1,0},{2,3},{3,2},{4,5},{5,4},{6,7},{7,6},{8,9},{9,8},{10,11... | collective-permute-start | bytes 7864328 | tf_op jit(solution)/shard_map/ppermute | solution.py:283
  1.1 8.8 %collective-permute-start = (bf16[128,2560]{1,0:T(8,128)(2,1)}, bf16[128,2560]{1,0:T(8,128)(2,1)S(1)}, u32[]{:S(2)}, u32[]{:S(2)}) collective-permute-start(bf16[128,2560]{1,0:T(8,128)(2,1)} %own_ref.7), channel_id=1, source_target_pairs={{0,1},{1,0},{2,3},{3,2},{4,5},{5,4},{6,7},{7,6},{8,9},{9,8},{10,11... | collective-permute-start | bytes 1966088 | tf_op jit(solution)/shard_map/ppermute | solution.py:281
  1.2 32.6 %collective-permute-start.1 = (bf16[128,256]{1,0:T(8,128)(2,1)}, bf16[128,256]{1,0:T(8,128)(2,1)S(1)}, u32[]{:S(2)}, u32[]{:S(2)}) collective-permute-start(bf16[128,256]{1,0:T(8,128)(2,1)} %g_ref.1), channel_id=1, source_target_pairs={{0,1},{1,0},{2,3},{3,2},{4,5},{5,4},{6,7},{7,6},{8,9},{9,8},{10,11... | collective-permute-start | bytes 196616 | tf_op jit(solution)/shard_map/ppermute | solution.py:282
  2.7 0.9 %copy-start.4 = (bf16[128,256]{1,0:T(8,128)(2,1)S(1)}, bf16[128,256]{1,0:T(8,128)(2,1)}, u32[]{:S(2)}) copy-start(bf16[128,256]{1,0:T(8,128)(2,1)} %g_ref.1) | copy-start | bytes 196612
  3.6 0.9 %copy-start.6 = (bf16[512,256]{1,0:T(8,128)(2,1)S(1)}, bf16[512,256]{1,0:T(8,128)(2,1)}, u32[]{:S(2)}) copy-start(bf16[512,256]{1,0:T(8,128)(2,1)} %constant.12.clone.back_ref) | copy-start | bytes 786436
  4.5 0.9 %copy-start.7 = (bf16[256,512]{1,0:T(8,128)(2,1)S(1)}, bf16[256,512]{1,0:T(8,128)(2,1)}, u32[]{:S(2)}) copy-start(bf16[256,512]{1,0:T(8,128)(2,1)} %constant.11.clone.plain_ref) | copy-start | bytes 786436
  5.5 0.9 %copy-start.8 = (bf16[256,512]{1,0:T(8,128)(2,1)S(1)}, bf16[256,512]{1,0:T(8,128)(2,1)}, u32[]{:S(2)}) copy-start(bf16[256,512]{1,0:T(8,128)(2,1)} %constant.10.clone.decayed_ref) | copy-start | bytes 786436
  10.0 1.7 %copy-start.1 = (bf16[1,256,5120]{2,1,0:T(8,128)(2,1)S(1)}, bf16[1,256,5120]{2,1,0:T(8,128)(2,1)}, u32[]{:S(2)}) copy-start(bf16[1,256,5120]{2,1,0:T(8,128)(2,1)} %param.11) | copy-start | bytes 7864324
  11.7 1.1 %copy-start.3 = (bf16[128,2560]{1,0:T(8,128)(2,1)S(1)}, bf16[128,2560]{1,0:T(8,128)(2,1)}, u32[]{:S(2)}) copy-start(bf16[128,2560]{1,0:T(8,128)(2,1)} %own_ref.7) | copy-start | bytes 1966084
  12.8 12.9 %copy-start = (bf16[256,5120]{1,0:T(8,128)(2,1)S(1)}, bf16[256,5120]{1,0:T(8,128)(2,1)}, u32[]{:S(2)}) copy-start(bf16[256,5120]{1,0:T(8,128)(2,1)} %w_ref.3) | copy-start | bytes 7864324
  14.6 12.7 %copy-start.2 = (bf16[1,256,5120]{2,1,0:T(8,128)(2,1)S(1)}, bf16[1,256,5120]{2,1,0:T(8,128)(2,1)}, u32[]{:S(2)}) copy-start(bf16[1,256,5120]{2,1,0:T(8,128)(2,1)} %param.11) | copy-start | bytes 7864324
  14.6 4.3 %collective-permute-start.3 = (f32[20,128]{1,0:T(8,128)S(1)}, f32[20,128]{1,0:T(8,128)S(1)}, u32[]{:S(2)}, u32[]{:S(2)}) collective-permute-start(f32[20,128]{1,0:T(8,128)S(1)} %get-tuple-element.20), channel_id=1, source_target_pairs={{0,2},{2,0},{4,6},{6,4},{8,10},{10,8},{12,14},{14,12},{1,3},{3,1},... | collective-permute-start | bytes 30728 | tf_op jit(solution)/shard_map/ppermute | solution.py:272
  18.9 3.7 %collective-permute-start.4 = (f32[20,128]{1,0:T(8,128)S(1)}, f32[20,128]{1,0:T(8,128)S(1)}, u32[]{:S(2)}, u32[]{:S(2)}) collective-permute-start(f32[20,128]{1,0:T(8,128)S(1)} %add.9), channel_id=1, source_target_pairs={{0,4},{2,6},{4,0},{6,2},{8,12},{10,14},{12,8},{14,10},{1,5},{3,7},... | collective-permute-start | bytes 30728 | tf_op jit(solution)/shard_map/ppermute | solution.py:272
  22.6 7.5 %collective-permute-start.5 = (f32[20,128]{1,0:T(8,128)S(1)}, f32[20,128]{1,0:T(8,128)S(1)}, u32[]{:S(2)}, u32[]{:S(2)}) collective-permute-start(f32[20,128]{1,0:T(8,128)S(1)} %add.10), channel_id=1, source_target_pairs={{0,8},{2,10},{4,12},{6,14},{8,0},{10,2},{12,4},{14,6},{1,9},{3,11}... | collective-permute-start | bytes 30728 | tf_op jit(solution)/shard_map/ppermute | solution.py:272
  30.2 3.7 %copy-start.5 = (bf16[128,256]{1,0:T(8,128)(2,1)S(1)}, bf16[128,256]{1,0:T(8,128)(2,1)}, u32[]{:S(2)}) copy-start(bf16[128,256]{1,0:T(8,128)(2,1)} %g_ref.1) | copy-start | bytes 196612

commit v2 on v0

v2 whole, which is shorter than its diff:
```python
import functools

import jax
import jax.numpy as jnp
import numpy as np
from jax import lax
from jax.experimental import pallas as pl
from jax.experimental.pallas import tpu as pltpu
from jax.sharding import PartitionSpec as P

SPAN = 64
GROUP = 4
SIDE = SPAN * GROUP
LANES = 128
ROWS = 16
decay_rate = 0.9
bf16 = jnp.bfloat16
f32 = jnp.float32
VMEM = pltpu.VMEM


def split(x):
    hi = x.astype(bf16)
    return hi, (x - hi.astype(f32)).astype(bf16)


def block_table():
    freq = np.arange(SPAN, dtype=np.float64)[:, None]
    place = np.arange(SPAN, dtype=np.float64)[None, :]
    scale = np.where(freq == 0, np.sqrt(1.0 / SPAN), np.sqrt(2.0 / SPAN))
    table = scale * np.cos(np.pi * (2.0 * place + 1.0) * freq / (2.0 * SPAN))
    return np.kron(np.eye(GROUP), table).astype(np.float32)


def mm(a, b):
    return jnp.dot(a, b, preferred_element_type=f32)


def mm_t(a, b):
    return lax.dot_general(a, b, (((1,), (1,)), ((), ())), preferred_element_type=f32)


def call(kernel, name, flops=0, nbytes=0, **kw):
    return pl.pallas_call(
        kernel,
        name=name,
        compiler_params=pltpu.CompilerParams(vmem_limit_bytes=8 * 2**20),
        cost_estimate=pl.CostEstimate(flops=flops, bytes_accessed=nbytes, transcendentals=0),
        **kw,
    )


def vmem(*xs):
    return [pltpu.with_memory_space_constraint(x, VMEM) for x in xs]


def hbm(*xs):
    return [pltpu.with_memory_space_constraint(x, pltpu.HBM) for x in xs]


def whole(n):
    return [pl.BlockSpec(memory_space=VMEM)] * n


def anywhere(n):
    return [pl.BlockSpec(memory_space=pl.ANY)] * n


SCALAR = pl.BlockSpec(memory_space=pltpu.SMEM)


def column(z, j):
    keep = z.shape[0] // GROUP
    parts = [
        jnp.broadcast_to(z[i * keep : (i + 1) * keep, c : c + 1], (keep, LANES))
        for i in range(GROUP)
        for c in range(j * GROUP, (j + 1) * GROUP)
    ]
    return jnp.concatenate(parts, axis=0)


def flat(ref):
    nrow, keep, ncol = ref.shape
    return ref[...].reshape(nrow * keep, ncol)


def plan_kernel(idx_ref, g_ref, tab_ref, m_hbm, x_hbm, sel_ref, sec_ref, lt_ref, gt_ref, m_ref, x_ref, sems):
    loads = [
        pltpu.make_async_copy(src, dst, sems.at[n])
        for n, (src, dst) in enumerate(((x_hbm, x_ref), (m_hbm, m_ref)))
    ]
    for load in loads:
        load.start()
    blocks, kept = sec_ref.shape[:2]
    per = kept // GROUP
    half = kept // 2
    z = flat(idx_ref)
    tab = tab_ref[...]
    hi, lo = split(tab)
    g = g_ref[...]
    gt_ref[...] = g.T
    row_g = (mm_t(hi, g) + mm_t(lo, g)) * (1.0 / decay_rate)
    ghi, glo = split(row_g)
    rhi, rlo = split(tab[:, :LANES] + tab[:, LANES:])
    row_tab = jnp.concatenate([rhi, ghi, rlo, glo], axis=1)
    chi, clo = split(tab[:SPAN, :LANES] + tab[SPAN : 2 * SPAN, :LANES])
    col_tab = jnp.concatenate([chi, clo], axis=0)
    lane = lax.broadcasted_iota(jnp.int32, (kept, LANES), 1)
    row = lax.broadcasted_iota(jnp.int32, (kept, LANES), 0)
    place = lane - SPAN * ((row // per) & 1)
    lane_in = lane & (SPAN - 1)
    mine = (lane // SPAN) == ((row // (per // GROUP)) & 1)
    none = jnp.zeros((half, LANES), bf16)
    for j in range(blocks):
        col = column(z, j)
        one = jnp.where((col >> 6) == place, 1.0, 0.0).astype(bf16)
        one_a = jnp.concatenate(
            [jnp.concatenate([one[:half], none], axis=1), jnp.concatenate([none, one[half:]], axis=1)], axis=0
        )
        rows = mm(one_a, row_tab).astype(bf16)
        for p in range(2):
            at = slice(p * half, (p + 1) * half)
            sel_ref[j, p, :half, :] = rows[at, :SIDE]
            sel_ref[j, p, half:, :] = rows[at, SIDE:]
            lt_ref[j, p] = jnp.concatenate([rows[at, :LANES], rows[at, SIDE : SIDE + LANES]], axis=0).T
        one_b = jnp.where((col & (SPAN - 1)) == lane_in, 1.0, 0.0).astype(bf16)
        sec_ref[j] = jnp.where(mine, mm(one_b, col_tab), 0.0)
    for load in loads:
        load.wait()


def plan(idx, g, tab, m, x):
    nrow, keep, ncol = idx.shape
    blocks, kept = ncol // GROUP, GROUP * GROUP * keep
    tok = g.shape[0]
    return call(
        plan_kernel,
        "plan",
        flops=2 * 10**9,
        nbytes=4 * 10**6,
        in_specs=whole(3) + anywhere(2),
        out_specs=whole(6),
        out_shape=[
            VMEM((blocks, 2, kept, LANES + tok), bf16),
            VMEM((blocks, kept, LANES), f32),
            VMEM((blocks, 2, LANES, kept), bf16),
            VMEM((g.shape[1], tok), bf16),
            VMEM(m.shape, bf16),
            VMEM(x.shape, bf16),
        ],
        scratch_shapes=[pltpu.SemaphoreType.DMA((2,))],
    )(*vmem(idx, g, tab), *hbm(m, x))


def pick(t_ref, own_ref, peer_ref, j, half):
    h, at = divmod(j, half)
    cols = slice(at * SIDE, (at + 1) * SIDE)
    return jnp.where(t_ref[0] == h, own_ref[:, cols], peer_ref[:, cols])


def select_kernel(t_ref, sel_ref, sec_ref, m_ref, own_ref, peer_ref, out_ref):
    blocks, kept = sec_ref.shape[:2]
    nrow, keep, ncol = out_ref.shape
    half = kept // 2
    lane = lax.broadcasted_iota(jnp.int32, (nrow * keep, LANES), 1)
    acc = jnp.zeros((nrow * keep, LANES), f32)
    for j in range(blocks):
        x = pick(t_ref, own_ref, peer_ref, j, blocks // 2)
        parts = []
        for p in range(2):
            m = m_ref[p * LANES : (p + 1) * LANES, j * SIDE : (j + 1) * SIDE]
            r = mm(sel_ref[j, p], jnp.concatenate([m, x], axis=0))
            for n in range(0, half, ROWS):
                at = slice(0, LANES) if (n // ROWS) % 2 == 0 else slice(LANES, SIDE)
                parts.append(r[n : n + ROWS, at] + r[half + n : half + n + ROWS, at])
        r = jnp.concatenate(parts, axis=0) * sec_ref[j]
        total = jnp.broadcast_to(jnp.sum(r, axis=1, keepdims=True), r.shape)
        for c in range(GROUP):
            parts = [total[(i * GROUP + c) * keep : (i * GROUP + c + 1) * keep] for i in range(nrow)]
            acc = jnp.where(lane == j * GROUP + c, jnp.concatenate(parts, axis=0), acc)
    out_ref[...] = (acc * decay_rate)[:, :ncol].reshape(nrow, keep, ncol)


def select(t, sel, sec, m, own, peer, shape):
    return call(
        select_kernel,
        "select",
        flops=10**9,
        nbytes=6 * 10**6,
        in_specs=[SCALAR] + whole(5),
        out_specs=whole(1)[0],
        out_shape=VMEM(shape, f32),
    )(t, *vmem(sel, sec, m, own, peer))


def decoded(lt, sec, col):
    parts = split(sec * col)
    half = sec.shape[0] // 2
    none = jnp.zeros((ROWS, LANES), bf16)
    outs = []
    for p in range(2):
        wide = []
        for part in parts:
            at = [part[n : n + ROWS] for n in range(p * half, (p + 1) * half, ROWS)]
            left = [a if n % 2 == 0 else none for n, a in enumerate(at)]
            right = [none if n % 2 == 0 else a for n, a in enumerate(at)]
            wide.append(jnp.concatenate([jnp.concatenate(left, axis=0), jnp.concatenate(right, axis=0)], axis=1))
        hi, lo = wide
        rhs = jnp.concatenate([hi, hi, lo, jnp.zeros_like(lo)], axis=0)
        outs.append(mm(jnp.concatenate([lt[p], lt[p]], axis=1), rhs))
    return outs


CHUNKS = 10


def store_block(j, blocks, buf, out_ref, sems, copies):
    per = blocks // CHUNKS
    if (j + 1) % per == 0:
        at = pl.ds((j + 1 - per) * SIDE, per * SIDE)
        copies.append(pltpu.make_async_copy(buf.at[:, at], out_ref.at[:, at], sems.at[j // per]))
        copies[-1].start()


def remain_kernel(t_ref, lt_ref, sec_ref, gt_ref, m_ref, own_ref, peer_ref, c_ref, out_ref, buf, sems):
    blocks = lt_ref.shape[0]
    copies = []
    c = -flat(c_ref)
    for j in range(blocks):
        x = pick(t_ref, own_ref, peer_ref, j, blocks // 2)
        cols = slice(j * SIDE, (j + 1) * SIDE)
        grad = mm(gt_ref[...], x)
        less = decoded(lt_ref[j], sec_ref[j], column(c, j))
        for p in range(2):
            at = slice(p * LANES, (p + 1) * LANES)
            moved = decay_rate * m_ref[at, cols].astype(f32) + grad[at]
            buf[at, cols] = (moved + less[p]).astype(bf16)
        store_block(j, blocks, buf, out_ref, sems, copies)
    for copy in copies:
        copy.wait()


def remain(t, lt, sec, gt, m, own, peer, c):
    return call(
        remain_kernel,
        "remain",
        flops=2 * 10**9,
        nbytes=8 * 10**6,
        in_specs=[SCALAR] + whole(7),
        out_specs=anywhere(1)[0],
        out_shape=jax.ShapeDtypeStruct(m.shape, bf16),
        scratch_shapes=[pltpu.VMEM(m.shape, bf16), pltpu.SemaphoreType.DMA((CHUNKS,))],
    )(t, *vmem(lt, sec, gt, m, own, peer, c))


def update_kernel(scale, lt_ref, sec_ref, sum_ref, out_ref, mean_ref, buf, mean, sems):
    blocks = lt_ref.shape[0]
    mean[...] = sum_ref[...] * scale
    copies = [pltpu.make_async_copy(mean, mean_ref, sems.at[CHUNKS])]
    copies[0].start()
    c = flat(mean)
    for j in range(blocks):
        out = decoded(lt_ref[j], sec_ref[j], column(c, j))
        for p in range(2):
            buf[p * LANES : (p + 1) * LANES, j * SIDE : (j + 1) * SIDE] = out[p].astype(bf16)
        store_block(j, blocks, buf, out_ref, sems, copies)
    for copy in copies:
        copy.wait()


def update(lt, sec, total, replicas, shape):
    return call(
        functools.partial(update_kernel, 1.0 / replicas),
        "update",
        flops=10**9,
        nbytes=6 * 10**6,
        in_specs=whole(3),
        out_specs=anywhere(2),
        out_shape=[jax.ShapeDtypeStruct(shape, bf16), jax.ShapeDtypeStruct(total.shape, f32)],
        scratch_shapes=[
            pltpu.VMEM(shape, bf16),
            pltpu.VMEM(total.shape, f32),
            pltpu.SemaphoreType.DMA((CHUNKS + 1,)),
        ],
    )(*vmem(lt, sec, total))


def halves(t_ref, width, at, size):
    t = t_ref[0]
    mine = pl.ds(pl.multiple_of(t * width + at, LANES), size)
    theirs = pl.ds(pl.multiple_of((1 - t) * width + at, LANES), size)
    return mine, theirs


def keys_kernel(t_ref, own_ref, peer_ref, w_ref, dep_ref, out_ref):
    mine, theirs = halves(t_ref, own_ref.shape[1], 0, own_ref.shape[1])
    out_ref[...] = (mm_t(own_ref[...], w_ref[:, mine]) + mm_t(peer_ref[...], w_ref[:, theirs])).astype(bf16)


def keys_of(t, own, peer, w, dep):
    return call(
        keys_kernel,
        "keys",
        flops=2 * own.shape[0] * w.shape[0] * w.shape[1],
        nbytes=4 * 10**6,
        in_specs=[SCALAR] + whole(3) + anywhere(1),
        out_specs=whole(1)[0],
        out_shape=jax.ShapeDtypeStruct((own.shape[0], w.shape[0]), bf16),
    )(t, *vmem(own, peer, w), dep)


def input_kernel(t_ref, own_ref, peer_ref, w_ref, wp_ref, dep_ref, out_ref, buf, sems):
    width = out_ref.shape[1]
    g = jnp.concatenate([own_ref[...], peer_ref[...]], axis=1)
    copies = []
    per = width // (sems.shape[0] * SIDE)
    for n, at in enumerate(range(0, width, SIDE)):
        mine, _ = halves(t_ref, width, at, SIDE)
        w = jnp.concatenate([w_ref[:, mine], wp_ref[:, mine]], axis=0)
        buf[:, at : at + SIDE] = mm(g, w).astype(bf16)
        if (n + 1) % per == 0:
            cols = pl.ds((n + 1 - per) * SIDE, per * SIDE)
            copies.append(pltpu.make_async_copy(buf.at[:, cols], out_ref.at[:, cols], sems.at[n // per]))
            copies[-1].start()
    for copy in copies:
        copy.wait()


def input_of(t, own, peer, w, wp, dep):
    shape = (own.shape[0], w.shape[1] // 2)
    return call(
        input_kernel,
        "input_grad",
        flops=2 * own.shape[0] * w.shape[0] * w.shape[1],
        nbytes=4 * 10**6,
        in_specs=[SCALAR] + whole(4) + anywhere(1),
        out_specs=anywhere(1)[0],
        out_shape=jax.ShapeDtypeStruct(shape, bf16),
        scratch_shapes=[pltpu.VMEM(shape, bf16), pltpu.SemaphoreType.DMA((5,))],
    )(t, *vmem(own, peer, w, wp), dep)


def shards(tokens, cotangent, key_weight, momentum, indices):
    replicas = lax.axis_size("replica")
    swap = [(0, 1), (1, 0)]
    t = lax.axis_index("tensor").astype(jnp.int32).reshape(1)
    peer = lax.ppermute(tokens, "tensor", swap)
    m = momentum[0]
    idx = indices.transpose(0, 2, 1)
    sel, sec, lt, gt, m_in, own = plan(idx, cotangent, block_table(), m, tokens)
    cot_peer = lax.ppermute(cotangent, "tensor", swap)
    w_peer = lax.ppermute(lax.optimization_barrier((key_weight, peer))[0], "tensor", swap)
    total = select(t, sel, sec, m_in, own, peer, idx.shape)
    mine = total

    def exchange(x, step):
        return lax.ppermute(x, "replica", [(i, i ^ step) for i in range(replicas)])

    steps = [1 << k for k in range(replicas.bit_length() - 1)]
    got = exchange(total, steps[0])
    keys = keys_of(t, own, peer, key_weight, total)
    total, keys = lax.optimization_barrier((total + got, keys))
    got = exchange(total, steps[1])
    input_grad = input_of(t, cotangent, cot_peer, key_weight, w_peer, total)
    total, input_grad = lax.optimization_barrier((total + got, input_grad))
    got = exchange(total, steps[2])
    remaining = remain(t, lt, sec, gt, m_in, own, peer, mine)
    total = total + got
    for step in steps[3:]:
        total = total + exchange(total, step)
    new_update, pooled = update(lt, sec, total, replicas, m.shape)
    return (keys, input_grad, remaining[None], new_update, pooled.transpose(0, 2, 1))


def solution(mesh):
    placed = (
        P(("groups", "replica"), "tensor"),
        P(("groups", "replica"), "tensor"),
        P("tensor", None),
        P(("groups", "replica"), "tensor", None),
        P("tensor", None, None),
    )
    return jax.shard_map(
        shards,
        mesh=mesh,
        in_specs=placed,
        out_specs=(
            P(("groups", "replica"), "tensor"),
            P(("groups", "replica"), "tensor"),
            P(("groups", "replica"), "tensor", None),
            P(("groups", "tensor"), None),
            P(("groups", "tensor"), None, None),
        ),
        check_vma=False,
    )
```

time: 186 us -> 26.6 us (0.14)
  matrix products: 68.9 us -> 0 us
  local copies, waits for them, and re-layouts: 59.6 us -> 2.52 us
  blocking collectives: 32.6 us -> 0 us
  between operations: 14.1 us -> 0.72 us
  Pallas kernels: 0 us -> 10.1 us
  starting transfers between devices: 0.08 us -> 9.16 us
  other arithmetic: 8.65 us -> 0.01 us
  waiting for transfers between devices: 0.7 us -> 3.74 us
    dot_general x6 -> x0, matrix products: 68.9 us -> none  [the longest x2 42.1 us: decode(): jnp.einsum('ijta,ijt,ijtb->iajb', first, coefs, second, precision=lax.Pre...]
    all_gather x1 -> x0, blocking collectives: 32.6 us -> none  [shards(): lax.all_gather(coefs[None], 'replica', axis=0, tiled=True)]
    reshape x2 -> x0, local copies, waits for them, and re-layouts: 17.9 us -> none  [the longest x1 9.27 us: decode(): return blocks.reshape(nrow * side, ncol * other)]
    convert_element_type x2 -> x0, local copies, waits for them, and re-layouts: 15.9 us -> none  [shards(): update = decode(pooled, first, second).astype(jnp.bfloat16)]
    transpose x1 -> x0, local copies, waits for them, and re-layouts: 11.3 us -> none  [decode(): jnp.einsum('ijta,ijt,ijtb->iajb', first, coefs, second, precision=lax.Pre...]
    gather x2 -> x0, local copies, waits for them, and re-layouts: 11.3 us -> none  [the longest x1 5.64 us: table_rows(): first = jnp.take(table, indices // side, axis=0)]
    pallas_call x0 -> x6, Pallas kernels: none -> 10.1 us  [the longest x1 2.41 us: remain(): call(remain_kernel, 'remain', flops=2 * 10 ** 9, nbytes=8 * 10 ** 6, in_s...]
    ppermute x0 -> x6, starting transfers between devices: none -> 9.16 us  [the longest x3 8.13 us: exchange(): return lax.ppermute(x, 'replica', [(i, i ^ step) for i in range(replicas)])]
  transfers between devices with their start and end apart: 2 -> 6, of which waited for: 0 -> 3; matrix products, arithmetic and copies ran while one was open for 72% -> 0% of each run, Pallas kernels for 0% -> 27%
where the time goes in v2:
time: 26.6 us; the launch traced here: 26.3 us
  Pallas kernels  10.1 us (38%)
  starting transfers between devices  9.16 us (34%)
  waiting for transfers between devices  3.74 us (14%)
  local copies, waits for them, and re-layouts  2.52 us (9%)
  between operations  0.72 us (3%)
    ppermute x3, starting transfers between devices, exchange(): return lax.ppermute(x, 'replica', [(i, i ^ step) for i in range(replicas)])  8.13 us
    unnamed x10, local copies, waits for them, and re-layouts  2.52 us
    pallas_call x1, Pallas kernels, remain(): call(remain_kernel, 'remain', flops=2 * 10 ** 9, nbytes=8 * 10 ** 6, in_s...  2.41 us
    pallas_call x1, Pallas kernels, plan(): call(plan_kernel, 'plan', flops=2 * 10 ** 9, nbytes=4 * 10 ** 6, in_specs...  1.97 us
    ppermute x1, waiting for transfers between devices, shards(): peer = lax.ppermute(tokens, 'tensor', swap)  1.93 us
    pallas_call x1, Pallas kernels, update(): call(functools.partial(update_kernel, 1.0 / replicas), 'update', flops=10...  1.91 us
    ppermute x3, waiting for transfers between devices, exchange(): return lax.ppermute(x, 'replica', [(i, i ^ step) for i in range(replicas)])  1.8 us
    pallas_call x1, Pallas kernels, keys_of(): call(keys_kernel, 'keys', flops=2 * own.shape[0] * w.shape[0] * w.shape[1...  1.63 us
  transfers between devices with their start and end apart: 6, of which 3 were waited for; matrix products, arithmetic and copies ran while one was open for 0% of the time, Pallas kernels for 27%

profile of v2, /device:TPU:0, one launch (start us, length us, event | category | flops | bytes accessed | tf_op | source)
XLA Modules:
  0.0 26.3 jit_solution(16600279897054558319)
XLA Ops:
  0.6 0.5 %collective-permute-start = (bf16[128,2560]{1,0:T(8,128)(2,1)}, bf16[128,2560]{1,0:T(8,128)(2,1)S(1)}, u32[]{:S(2)}, u32[]{:S(2)}) collective-permute-start(bf16[128,2560]{1,0:T(8,128)(2,1)} %x_hbm.1), channel_id=1, source_target_pairs={{0,1},{1,0},{2,3},{3,2},{4,5},{5,4},{6,7},{7,6},{8,9},{9,8},{10,11... | collective-permute-start | bytes 1966088 | tf_op jit(solution)/shard_map/ppermute | solution.py:347
  1.1 1.9 %collective-permute-done.peer_ref = bf16[128,2560]{1,0:T(8,128)(2,1)S(1)} collective-permute-done((bf16[128,2560]{1,0:T(8,128)(2,1)}, bf16[128,2560]{1,0:T(8,128)(2,1)S(1)}, u32[]{:S(2)}, u32[]{:S(2)}) %collective-permute-start) | collective-permute-done | bytes 655392 | tf_op jit(solution)/shard_map/ppermute | solution.py:347
  3.1 0.4 %collective-permute-start.4 = (bf16[256,5120]{1,0:T(8,128)(2,1)}, bf16[256,5120]{1,0:T(8,128)(2,1)S(1)}, u32[]{:S(2)}, u32[]{:S(2)}) collective-permute-start(bf16[256,5120]{1,0:T(8,128)(2,1)} %w_ref.3), channel_id=1, source_target_pairs={{0,1},{1,0},{2,3},{3,2},{4,5},{5,4},{6,7},{7,6},{8,9},{9,8},{10,11... | collective-permute-start | bytes 7864328 | tf_op jit(solution)/shard_map/ppermute | solution.py:352
  3.5 0.1 collective-permute-start.3
  3.6 0.0 copy-start.1
  3.6 0.8 %copy-done.1 = bf16[128,256]{1,0:T(8,128)(2,1)S(1)} copy-done((bf16[128,256]{1,0:T(8,128)(2,1)S(1)}, bf16[128,256]{1,0:T(8,128)(2,1)}, u32[]{:S(2)}) %copy-start.1) | copy-done | bytes 65560
  4.4 0.0 copy-start.3
  4.4 0.7 %copy-done.3 = s32[4,80,8]{1,2,0:T(8,128)S(1)} copy-done((s32[4,80,8]{1,2,0:T(8,128)S(1)}, s32[4,80,8]{1,2,0:T(8,128)}, u32[]{:S(2)}) %copy-start.3) | copy-done | bytes 10264
  5.2 0.0 copy-start.4
  5.2 0.9 %copy-done.4 = f32[256,256]{1,0:T(8,128)S(1)} copy-done((f32[256,256]{1,0:T(8,128)S(1)}, f32[256,256]{1,0:T(8,128)}, u32[]{:S(2)}) %copy-start.4) | copy-done | bytes 262168
  6.1 2.0 %plan.1 = (bf16[20,2,128,256]{3,2,1,0:T(8,128)(2,1)S(1)}, f32[20,128,128]{2,1,0:T(8,128)S(1)}, bf16[20,2,128,128]{3,2,1,0:T(8,128)(2,1)S(1)}, bf16[256,128]{1,0:...) custom-call(s32[4,8,80]{2,1,0:T(8,128)S(1)} %bitcast.5, bf16[128,256]{1,0:T(8,128)(2,1)S(1)} %copy-done.1, ...), custom_call_target="tpu_custom_call" | custom-call | flops 2000000000 | bytes 4000000 | tf_op jit(solution)/shard_map/plan/pallas_call | solution.py:136
  8.1 0.0 copy-start
  8.1 1.0 %select.1.dep_ref.c_ref = f32[4,8,80]{2,1,0:T(8,128)S(1)} custom-call(s32[1]{0:T(128)} %bitcast.t_ref, bf16[20,2,128,256]{3,2,1,0:T(8,128)(2,1)S(1)} %get-tuple-element.18.sel_ref, f32[20,128,128]{2,1,0:T(8,128)S(1)} %get-tuple-element.19.sec_ref, bf16[256,5120]{1,0:T(8,128)(2,1)S(1)} %get-tuple-element.20.m_ref, ...), custom_call_target="tpu_custom_call" | custom-call | flops 1000000000 | bytes 6000000 | tf_op jit(solution)/shard_map/select/pallas_call | solution.py:185
  9.1 0.0 copy-start.2
  9.1 3.0 %collective-permute-start.1 = (f32[4,8,80]{2,1,0:T(8,128)S(1)}, f32[4,8,80]{2,1,0:T(8,128)S(1)}, u32[]{:S(2)}, u32[]{:S(2)}) collective-permute-start(f32[4,8,80]{2,1,0:T(8,128)S(1)} %select.1.dep_ref.c_ref), channel_id=1, source_target_pairs={{0,2},{2,0},{4,6},{6,4},{8,10},{10,8},{12,14},{14,12},{1,3},{3,1},... | collective-permute-start | bytes 30728 | tf_op jit(solution)/shard_map/ppermute | solution.py:357
  12.0 0.0 copy-done
  12.1 1.6 %keys.1 = bf16[128,256]{1,0:T(8,128)(2,1)} custom-call(s32[1]{0:T(128)} %bitcast.t_ref, bf16[128,2560]{1,0:T(8,128)(2,1)S(1)} %get-tuple-element.21.own_ref, bf16[128,2560]{1,0:T(8,128)(2,1)S(1)} %collective-permute-done.peer_ref, bf16[256,5120]{1,0:T(8,128)(2,1)S(1)} %copy-done, f32[4,8,80]{2,1,0:T(8,128)S(1)} %select.1.dep_ref.c_ref), custom_call_target="tpu_custom_call" | custom-call | flops 335544320 | bytes 4000000 | tf_op jit(solution)/shard_map/keys/pallas_call | solution.py:301
  13.7 0.1 collective-permute-done.1
  13.8 2.1 %collective-permute-start.2 = (f32[4,8,80]{2,1,0:T(8,128)S(1)}, f32[4,8,80]{2,1,0:T(8,128)S(1)}, u32[]{:S(2)}, u32[]{:S(2)}) collective-permute-start(f32[4,8,80]{2,1,0:T(8,128)S(1)} %add.9.dep_ref), channel_id=1, source_target_pairs={{0,4},{2,6},{4,0},{6,2},{8,12},{10,14},{12,8},{14,10},{1,5},{3,7},... | collective-permute-start | bytes 30728 | tf_op jit(solution)/shard_map/ppermute | solution.py:357
  15.8 1.7 %collective-permute-done.2 = f32[4,8,80]{2,1,0:T(8,128)S(1)} collective-permute-done((f32[4,8,80]{2,1,0:T(8,128)S(1)}, f32[4,8,80]{2,1,0:T(8,128)S(1)}, u32[]{:S(2)}, u32[]{:S(2)}) %collective-permute-start.2) | collective-permute-done | bytes 10272 | tf_op jit(solution)/shard_map/ppermute | solution.py:357
  17.6 0.0 collective-permute-done.3.peer_ref
  17.6 0.0 collective-permute-done.4.wp_ref
  17.6 0.0 copy-done.2
  17.6 1.2 %input_grad.1 = bf16[128,2560]{1,0:T(8,128)(2,1)} custom-call(s32[1]{0:T(128)} %bitcast.t_ref, bf16[128,256]{1,0:T(8,128)(2,1)S(1)} %copy-done.2, bf16[128,256]{1,0:T(8,128)(2,1)S(1)} %collective-permute-done.3.peer_ref, bf16[256,5120]{1,0:T(8,128)(2,1)S(1)} %copy-done, bf16[256,5120]{1,0:T(8,128)(2,1)S(1)} %collective-permute-done.4.wp_ref, ...), custom_call_target="tpu_custom_call" | custom-call | flops 335544320 | bytes 4000000 | tf_op jit(solution)/shard_map/input_grad/pallas_call | solution.py:331
  18.9 3.1 %collective-permute-start.5 = (f32[4,8,80]{2,1,0:T(8,128)S(1)}, f32[4,8,80]{2,1,0:T(8,128)S(1)}, u32[]{:S(2)}, u32[]{:S(2)}) collective-permute-start(f32[4,8,80]{2,1,0:T(8,128)S(1)} %add.10), channel_id=1, source_target_pairs={{0,8},{2,10},{4,12},{6,14},{8,0},{10,2},{12,4},{14,6},{1,9},{3,11}... | collective-permute-start | bytes 30728 | tf_op jit(solution)/shard_map/ppermute | solution.py:357
  22.0 2.4 %remain.1 = bf16[256,5120]{1,0:T(8,128)(2,1)} custom-call(s32[1]{0:T(128)} %bitcast.t_ref, bf16[20,2,128,128]{3,2,1,0:T(8,128)(2,1)S(1)} %get-tuple-element.26.lt_ref, f32[20,128,128]{2,1,0:T(8,128)S(1)} %get-tuple-element.19.sec_ref, bf16[256,128]{1,0:T(8,128)(2,1)S(1)} %get-tuple-element.27.gt_ref, bf16[256,5120]{1,0:T(8,128)(2,1)S(1)} %get-tuple-element.20.m_ref, ...), custom_call_target="tpu_custom_call" | custom-call | flops 2000000000 | bytes 8000000 | tf_op jit(solution)/shard_map/remain/pallas_call | solution.py:244
  24.4 0.0 collective-permute-done.5
  24.4 1.9 %update.1 = (bf16[256,5120]{1,0:T(8,128)(2,1)}, f32[4,8,80]{2,1,0:T(8,128)}) custom-call(bf16[20,2,128,128]{3,2,1,0:T(8,128)(2,1)S(1)} %get-tuple-element.26.lt_ref, f32[20,128,128]{2,1,0:T(8,128)S(1)} %get-tuple-element.19.sec_ref, f32[4,8,80]{2,1,0:T(8,128)S(1)} %add.11.sum_ref), custom_call_target="tpu_custom_call" | custom-call | flops 1000000000 | bytes 6000000 | tf_op jit(solution)/shard_map/update/pallas_call | solution.py:272
  (3 shorter events, 0.0 us)
Async XLA Ops:
  0.6 2.5 %collective-permute-start = (bf16[128,2560]{1,0:T(8,128)(2,1)}, bf16[128,2560]{1,0:T(8,128)(2,1)S(1)}, u32[]{:S(2)}, u32[]{:S(2)}) collective-permute-start(bf16[128,2560]{1,0:T(8,128)(2,1)} %x_hbm.1), channel_id=1, source_target_pairs={{0,1},{1,0},{2,3},{3,2},{4,5},{5,4},{6,7},{7,6},{8,9},{9,8},{10,11... | collective-permute-start | bytes 1966088 | tf_op jit(solution)/shard_map/ppermute | solution.py:347
  3.1 14.5 %collective-permute-start.4 = (bf16[256,5120]{1,0:T(8,128)(2,1)}, bf16[256,5120]{1,0:T(8,128)(2,1)S(1)}, u32[]{:S(2)}, u32[]{:S(2)}) collective-permute-start(bf16[256,5120]{1,0:T(8,128)(2,1)} %w_ref.3), channel_id=1, source_target_pairs={{0,1},{1,0},{2,3},{3,2},{4,5},{5,4},{6,7},{7,6},{8,9},{9,8},{10,11... | collective-permute-start | bytes 7864328 | tf_op jit(solution)/shard_map/ppermute | solution.py:352
  3.5 14.1 %collective-permute-start.3 = (bf16[128,256]{1,0:T(8,128)(2,1)}, bf16[128,256]{1,0:T(8,128)(2,1)S(1)}, u32[]{:S(2)}, u32[]{:S(2)}) collective-permute-start(bf16[128,256]{1,0:T(8,128)(2,1)} %own_ref.1), channel_id=1, source_target_pairs={{0,1},{1,0},{2,3},{3,2},{4,5},{5,4},{6,7},{7,6},{8,9},{9,8},{10,11... | collective-permute-start | bytes 196616 | tf_op jit(solution)/shard_map/ppermute | solution.py:351
  3.6 0.8 %copy-start.1 = (bf16[128,256]{1,0:T(8,128)(2,1)S(1)}, bf16[128,256]{1,0:T(8,128)(2,1)}, u32[]{:S(2)}) copy-start(bf16[128,256]{1,0:T(8,128)(2,1)} %own_ref.1) | copy-start | bytes 196612
  4.4 0.7 %copy-start.3 = (s32[4,80,8]{1,2,0:T(8,128)S(1)}, s32[4,80,8]{1,2,0:T(8,128)}, u32[]{:S(2)}) copy-start(s32[4,80,8]{1,2,0:T(8,128)} %param.10) | copy-start | bytes 30724
  5.2 0.9 %copy-start.4 = (f32[256,256]{1,0:T(8,128)S(1)}, f32[256,256]{1,0:T(8,128)}, u32[]{:S(2)}) copy-start(f32[256,256]{1,0:T(8,128)} %constant.6.clone.tab_ref) | copy-start | bytes 786436
  8.1 4.0 %copy-start = (bf16[256,5120]{1,0:T(8,128)(2,1)S(1)}, bf16[256,5120]{1,0:T(8,128)(2,1)}, u32[]{:S(2)}) copy-start(bf16[256,5120]{1,0:T(8,128)(2,1)} %w_ref.3) | copy-start | bytes 7864324
  9.1 8.5 %copy-start.2 = (bf16[128,256]{1,0:T(8,128)(2,1)S(1)}, bf16[128,256]{1,0:T(8,128)(2,1)}, u32[]{:S(2)}) copy-start(bf16[128,256]{1,0:T(8,128)(2,1)} %own_ref.1) | copy-start | bytes 196612
  9.1 4.7 %collective-permute-start.1 = (f32[4,8,80]{2,1,0:T(8,128)S(1)}, f32[4,8,80]{2,1,0:T(8,128)S(1)}, u32[]{:S(2)}, u32[]{:S(2)}) collective-permute-start(f32[4,8,80]{2,1,0:T(8,128)S(1)} %select.1.dep_ref.c_ref), channel_id=1, source_target_pairs={{0,2},{2,0},{4,6},{6,4},{8,10},{10,8},{12,14},{14,12},{1,3},{3,1},... | collective-permute-start | bytes 30728 | tf_op jit(solution)/shard_map/ppermute | solution.py:357
  13.8 3.8 %collective-permute-start.2 = (f32[4,8,80]{2,1,0:T(8,128)S(1)}, f32[4,8,80]{2,1,0:T(8,128)S(1)}, u32[]{:S(2)}, u32[]{:S(2)}) collective-permute-start(f32[4,8,80]{2,1,0:T(8,128)S(1)} %add.9.dep_ref), channel_id=1, source_target_pairs={{0,4},{2,6},{4,0},{6,2},{8,12},{10,14},{12,8},{14,10},{1,5},{3,7},... | collective-permute-start | bytes 30728 | tf_op jit(solution)/shard_map/ppermute | solution.py:357
  18.9 5.5 %collective-permute-start.5 = (f32[4,8,80]{2,1,0:T(8,128)S(1)}, f32[4,8,80]{2,1,0:T(8,128)S(1)}, u32[]{:S(2)}, u32[]{:S(2)}) collective-permute-start(f32[4,8,80]{2,1,0:T(8,128)S(1)} %add.10), channel_id=1, source_target_pairs={{0,8},{2,10},{4,12},{6,14},{8,0},{10,2},{12,4},{14,6},{1,9},{3,11}... | collective-permute-start | bytes 30728 | tf_op jit(solution)/shard_map/ppermute | solution.py:357

commit v3 on v2

--- a/solution.py
+++ b/solution.py
@@ -24,12 +24,12 @@
     return hi, (x - hi.astype(f32)).astype(bf16)
 
 
-def block_table():
+def dct_table():
     freq = np.arange(SPAN, dtype=np.float64)[:, None]
     place = np.arange(SPAN, dtype=np.float64)[None, :]
     scale = np.where(freq == 0, np.sqrt(1.0 / SPAN), np.sqrt(2.0 / SPAN))
     table = scale * np.cos(np.pi * (2.0 * place + 1.0) * freq / (2.0 * SPAN))
-    return np.kron(np.eye(GROUP), table).astype(np.float32)
+    return np.tile(table, (1, LANES // SPAN)).astype(np.float32)
 
 
 def mm(a, b):
@@ -84,27 +84,33 @@
     return ref[...].reshape(nrow * keep, ncol)
 
 
-def plan_kernel(idx_ref, g_ref, tab_ref, m_hbm, x_hbm, sel_ref, sec_ref, lt_ref, gt_ref, m_ref, x_ref, sems):
-    loads = [
-        pltpu.make_async_copy(src, dst, sems.at[n])
-        for n, (src, dst) in enumerate(((x_hbm, x_ref), (m_hbm, m_ref)))
-    ]
+def plan_kernel(
+    idx_hbm, tab_hbm, g_hbm, x_hbm, m_hbm, sel_ref, sec_ref, lt_ref, gt_ref, m_ref, x_ref, idx_ref, tab_ref, g_ref, sems
+):
+    pairs = ((idx_hbm, idx_ref), (tab_hbm, tab_ref), (g_hbm, g_ref), (x_hbm, x_ref), (m_hbm, m_ref))
+    loads = [pltpu.make_async_copy(src, dst, sems.at[n]) for n, (src, dst) in enumerate(pairs)]
     for load in loads:
         load.start()
+    for load in loads[:3]:
+        load.wait()
     blocks, kept = sec_ref.shape[:2]
     per = kept // GROUP
     half = kept // 2
     z = flat(idx_ref)
-    tab = tab_ref[...]
-    hi, lo = split(tab)
+    chi, clo = split(tab_ref[...])
+    col_tab = jnp.concatenate([chi, clo], axis=0)
+    hi = jnp.concatenate([chi, chi], axis=0)
+    lo = jnp.concatenate([clo, clo], axis=0)
+    square = (LANES, LANES)
+    near = lax.broadcasted_iota(jnp.int32, square, 0) // SPAN == lax.broadcasted_iota(jnp.int32, square, 1) // SPAN
+    hi = jnp.where(near, hi, jnp.zeros_like(hi))
+    lo = jnp.where(near, lo, jnp.zeros_like(lo))
     g = g_ref[...]
     gt_ref[...] = g.T
-    row_g = (mm_t(hi, g) + mm_t(lo, g)) * (1.0 / decay_rate)
-    ghi, glo = split(row_g)
-    rhi, rlo = split(tab[:, :LANES] + tab[:, LANES:])
-    row_tab = jnp.concatenate([rhi, ghi, rlo, glo], axis=1)
-    chi, clo = split(tab[:SPAN, :LANES] + tab[SPAN : 2 * SPAN, :LANES])
-    col_tab = jnp.concatenate([chi, clo], axis=0)
+    row_g = [mm_t(hi, g[:, at : at + LANES]) + mm_t(lo, g[:, at : at + LANES]) for at in range(0, SIDE, LANES)]
+    ghi, glo = split(jnp.concatenate(row_g, axis=0) * (1.0 / decay_rate))
+    hi, lo = [jnp.concatenate([part, part], axis=0) for part in (hi, lo)]
+    row_tab = jnp.concatenate([hi, ghi, lo, glo], axis=1)
     lane = lax.broadcasted_iota(jnp.int32, (kept, LANES), 1)
     row = lax.broadcasted_iota(jnp.int32, (kept, LANES), 0)
     place = lane - SPAN * ((row // per) & 1)
@@ -125,7 +131,7 @@
             lt_ref[j, p] = jnp.concatenate([rows[at, :LANES], rows[at, SIDE : SIDE + LANES]], axis=0).T
         one_b = jnp.where((col & (SPAN - 1)) == lane_in, 1.0, 0.0).astype(bf16)
         sec_ref[j] = jnp.where(mine, mm(one_b, col_tab), 0.0)
-    for load in loads:
+    for load in loads[3:]:
         load.wait()
 
 
@@ -138,7 +144,7 @@
         "plan",
         flops=2 * 10**9,
         nbytes=4 * 10**6,
-        in_specs=whole(3) + anywhere(2),
+        in_specs=anywhere(5),
         out_specs=whole(6),
         out_shape=[
             VMEM((blocks, 2, kept, LANES + tok), bf16),
@@ -148,8 +154,13 @@
             VMEM(m.shape, bf16),
             VMEM(x.shape, bf16),
         ],
-        scratch_shapes=[pltpu.SemaphoreType.DMA((2,))],
-    )(*vmem(idx, g, tab), *hbm(m, x))
+        scratch_shapes=[
+            pltpu.VMEM(idx.shape, jnp.int32),
+            pltpu.VMEM(tab.shape, f32),
+            pltpu.VMEM(g.shape, bf16),
+            pltpu.SemaphoreType.DMA((5,)),
+        ],
+    )(*hbm(idx, tab, g, x, m))
 
 
 def pick(t_ref, own_ref, peer_ref, j, half):
@@ -347,9 +358,8 @@
     peer = lax.ppermute(tokens, "tensor", swap)
     m = momentum[0]
     idx = indices.transpose(0, 2, 1)
-    sel, sec, lt, gt, m_in, own = plan(idx, cotangent, block_table(), m, tokens)
+    sel, sec, lt, gt, m_in, own = plan(idx, cotangent, jnp.asarray(dct_table()), m, tokens)
     cot_peer = lax.ppermute(cotangent, "tensor", swap)
-    w_peer = lax.ppermute(lax.optimization_barrier((key_weight, peer))[0], "tensor", swap)
     total = select(t, sel, sec, m_in, own, peer, idx.shape)
     mine = total
 
@@ -359,13 +369,14 @@
     steps = [1 << k for k in range(replicas.bit_length() - 1)]
     got = exchange(total, steps[0])
     keys = keys_of(t, own, peer, key_weight, total)
-    total, keys = lax.optimization_barrier((total + got, keys))
+    total, keys, w_out = lax.optimization_barrier((total + got, keys, key_weight))
+    w_peer = lax.ppermute(w_out, "tensor", swap)
     got = exchange(total, steps[1])
+    remaining = remain(t, lt, sec, gt, m_in, own, peer, mine)
+    total, remaining, w_peer = lax.optimization_barrier((total + got, remaining, w_peer))
+    got = exchange(total, steps[2])
     input_grad = input_of(t, cotangent, cot_peer, key_weight, w_peer, total)
     total, input_grad = lax.optimization_barrier((total + got, input_grad))
-    got = exchange(total, steps[2])
-    remaining = remain(t, lt, sec, gt, m_in, own, peer, mine)
-    total = total + got
     for step in steps[3:]:
         total = total + exchange(total, step)
     new_update, pooled = update(lt, sec, total, replicas, m.shape)

time: 26.6 us -> 20.9 us (0.79)
  waiting for transfers between devices: 3.74 us -> 0.6 us
  local copies, waits for them, and re-layouts: 2.52 us -> 0.01 us
  Pallas kernels: 10.1 us -> 10.7 us
  starting transfers between devices: 9.16 us -> 8.66 us
    unnamed x10 -> x4, local copies, waits for them, and re-layouts: 2.52 us -> 0.01 us
    ppermute x1, waiting for transfers between devices: 1.93 us -> 0.01 us  [shards(): peer = lax.ppermute(tokens, 'tensor', swap)]
    ppermute x3, waiting for transfers between devices: 1.8 us -> 0.59 us  [exchange(): return lax.ppermute(x, 'replica', [(i, i ^ step) for i in range(replicas)])]
    pallas_call x1, Pallas kernels: 1.97 us -> 2.51 us  [plan(): call(plan_kernel, 'plan', flops=2 * 10 ** 9, nbytes=4 * 10 ** 6, in_specs...]
    ppermute x3, starting transfers between devices: 8.13 us -> 7.63 us  [exchange(): return lax.ppermute(x, 'replica', [(i, i ^ step) for i in range(replicas)])]
  transfers between devices with their start and end apart: 6 -> 6, of which waited for: 3 -> 2; matrix products, arithmetic and copies ran while one was open for 0% -> 0% of each run, Pallas kernels for 27% -> 38%
where the time goes in v3:
time: 20.9 us; the launch traced here: 20.7 us
  Pallas kernels  10.7 us (51%)
  starting transfers between devices  8.66 us (41%)
  between operations  0.71 us (3%)
  waiting for transfers between devices  0.6 us (3%)
    ppermute x3, starting transfers between devices, exchange(): return lax.ppermute(x, 'replica', [(i, i ^ step) for i in range(replicas)])  7.63 us
    pallas_call x1, Pallas kernels, plan(): call(plan_kernel, 'plan', flops=2 * 10 ** 9, nbytes=4 * 10 ** 6, in_specs...  2.51 us
    pallas_call x1, Pallas kernels, remain(): call(remain_kernel, 'remain', flops=2 * 10 ** 9, nbytes=8 * 10 ** 6, in_s...  2.43 us
    pallas_call x1, Pallas kernels, update(): call(functools.partial(update_kernel, 1.0 / replicas), 'update', flops=10...  1.9 us
    pallas_call x1, Pallas kernels, keys_of(): call(keys_kernel, 'keys', flops=2 * own.shape[0] * w.shape[0] * w.shape[1...  1.63 us
    pallas_call x1, Pallas kernels, input_of(): call(input_kernel, 'input_grad', flops=2 * own.shape[0] * w.shape[0] * w....  1.24 us
    pallas_call x1, Pallas kernels, select(): call(select_kernel, 'select', flops=10 ** 9, nbytes=6 * 10 ** 6, in_specs...  0.98 us
    ppermute x3, waiting for transfers between devices, exchange(): return lax.ppermute(x, 'replica', [(i, i ^ step) for i in range(replicas)])  0.59 us
  transfers between devices with their start and end apart: 6, of which 2 were waited for; matrix products, arithmetic and copies ran while one was open for 0% of the time, Pallas kernels for 38%

profile of v3, /device:TPU:0, one launch (start us, length us, event | category | flops | bytes accessed | tf_op | source)
XLA Modules:
  0.0 20.7 jit_solution(12586439374095408870)
XLA Ops:
  0.6 0.5 %collective-permute-start = (bf16[128,2560]{1,0:T(8,128)(2,1)}, bf16[128,2560]{1,0:T(8,128)(2,1)S(1)}, u32[]{:S(2)}, u32[]{:S(2)}) collective-permute-start(bf16[128,2560]{1,0:T(8,128)(2,1)} %x_hbm.1), channel_id=1, source_target_pairs={{0,1},{1,0},{2,3},{3,2},{4,5},{5,4},{6,7},{7,6},{8,9},{9,8},{10,11... | collective-permute-start | bytes 1966088 | tf_op jit(solution)/shard_map/ppermute | solution.py:358
  1.1 2.5 %plan.1 = (bf16[20,2,128,256]{3,2,1,0:T(8,128)(2,1)S(1)}, f32[20,128,128]{2,1,0:T(8,128)S(1)}, bf16[20,2,128,128]{3,2,1,0:T(8,128)(2,1)S(1)}, bf16[256,128]{1,0:...) custom-call(s32[4,8,80]{2,1,0:T(8,128)} %bitcast.7, f32[64,128]{1,0:T(8,128)} %constant.6.clone.tab_hbm, ...), custom_call_target="tpu_custom_call" | custom-call | flops 2000000000 | bytes 4000000 | tf_op jit(solution)/shard_map/plan/pallas_call | solution.py:142
  3.7 0.0 collective-permute-done.peer_ref
  3.7 0.0 copy-start
  3.7 1.0 %select.1.dep_ref.c_ref = f32[4,8,80]{2,1,0:T(8,128)S(1)} custom-call(s32[1]{0:T(128)} %bitcast.t_ref, bf16[20,2,128,256]{3,2,1,0:T(8,128)(2,1)S(1)} %get-tuple-element.21.sel_ref, f32[20,128,128]{2,1,0:T(8,128)S(1)} %get-tuple-element.22.sec_ref, bf16[256,5120]{1,0:T(8,128)(2,1)S(1)} %get-tuple-element.23.m_ref, ...), custom_call_target="tpu_custom_call" | custom-call | flops 1000000000 | bytes 6000000 | tf_op jit(solution)/shard_map/select/pallas_call | solution.py:196
  4.7 0.0 copy-start.1
  4.7 2.6 %collective-permute-start.1 = (f32[4,8,80]{2,1,0:T(8,128)S(1)}, f32[4,8,80]{2,1,0:T(8,128)S(1)}, u32[]{:S(2)}, u32[]{:S(2)}) collective-permute-start(f32[4,8,80]{2,1,0:T(8,128)S(1)} %select.1.dep_ref.c_ref), channel_id=1, source_target_pairs={{0,2},{2,0},{4,6},{6,4},{8,10},{10,8},{12,14},{14,12},{1,3},{3,1},... | collective-permute-start | bytes 30728 | tf_op jit(solution)/shard_map/ppermute | solution.py:367
  7.3 0.0 copy-done
  7.3 1.6 %keys.1 = bf16[128,256]{1,0:T(8,128)(2,1)} custom-call(s32[1]{0:T(128)} %bitcast.t_ref, bf16[128,2560]{1,0:T(8,128)(2,1)S(1)} %get-tuple-element.24.own_ref, bf16[128,2560]{1,0:T(8,128)(2,1)S(1)} %collective-permute-done.peer_ref, bf16[256,5120]{1,0:T(8,128)(2,1)S(1)} %copy-done, f32[4,8,80]{2,1,0:T(8,128)S(1)} %select.1.dep_ref.c_ref), custom_call_target="tpu_custom_call" | custom-call | flops 335544320 | bytes 4000000 | tf_op jit(solution)/shard_map/keys/pallas_call | solution.py:312
  8.9 0.1 collective-permute-done.1
  9.0 0.2 collective-permute-start.3
  9.2 0.0 copy-done.1
  9.2 0.3 %collective-permute-start.5 = (bf16[128,256]{1,0:T(8,128)(2,1)S(1)}, bf16[128,256]{1,0:T(8,128)(2,1)S(1)}, u32[]{:S(2)}, u32[]{:S(2)}) collective-permute-start(bf16[128,256]{1,0:T(8,128)(2,1)S(1)} %copy-done.1), channel_id=1, source_target_pairs={{0,1},{1,0},{2,3},{3,2},{4,5},{5,4},{6,7},{7,6},{8,9},{9,8},{10,11... | collective-permute-start | bytes 196616 | tf_op jit(solution)/shard_map/ppermute | solution.py:362
  9.5 2.1 %collective-permute-start.2 = (f32[4,8,80]{2,1,0:T(8,128)S(1)}, f32[4,8,80]{2,1,0:T(8,128)S(1)}, u32[]{:S(2)}, u32[]{:S(2)}) collective-permute-start(f32[4,8,80]{2,1,0:T(8,128)S(1)} %add.9), channel_id=1, source_target_pairs={{0,4},{2,6},{4,0},{6,2},{8,12},{10,14},{12,8},{14,10},{1,5},{3,7},... | collective-permute-start | bytes 30728 | tf_op jit(solution)/shard_map/ppermute | solution.py:367
  11.6 2.4 %remain.1 = bf16[256,5120]{1,0:T(8,128)(2,1)} custom-call(s32[1]{0:T(128)} %bitcast.t_ref, bf16[20,2,128,128]{3,2,1,0:T(8,128)(2,1)S(1)} %get-tuple-element.27.lt_ref, f32[20,128,128]{2,1,0:T(8,128)S(1)} %get-tuple-element.22.sec_ref, bf16[256,128]{1,0:T(8,128)(2,1)S(1)} %get-tuple-element.28.gt_ref, bf16[256,5120]{1,0:T(8,128)(2,1)S(1)} %get-tuple-element.23.m_ref, ...), custom_call_target="tpu_custom_call" | custom-call | flops 2000000000 | bytes 8000000 | tf_op jit(solution)/shard_map/remain/pallas_call | solution.py:255
  14.0 0.0 collective-permute-done.2
  14.1 0.0 collective-permute-done.3.wp_ref
  14.1 2.9 %collective-permute-start.4 = (f32[4,8,80]{2,1,0:T(8,128)S(1)}, f32[4,8,80]{2,1,0:T(8,128)S(1)}, u32[]{:S(2)}, u32[]{:S(2)}) collective-permute-start(f32[4,8,80]{2,1,0:T(8,128)S(1)} %add.10.dep_ref), channel_id=1, source_target_pairs={{0,8},{2,10},{4,12},{6,14},{8,0},{10,2},{12,4},{14,6},{1,9},{3,11}... | collective-permute-start | bytes 30728 | tf_op jit(solution)/shard_map/ppermute | solution.py:367
  17.0 0.0 collective-permute-done.5.peer_ref
  17.0 1.2 %input_grad.1 = bf16[128,2560]{1,0:T(8,128)(2,1)} custom-call(s32[1]{0:T(128)} %bitcast.t_ref, bf16[128,256]{1,0:T(8,128)(2,1)S(1)} %copy-done.1, bf16[128,256]{1,0:T(8,128)(2,1)S(1)} %collective-permute-done.5.peer_ref, bf16[256,5120]{1,0:T(8,128)(2,1)S(1)} %copy-done, bf16[256,5120]{1,0:T(8,128)(2,1)S(1)} %collective-permute-done.3.wp_ref, ...), custom_call_target="tpu_custom_call" | custom-call | flops 335544320 | bytes 4000000 | tf_op jit(solution)/shard_map/input_grad/pallas_call | solution.py:342
  18.3 0.5 %collective-permute-done.4 = f32[4,8,80]{2,1,0:T(8,128)S(1)} collective-permute-done((f32[4,8,80]{2,1,0:T(8,128)S(1)}, f32[4,8,80]{2,1,0:T(8,128)S(1)}, u32[]{:S(2)}, u32[]{:S(2)}) %collective-permute-start.4) | collective-permute-done | bytes 10272 | tf_op jit(solution)/shard_map/ppermute | solution.py:367
  18.8 1.9 %update.1 = (bf16[256,5120]{1,0:T(8,128)(2,1)}, f32[4,8,80]{2,1,0:T(8,128)}) custom-call(bf16[20,2,128,128]{3,2,1,0:T(8,128)(2,1)S(1)} %get-tuple-element.27.lt_ref, f32[20,128,128]{2,1,0:T(8,128)S(1)} %get-tuple-element.22.sec_ref, f32[4,8,80]{2,1,0:T(8,128)S(1)} %add.11.sum_ref), custom_call_target="tpu_custom_call" | custom-call | flops 1000000000 | bytes 6000000 | tf_op jit(solution)/shard_map/update/pallas_call | solution.py:283
  (3 shorter events, 0.0 us)
Async XLA Ops:
  0.6 3.0 %collective-permute-start = (bf16[128,2560]{1,0:T(8,128)(2,1)}, bf16[128,2560]{1,0:T(8,128)(2,1)S(1)}, u32[]{:S(2)}, u32[]{:S(2)}) collective-permute-start(bf16[128,2560]{1,0:T(8,128)(2,1)} %x_hbm.1), channel_id=1, source_target_pairs={{0,1},{1,0},{2,3},{3,2},{4,5},{5,4},{6,7},{7,6},{8,9},{9,8},{10,11... | collective-permute-start | bytes 1966088 | tf_op jit(solution)/shard_map/ppermute | solution.py:358
  3.7 3.6 %copy-start = (bf16[256,5120]{1,0:T(8,128)(2,1)S(1)}, bf16[256,5120]{1,0:T(8,128)(2,1)}, u32[]{:S(2)}) copy-start(bf16[256,5120]{1,0:T(8,128)(2,1)} %w_ref.3) | copy-start | bytes 7864324
  4.7 4.5 %copy-start.1 = (bf16[128,256]{1,0:T(8,128)(2,1)S(1)}, bf16[128,256]{1,0:T(8,128)(2,1)}, u32[]{:S(2)}) copy-start(bf16[128,256]{1,0:T(8,128)(2,1)} %own_ref.1) | copy-start | bytes 196612
  4.7 4.3 %collective-permute-start.1 = (f32[4,8,80]{2,1,0:T(8,128)S(1)}, f32[4,8,80]{2,1,0:T(8,128)S(1)}, u32[]{:S(2)}, u32[]{:S(2)}) collective-permute-start(f32[4,8,80]{2,1,0:T(8,128)S(1)} %select.1.dep_ref.c_ref), channel_id=1, source_target_pairs={{0,2},{2,0},{4,6},{6,4},{8,10},{10,8},{12,14},{14,12},{1,3},{3,1},... | collective-permute-start | bytes 30728 | tf_op jit(solution)/shard_map/ppermute | solution.py:367
  9.0 5.1 %collective-permute-start.3 = (bf16[256,5120]{1,0:T(8,128)(2,1)S(1)}, bf16[256,5120]{1,0:T(8,128)(2,1)S(1)}, u32[]{:S(2)}, u32[]{:S(2)}) collective-permute-start(bf16[256,5120]{1,0:T(8,128)(2,1)S(1)} %copy-done), channel_id=1, source_target_pairs={{0,1},{1,0},{2,3},{3,2},{4,5},{5,4},{6,7},{7,6},{8,9},{9,8},{10,11... | collective-permute-start | bytes 7864328 | tf_op jit(solution)/shard_map/ppermute | solution.py:373
  9.2 7.8 %collective-permute-start.5 = (bf16[128,256]{1,0:T(8,128)(2,1)S(1)}, bf16[128,256]{1,0:T(8,128)(2,1)S(1)}, u32[]{:S(2)}, u32[]{:S(2)}) collective-permute-start(bf16[128,256]{1,0:T(8,128)(2,1)S(1)} %copy-done.1), channel_id=1, source_target_pairs={{0,1},{1,0},{2,3},{3,2},{4,5},{5,4},{6,7},{7,6},{8,9},{9,8},{10,11... | collective-permute-start | bytes 196616 | tf_op jit(solution)/shard_map/ppermute | solution.py:362
  9.5 4.5 %collective-permute-start.2 = (f32[4,8,80]{2,1,0:T(8,128)S(1)}, f32[4,8,80]{2,1,0:T(8,128)S(1)}, u32[]{:S(2)}, u32[]{:S(2)}) collective-permute-start(f32[4,8,80]{2,1,0:T(8,128)S(1)} %add.9), channel_id=1, source_target_pairs={{0,4},{2,6},{4,0},{6,2},{8,12},{10,14},{12,8},{14,10},{1,5},{3,7},... | collective-permute-start | bytes 30728 | tf_op jit(solution)/shard_map/ppermute | solution.py:367
  14.1 4.7 %collective-permute-start.4 = (f32[4,8,80]{2,1,0:T(8,128)S(1)}, f32[4,8,80]{2,1,0:T(8,128)S(1)}, u32[]{:S(2)}, u32[]{:S(2)}) collective-permute-start(f32[4,8,80]{2,1,0:T(8,128)S(1)} %add.10.dep_ref), channel_id=1, source_target_pairs={{0,8},{2,10},{4,12},{6,14},{8,0},{10,2},{12,4},{14,6},{1,9},{3,11}... | collective-permute-start | bytes 30728 | tf_op jit(solution)/shard_map/ppermute | solution.py:367

commit v4 on v3

--- a/solution.py
+++ b/solution.py
@@ -44,7 +44,7 @@
     return pl.pallas_call(
         kernel,
         name=name,
-        compiler_params=pltpu.CompilerParams(vmem_limit_bytes=8 * 2**20),
+        compiler_params=pltpu.CompilerParams(vmem_limit_bytes=16 * 2**20),
         cost_estimate=pl.CostEstimate(flops=flops, bytes_accessed=nbytes, transcendentals=0),
         **kw,
     )
@@ -99,38 +99,43 @@
     z = flat(idx_ref)
     chi, clo = split(tab_ref[...])
     col_tab = jnp.concatenate([chi, clo], axis=0)
-    hi = jnp.concatenate([chi, chi], axis=0)
-    lo = jnp.concatenate([clo, clo], axis=0)
-    square = (LANES, LANES)
-    near = lax.broadcasted_iota(jnp.int32, square, 0) // SPAN == lax.broadcasted_iota(jnp.int32, square, 1) // SPAN
-    hi = jnp.where(near, hi, jnp.zeros_like(hi))
-    lo = jnp.where(near, lo, jnp.zeros_like(lo))
-    g = g_ref[...]
-    gt_ref[...] = g.T
-    row_g = [mm_t(hi, g[:, at : at + LANES]) + mm_t(lo, g[:, at : at + LANES]) for at in range(0, SIDE, LANES)]
-    ghi, glo = split(jnp.concatenate(row_g, axis=0) * (1.0 / decay_rate))
-    hi, lo = [jnp.concatenate([part, part], axis=0) for part in (hi, lo)]
-    row_tab = jnp.concatenate([hi, ghi, lo, glo], axis=1)
+    none = jnp.zeros((LANES, LANES), bf16)
+    col_tab = jnp.concatenate(
+        [jnp.concatenate([col_tab, none], axis=1), jnp.concatenate([none, col_tab], axis=1)], axis=0
+    )
     lane = lax.broadcasted_iota(jnp.int32, (kept, LANES), 1)
     row = lax.broadcasted_iota(jnp.int32, (kept, LANES), 0)
     place = lane - SPAN * ((row // per) & 1)
     lane_in = lane & (SPAN - 1)
     mine = (lane // SPAN) == ((row // (per // GROUP)) & 1)
+    hi = jnp.concatenate([chi, chi], axis=0)
+    lo = jnp.concatenate([clo, clo], axis=0)
+    near = lax.broadcasted_iota(jnp.int32, hi.shape, 0) // SPAN == lax.broadcasted_iota(jnp.int32, hi.shape, 1) // SPAN
+    hi = jnp.where(near, hi, jnp.zeros_like(hi))
+    lo = jnp.where(near, lo, jnp.zeros_like(lo))
+    g = g_ref[...]
+    row_g = [mm_t(hi, g[:, at : at + LANES]) + mm_t(lo, g[:, at : at + LANES]) for at in range(0, SIDE, LANES)]
+    ghi, glo = split(jnp.concatenate(row_g, axis=0) * (1.0 / decay_rate))
+    hi, lo = [jnp.concatenate([part, part], axis=0) for part in (hi, lo)]
+    row_tab = jnp.concatenate([hi, ghi, lo, glo], axis=1)
     none = jnp.zeros((half, LANES), bf16)
-    for j in range(blocks):
-        col = column(z, j)
-        one = jnp.where((col >> 6) == place, 1.0, 0.0).astype(bf16)
-        one_a = jnp.concatenate(
-            [jnp.concatenate([one[:half], none], axis=1), jnp.concatenate([none, one[half:]], axis=1)], axis=0
-        )
-        rows = mm(one_a, row_tab).astype(bf16)
-        for p in range(2):
-            at = slice(p * half, (p + 1) * half)
-            sel_ref[j, p, :half, :] = rows[at, :SIDE]
-            sel_ref[j, p, half:, :] = rows[at, SIDE:]
-            lt_ref[j, p] = jnp.concatenate([rows[at, :LANES], rows[at, SIDE : SIDE + LANES]], axis=0).T
-        one_b = jnp.where((col & (SPAN - 1)) == lane_in, 1.0, 0.0).astype(bf16)
-        sec_ref[j] = jnp.where(mine, mm(one_b, col_tab), 0.0)
+    for j in range(0, blocks, 2):
+        cols = [column(z, k) for k in (j, j + 1)]
+        one_b = [jnp.where((col & (SPAN - 1)) == lane_in, 1.0, 0.0).astype(bf16) for col in cols]
+        sec = mm(jnp.concatenate(one_b, axis=1), col_tab)
+        for k in range(2):
+            sec_ref[j + k] = jnp.where(mine, sec[:, k * LANES : (k + 1) * LANES], 0.0)
+            one = jnp.where((cols[k] >> 6) == place, 1.0, 0.0).astype(bf16)
+            one_a = jnp.concatenate(
+                [jnp.concatenate([one[:half], none], axis=1), jnp.concatenate([none, one[half:]], axis=1)], axis=0
+            )
+            rows = mm(one_a, row_tab).astype(bf16)
+            for p in range(2):
+                at = slice(p * half, (p + 1) * half)
+                sel_ref[j + k, p, :half, :] = rows[at, :SIDE]
+                sel_ref[j + k, p, half:, :] = rows[at, SIDE:]
+                lt_ref[j + k, p] = jnp.concatenate([rows[at, :LANES], rows[at, SIDE : SIDE + LANES]], axis=0).T
+    gt_ref[...] = g.T
     for load in loads[3:]:
         load.wait()
 
@@ -222,22 +227,29 @@
     return outs
 
 
-CHUNKS = 10
-
-
-def store_block(j, blocks, buf, out_ref, sems, copies):
-    per = blocks // CHUNKS
-    if (j + 1) % per == 0:
-        at = pl.ds((j + 1 - per) * SIDE, per * SIDE)
-        copies.append(pltpu.make_async_copy(buf.at[:, at], out_ref.at[:, at], sems.at[j // per]))
-        copies[-1].start()
-
-
-def remain_kernel(t_ref, lt_ref, sec_ref, gt_ref, m_ref, own_ref, peer_ref, c_ref, out_ref, buf, sems):
+class Writer:
+    def __init__(self, buf, out, sems):
+        self.buf, self.out, self.sems, self.copies = buf, out, sems, []
+
+    def put(self, start, stop):
+        at = pl.ds(start * SIDE, (stop - start) * SIDE)
+        copy = pltpu.make_async_copy(self.buf.at[:, at], self.out.at[:, at], self.sems.at[len(self.copies)])
+        copy.start()
+        self.copies.append(copy)
+
+    def wait(self):
+        for copy in self.copies:
+            copy.wait()
+
+
+STEP = 2
+FIRST = 14
+
+
+def remain_blocks(t_ref, lt_ref, sec_ref, gt_ref, m_ref, own_ref, peer_ref, c_ref, buf, writer, start, stop):
     blocks = lt_ref.shape[0]
-    copies = []
     c = -flat(c_ref)
-    for j in range(blocks):
+    for j in range(start, stop):
         x = pick(t_ref, own_ref, peer_ref, j, blocks // 2)
         cols = slice(j * SIDE, (j + 1) * SIDE)
         grad = mm(gt_ref[...], x)
@@ -246,37 +258,85 @@
             at = slice(p * LANES, (p + 1) * LANES)
             moved = decay_rate * m_ref[at, cols].astype(f32) + grad[at]
             buf[at, cols] = (moved + less[p]).astype(bf16)
-        store_block(j, blocks, buf, out_ref, sems, copies)
-    for copy in copies:
-        copy.wait()
-
-
-def remain(t, lt, sec, gt, m, own, peer, c):
-    return call(
-        remain_kernel,
+        if (j + 1 - start) % STEP == 0 or j + 1 == stop:
+            writer.put(j - (j - start) % STEP, j + 1)
+
+
+def remain_kernel(stop, *refs):
+    *ins, out_ref, buf, sems = refs
+    writer = Writer(buf, out_ref, sems)
+    remain_blocks(*ins, buf, writer, 0, stop)
+    writer.wait()
+
+
+def remain(stop, t, lt, sec, gt, m, own, peer, c):
+    return call(
+        functools.partial(remain_kernel, stop),
         "remain",
         flops=2 * 10**9,
         nbytes=8 * 10**6,
         in_specs=[SCALAR] + whole(7),
         out_specs=anywhere(1)[0],
         out_shape=jax.ShapeDtypeStruct(m.shape, bf16),
-        scratch_shapes=[pltpu.VMEM(m.shape, bf16), pltpu.SemaphoreType.DMA((CHUNKS,))],
+        scratch_shapes=[pltpu.VMEM(m.shape, bf16), pltpu.SemaphoreType.DMA((stop,))],
     )(t, *vmem(lt, sec, gt, m, own, peer, c))
+
+
+def finish_kernel(start, *refs):
+    *ins, g_ref, w_ref, wp_ref, dep_ref, begun_ref, out_ref, in_ref, buf, in_buf, sems, in_sems = refs
+    t_ref = ins[0]
+    blocks = ins[1].shape[0]
+    writer = Writer(buf, out_ref, sems)
+    remain_blocks(*ins, buf, writer, start, blocks)
+    width = in_buf.shape[1]
+    g = jnp.concatenate([g_ref[...], wp_ref[:, width:].T], axis=1)
+    in_writer = Writer(in_buf, in_ref, in_sems)
+    for n in range(width // SIDE):
+        at = slice(n * SIDE, (n + 1) * SIDE)
+        mine, _ = halves(t_ref, width, n * SIDE, SIDE)
+        w = jnp.concatenate([w_ref[:, mine], wp_ref[:, at]], axis=0)
+        in_buf[:, at] = mm(g, w).astype(bf16)
+        if n % STEP == STEP - 1:
+            in_writer.put(n + 1 - STEP, n + 1)
+    writer.wait()
+    in_writer.wait()
+
+
+def finish(start, begun, t, lt, sec, gt, m, own, peer, c, g, w, wp, dep):
+    shape = (g.shape[0], w.shape[1] // 2)
+    return call(
+        functools.partial(finish_kernel, start),
+        "finish",
+        flops=10**9,
+        nbytes=8 * 10**6,
+        in_specs=[SCALAR] + whole(10) + anywhere(2),
+        out_specs=anywhere(2),
+        out_shape=[jax.ShapeDtypeStruct(m.shape, bf16), jax.ShapeDtypeStruct(shape, bf16)],
+        scratch_shapes=[
+            pltpu.VMEM(m.shape, bf16),
+            pltpu.VMEM(shape, bf16),
+            pltpu.SemaphoreType.DMA((lt.shape[0],)),
+            pltpu.SemaphoreType.DMA((shape[1] // SIDE,)),
+        ],
+        input_output_aliases={12: 0},
+    )(t, *vmem(lt, sec, gt, m, own, peer, c, g, w, wp), dep, begun)
 
 
 def update_kernel(scale, lt_ref, sec_ref, sum_ref, out_ref, mean_ref, buf, mean, sems):
     blocks = lt_ref.shape[0]
     mean[...] = sum_ref[...] * scale
-    copies = [pltpu.make_async_copy(mean, mean_ref, sems.at[CHUNKS])]
-    copies[0].start()
+    writer = Writer(buf, out_ref, sems)
+    pooled = pltpu.make_async_copy(mean, mean_ref, sems.at[blocks])
+    pooled.start()
     c = flat(mean)
     for j in range(blocks):
         out = decoded(lt_ref[j], sec_ref[j], column(c, j))
         for p in range(2):
             buf[p * LANES : (p + 1) * LANES, j * SIDE : (j + 1) * SIDE] = out[p].astype(bf16)
-        store_block(j, blocks, buf, out_ref, sems, copies)
-    for copy in copies:
-        copy.wait()
+        if (j + 1) % STEP == 0:
+            writer.put(j + 1 - STEP, j + 1)
+    writer.wait()
+    pooled.wait()
 
 
 def update(lt, sec, total, replicas, shape):
@@ -291,7 +351,7 @@
         scratch_shapes=[
             pltpu.VMEM(shape, bf16),
             pltpu.VMEM(total.shape, f32),
-            pltpu.SemaphoreType.DMA((CHUNKS + 1,)),
+            pltpu.SemaphoreType.DMA((lt.shape[0] + 1,)),
         ],
     )(*vmem(lt, sec, total))
 
@@ -303,52 +363,34 @@
     return mine, theirs
 
 
-def keys_kernel(t_ref, own_ref, peer_ref, w_ref, dep_ref, out_ref):
-    mine, theirs = halves(t_ref, own_ref.shape[1], 0, own_ref.shape[1])
+def keys_kernel(t_ref, own_ref, peer_ref, w_ref, gt_ref, dep_ref, out_ref, part_ref, sems):
+    width = own_ref.shape[1]
+    mine, theirs = halves(t_ref, width, 0, width)
+    copies = [
+        pltpu.make_async_copy(w_ref.at[:, theirs], part_ref.at[:, :width], sems.at[0]),
+        pltpu.make_async_copy(gt_ref, part_ref.at[:, width:], sems.at[1]),
+    ]
+    for copy in copies:
+        copy.start()
     out_ref[...] = (mm_t(own_ref[...], w_ref[:, mine]) + mm_t(peer_ref[...], w_ref[:, theirs])).astype(bf16)
-
-
-def keys_of(t, own, peer, w, dep):
+    for copy in copies:
+        copy.wait()
+
+
+def keys_of(t, own, peer, w, gt, dep):
     return call(
         keys_kernel,
         "keys",
         flops=2 * own.shape[0] * w.shape[0] * w.shape[1],
         nbytes=4 * 10**6,
-        in_specs=[SCALAR] + whole(3) + anywhere(1),
-        out_specs=whole(1)[0],
-        out_shape=jax.ShapeDtypeStruct((own.shape[0], w.shape[0]), bf16),
-    )(t, *vmem(own, peer, w), dep)
-
-
-def input_kernel(t_ref, own_ref, peer_ref, w_ref, wp_ref, dep_ref, out_ref, buf, sems):
-    width = out_ref.shape[1]
-    g = jnp.concatenate([own_ref[...], peer_ref[...]], axis=1)
-    copies = []
-    per = width // (sems.shape[0] * SIDE)
-    for n, at in enumerate(range(0, width, SIDE)):
-        mine, _ = halves(t_ref, width, at, SIDE)
-        w = jnp.concatenate([w_ref[:, mine], wp_ref[:, mine]], axis=0)
-        buf[:, at : at + SIDE] = mm(g, w).astype(bf16)
-        if (n + 1) % per == 0:
-            cols = pl.ds((n + 1 - per) * SIDE, per * SIDE)
-            copies.append(pltpu.make_async_copy(buf.at[:, cols], out_ref.at[:, cols], sems.at[n // per]))
-            copies[-1].start()
-    for copy in copies:
-        copy.wait()
-
-
-def input_of(t, own, peer, w, wp, dep):
-    shape = (own.shape[0], w.shape[1] // 2)
-    return call(
-        input_kernel,
-        "input_grad",
-        flops=2 * own.shape[0] * w.shape[0] * w.shape[1],
-        nbytes=4 * 10**6,
         in_specs=[SCALAR] + whole(4) + anywhere(1),
-        out_specs=anywhere(1)[0],
-        out_shape=jax.ShapeDtypeStruct(shape, bf16),
-        scratch_shapes=[pltpu.VMEM(shape, bf16), pltpu.SemaphoreType.DMA((5,))],
-    )(t, *vmem(own, peer, w, wp), dep)
+        out_specs=whole(1) + anywhere(1),
+        out_shape=[
+            jax.ShapeDtypeStruct((own.shape[0], w.shape[0]), bf16),
+            jax.ShapeDtypeStruct((w.shape[0], own.shape[1] + gt.shape[1]), bf16),
+        ],
+        scratch_shapes=[pltpu.SemaphoreType.DMA((2,))],
+    )(t, *vmem(own, peer, w, gt), dep)
 
 
 def shards(tokens, cotangent, key_weight, momentum, indices):
@@ -358,8 +400,8 @@
     peer = lax.ppermute(tokens, "tensor", swap)
     m = momentum[0]
     idx = indices.transpose(0, 2, 1)
-    sel, sec, lt, gt, m_in, own = plan(idx, cotangent, jnp.asarray(dct_table()), m, tokens)
-    cot_peer = lax.ppermute(cotangent, "tensor", swap)
+    tab = jnp.asarray(dct_table())
+    sel, sec, lt, gt, m_in, own = plan(idx, cotangent, tab, m, tokens)
     total = select(t, sel, sec, m_in, own, peer, idx.shape)
     mine = total
 
@@ -367,15 +409,18 @@
         return lax.ppermute(x, "replica", [(i, i ^ step) for i in range(replicas)])
 
     steps = [1 << k for k in range(replicas.bit_length() - 1)]
+    split_at = FIRST
     got = exchange(total, steps[0])
-    keys = keys_of(t, own, peer, key_weight, total)
-    total, keys, w_out = lax.optimization_barrier((total + got, keys, key_weight))
-    w_peer = lax.ppermute(w_out, "tensor", swap)
+    keys, w_part = keys_of(t, own, peer, key_weight, gt, total)
+    total, keys, w_part = lax.optimization_barrier((total + got, keys, w_part))
+    w_peer = lax.ppermute(w_part, "tensor", swap)
     got = exchange(total, steps[1])
-    remaining = remain(t, lt, sec, gt, m_in, own, peer, mine)
-    total, remaining, w_peer = lax.optimization_barrier((total + got, remaining, w_peer))
+    begun = remain(split_at, t, lt, sec, gt, m_in, own, peer, mine)
+    total, begun, w_peer = lax.optimization_barrier((total + got, begun, w_peer))
     got = exchange(total, steps[2])
-    input_grad = input_of(t, cotangent, cot_peer, key_weight, w_peer, total)
+    remaining, input_grad = finish(
+        split_at, begun, t, lt, sec, gt, m_in, own, peer, mine, cotangent, key_weight, w_peer, total
+    )
     total, input_grad = lax.optimization_barrier((total + got, input_grad))
     for step in steps[3:]:
         total = total + exchange(total, step)

time: 20.9 us -> 20 us (0.957)
  starting transfers between devices: 8.66 us -> 7.98 us
  waiting for transfers between devices: 0.6 us -> 0.01 us
  Pallas kernels: 10.7 us -> 11 us
    ppermute x3, waiting for transfers between devices: 0.59 us -> 0.01 us  [exchange(): return lax.ppermute(x, 'replica', [(i, i ^ step) for i in range(replicas)])]
    ppermute x3, starting transfers between devices: 7.63 us -> 7.18 us  [exchange(): return lax.ppermute(x, 'replica', [(i, i ^ step) for i in range(replicas)])]
    pallas_call x2, Pallas kernels: 3.67 us -> 3.93 us  [the longest x1 2.02 us: remain(): call(functools.partial(remain_kernel, stop), 'remain', flops=2 * 10 ** 9,...]
    pallas_call x1, Pallas kernels: 2.51 us -> 2.27 us  [plan(): call(plan_kernel, 'plan', flops=2 * 10 ** 9, nbytes=4 * 10 ** 6, in_specs...]
    ppermute x2 -> x1, starting transfers between devices: 0.51 us -> 0.28 us  [shards(): w_peer = lax.ppermute(w_part, 'tensor', swap)]
  transfers between devices with their start and end apart: 6 -> 5, of which waited for: 2 -> 0; matrix products, arithmetic and copies ran while one was open for 0% -> 0% of each run, Pallas kernels for 38% -> 40%
where the time goes in v4:
time: 20 us; the launch traced here: 19.8 us
  Pallas kernels  11 us (55%)
  starting transfers between devices  7.98 us (40%)
  between operations  0.74 us (4%)
    ppermute x3, starting transfers between devices, exchange(): return lax.ppermute(x, 'replica', [(i, i ^ step) for i in range(replicas)])  7.18 us
    pallas_call x1, Pallas kernels, plan(): call(plan_kernel, 'plan', flops=2 * 10 ** 9, nbytes=4 * 10 ** 6, in_specs...  2.27 us
    pallas_call x1, Pallas kernels, remain(): call(functools.partial(remain_kernel, stop), 'remain', flops=2 * 10 ** 9,...  2.02 us
    pallas_call x1, Pallas kernels, update(): call(functools.partial(update_kernel, 1.0 / replicas), 'update', flops=10...  2 us
    pallas_call x1, Pallas kernels, finish(): call(functools.partial(finish_kernel, start), 'finish', flops=10 ** 9, nb...  1.92 us
    pallas_call x1, Pallas kernels, keys_of(): call(keys_kernel, 'keys', flops=2 * own.shape[0] * w.shape[0] * w.shape[1...  1.75 us
    pallas_call x1, Pallas kernels, select(): call(select_kernel, 'select', flops=10 ** 9, nbytes=6 * 10 ** 6, in_specs...  1.04 us
    ppermute x1, starting transfers between devices, shards(): peer = lax.ppermute(tokens, 'tensor', swap)  0.52 us
  transfers between devices with their start and end apart: 5, of which 0 were waited for; matrix products, arithmetic and copies ran while one was open for 0% of the time, Pallas kernels for 40%

profile of v4, /device:TPU:0, one launch (start us, length us, event | category | flops | bytes accessed | tf_op | source)
XLA Modules:
  0.0 19.8 jit_solution(9597394250821823782)
XLA Ops:
  0.6 0.5 %collective-permute-start = (bf16[128,2560]{1,0:T(8,128)(2,1)}, bf16[128,2560]{1,0:T(8,128)(2,1)S(1)}, u32[]{:S(2)}, u32[]{:S(2)}) collective-permute-start(bf16[128,2560]{1,0:T(8,128)(2,1)} %x_hbm.1), channel_id=1, source_target_pairs={{0,1},{1,0},{2,3},{3,2},{4,5},{5,4},{6,7},{7,6},{8,9},{9,8},{10,11... | collective-permute-start | bytes 1966088 | tf_op jit(solution)/shard_map/ppermute | solution.py:400
  1.1 2.3 %plan.1 = (bf16[20,2,128,256]{3,2,1,0:T(8,128)(2,1)S(1)}, f32[20,128,128]{2,1,0:T(8,128)S(1)}, bf16[20,2,128,128]{3,2,1,0:T(8,128)(2,1)S(1)}, bf16[256,128]{1,0:...) custom-call(s32[4,8,80]{2,1,0:T(8,128)} %bitcast.7, f32[64,128]{1,0:T(8,128)} %constant.6.clone.tab_hbm, ...), custom_call_target="tpu_custom_call" | custom-call | flops 2000000000 | bytes 4000000 | tf_op jit(solution)/shard_map/plan/pallas_call | solution.py:147
  3.4 0.0 collective-permute-done.peer_ref.refs_6_
  3.4 0.0 copy-start
  3.5 1.0 %select.1.dep_ref.refs_7_ = f32[4,8,80]{2,1,0:T(8,128)S(1)} custom-call(s32[1]{0:T(128)} %bitcast.t_ref.refs_0_, bf16[20,2,128,256]{3,2,1,0:T(8,128)(2,1)S(1)} %get-tuple-element.25.sel_ref, f32[20,128,128]{2,1,0:T(8,128)S(1)} %get-tuple-element.26.sec_ref.refs_2_, bf16[256,5120]{1,0:T(8,128)(2,1)S(1)} %get-tuple-element.27.m_ref.refs_4_, ...), custom_call_target="tpu_custom_call" | custom-call | flops 1000000000 | bytes 6000000 | tf_op jit(solution)/shard_map/select/pallas_call | solution.py:201
  4.5 2.6 %collective-permute-start.1 = (f32[4,8,80]{2,1,0:T(8,128)S(1)}, f32[4,8,80]{2,1,0:T(8,128)S(1)}, u32[]{:S(2)}, u32[]{:S(2)}) collective-permute-start(f32[4,8,80]{2,1,0:T(8,128)S(1)} %select.1.dep_ref.refs_7_), channel_id=1, source_target_pairs={{0,2},{2,0},{4,6},{6,4},{8,10},{10,8},{12,14},{14,12},{1,3},{3,1},... | collective-permute-start | bytes 30728 | tf_op jit(solution)/shard_map/ppermute | solution.py:409
  7.1 0.0 copy-done
  7.1 1.8 %keys.1 = (bf16[128,256]{1,0:T(8,128)(2,1)}, bf16[256,2688]{1,0:T(8,128)(2,1)S(1)}) custom-call(s32[1]{0:T(128)} %bitcast.t_ref.refs_0_, bf16[128,2560]{1,0:T(8,128)(2,1)S(1)} %get-tuple-element.28.own_ref.refs_5_, bf16[128,2560]{1,0:T(8,128)(2,1)S(1)} %collective-permute-done.peer_ref.refs_6_, bf16[256,5120]{1,0:T(8,128)(2,1)S(1)} %copy-done, ...), custom_call_target="tpu_custom_call" | custom-call | flops 335544320 | bytes 4000000 | tf_op jit(solution)/shard_map/keys/pallas_call | solution.py:381
  8.9 0.0 collective-permute-done.1
  8.9 0.3 %collective-permute-start.3 = (bf16[256,2688]{1,0:T(8,128)(2,1)S(1)}, bf16[256,2688]{1,0:T(8,128)(2,1)S(1)}, u32[]{:S(2)}, u32[]{:S(2)}) collective-permute-start(bf16[256,2688]{1,0:T(8,128)(2,1)S(1)} %get-tuple-element.35), channel_id=1, source_target_pairs={{0,1},{1,0},{2,3},{3,2},{4,5},{5,4},{6,7},{7,6},{8,9},{9,8},{10,11... | collective-permute-start | bytes 4128776 | tf_op jit(solution)/shard_map/ppermute | solution.py:416
  9.2 1.8 %collective-permute-start.2 = (f32[4,8,80]{2,1,0:T(8,128)S(1)}, f32[4,8,80]{2,1,0:T(8,128)S(1)}, u32[]{:S(2)}, u32[]{:S(2)}) collective-permute-start(f32[4,8,80]{2,1,0:T(8,128)S(1)} %add.9), channel_id=1, source_target_pairs={{0,4},{2,6},{4,0},{6,2},{8,12},{10,14},{12,8},{14,10},{1,5},{3,7},... | collective-permute-start | bytes 30728 | tf_op jit(solution)/shard_map/ppermute | solution.py:409
  11.0 0.0 copy-start.1
  11.0 2.0 %remain.1.refs_12_ = bf16[256,5120]{1,0:T(8,128)(2,1)} custom-call(s32[1]{0:T(128)} %bitcast.t_ref.refs_0_, bf16[20,2,128,128]{3,2,1,0:T(8,128)(2,1)S(1)} %get-tuple-element.34.refs_1_.lt_ref, f32[20,128,128]{2,1,0:T(8,128)S(1)} %get-tuple-element.26.sec_ref.refs_2_, bf16[256,128]{1,0:T(8,128)(2,1)S(1)} %get-tuple-element.29.gt_ref.refs_3_, ...), custom_call_target="tpu_custom_call" | custom-call | flops 2000000000 | bytes 8000000 | tf_op jit(solution)/shard_map/remain/pallas_call | solution.py:273
  13.0 0.0 collective-permute-done.2
  13.0 0.0 collective-permute-done.3.refs_10_
  13.0 2.8 %collective-permute-start.4 = (f32[4,8,80]{2,1,0:T(8,128)S(1)}, f32[4,8,80]{2,1,0:T(8,128)S(1)}, u32[]{:S(2)}, u32[]{:S(2)}) collective-permute-start(f32[4,8,80]{2,1,0:T(8,128)S(1)} %add.10.refs_11_), channel_id=1, source_target_pairs={{0,8},{2,10},{4,12},{6,14},{8,0},{10,2},{12,4},{14,6},{1,9},{3,11}... | collective-permute-start | bytes 30728 | tf_op jit(solution)/shard_map/ppermute | solution.py:409
  15.8 0.0 copy-done.1
  15.8 1.9 %finish.1 = (bf16[256,5120]{1,0:T(8,128)(2,1)}, bf16[128,2560]{1,0:T(8,128)(2,1)}) custom-call(s32[1]{0:T(128)} %bitcast.t_ref.refs_0_, bf16[20,2,128,128]{3,2,1,0:T(8,128)(2,1)S(1)} %get-tuple-element.34.refs_1_.lt_ref, f32[20,128,128]{2,1,0:T(8,128)S(1)} %get-tuple-element.26.sec_ref.refs_2_, ...), custom_call_target="tpu_custom_call", output_to_operand_aliasing={{0}: (12, {})} | custom-call | flops 1000000000 | bytes 8000000 | tf_op jit(solution)/shard_map/finish/pallas_call | solution.py:307
  17.7 0.0 collective-permute-done.4
  17.8 2.0 %update.1 = (bf16[256,5120]{1,0:T(8,128)(2,1)}, f32[4,8,80]{2,1,0:T(8,128)}) custom-call(bf16[20,2,128,128]{3,2,1,0:T(8,128)(2,1)S(1)} %get-tuple-element.34.refs_1_.lt_ref, f32[20,128,128]{2,1,0:T(8,128)S(1)} %get-tuple-element.26.sec_ref.refs_2_, f32[4,8,80]{2,1,0:T(8,128)S(1)} %add.11.sum_ref), custom_call_target="tpu_custom_call" | custom-call | flops 1000000000 | bytes 6000000 | tf_op jit(solution)/shard_map/update/pallas_call | solution.py:343
  (3 shorter events, 0.0 us)
Async XLA Ops:
  0.6 2.8 %collective-permute-start = (bf16[128,2560]{1,0:T(8,128)(2,1)}, bf16[128,2560]{1,0:T(8,128)(2,1)S(1)}, u32[]{:S(2)}, u32[]{:S(2)}) collective-permute-start(bf16[128,2560]{1,0:T(8,128)(2,1)} %x_hbm.1), channel_id=1, source_target_pairs={{0,1},{1,0},{2,3},{3,2},{4,5},{5,4},{6,7},{7,6},{8,9},{9,8},{10,11... | collective-permute-start | bytes 1966088 | tf_op jit(solution)/shard_map/ppermute | solution.py:400
  3.4 3.7 %copy-start = (bf16[256,5120]{1,0:T(8,128)(2,1)S(1)}, bf16[256,5120]{1,0:T(8,128)(2,1)}, u32[]{:S(2)}) copy-start(bf16[256,5120]{1,0:T(8,128)(2,1)} %refs_9_.1) | copy-start | bytes 7864324
  4.5 4.4 %collective-permute-start.1 = (f32[4,8,80]{2,1,0:T(8,128)S(1)}, f32[4,8,80]{2,1,0:T(8,128)S(1)}, u32[]{:S(2)}, u32[]{:S(2)}) collective-permute-start(f32[4,8,80]{2,1,0:T(8,128)S(1)} %select.1.dep_ref.refs_7_), channel_id=1, source_target_pairs={{0,2},{2,0},{4,6},{6,4},{8,10},{10,8},{12,14},{14,12},{1,3},{3,1},... | collective-permute-start | bytes 30728 | tf_op jit(solution)/shard_map/ppermute | solution.py:409
  8.9 4.1 %collective-permute-start.3 = (bf16[256,2688]{1,0:T(8,128)(2,1)S(1)}, bf16[256,2688]{1,0:T(8,128)(2,1)S(1)}, u32[]{:S(2)}, u32[]{:S(2)}) collective-permute-start(bf16[256,2688]{1,0:T(8,128)(2,1)S(1)} %get-tuple-element.35), channel_id=1, source_target_pairs={{0,1},{1,0},{2,3},{3,2},{4,5},{5,4},{6,7},{7,6},{8,9},{9,8},{10,11... | collective-permute-start | bytes 4128776 | tf_op jit(solution)/shard_map/ppermute | solution.py:416
  9.2 3.8 %collective-permute-start.2 = (f32[4,8,80]{2,1,0:T(8,128)S(1)}, f32[4,8,80]{2,1,0:T(8,128)S(1)}, u32[]{:S(2)}, u32[]{:S(2)}) collective-permute-start(f32[4,8,80]{2,1,0:T(8,128)S(1)} %add.9), channel_id=1, source_target_pairs={{0,4},{2,6},{4,0},{6,2},{8,12},{10,14},{12,8},{14,10},{1,5},{3,7},... | collective-permute-start | bytes 30728 | tf_op jit(solution)/shard_map/ppermute | solution.py:409
  11.0 4.8 %copy-start.1 = (bf16[128,256]{1,0:T(8,128)(2,1)S(1)}, bf16[128,256]{1,0:T(8,128)(2,1)}, u32[]{:S(2)}) copy-start(bf16[128,256]{1,0:T(8,128)(2,1)} %refs_8_.1) | copy-start | bytes 196612
  13.0 4.7 %collective-permute-start.4 = (f32[4,8,80]{2,1,0:T(8,128)S(1)}, f32[4,8,80]{2,1,0:T(8,128)S(1)}, u32[]{:S(2)}, u32[]{:S(2)}) collective-permute-start(f32[4,8,80]{2,1,0:T(8,128)S(1)} %add.10.refs_11_), channel_id=1, source_target_pairs={{0,8},{2,10},{4,12},{6,14},{8,0},{10,2},{12,4},{14,6},{1,9},{3,11}... | collective-permute-start | bytes 30728 | tf_op jit(solution)/shard_map/ppermute | solution.py:409

commit v5 on v4

--- a/solution.py
+++ b/solution.py
@@ -227,135 +227,6 @@
     return outs
 
 
-class Writer:
-    def __init__(self, buf, out, sems):
-        self.buf, self.out, self.sems, self.copies = buf, out, sems, []
-
-    def put(self, start, stop):
-        at = pl.ds(start * SIDE, (stop - start) * SIDE)
-        copy = pltpu.make_async_copy(self.buf.at[:, at], self.out.at[:, at], self.sems.at[len(self.copies)])
-        copy.start()
-        self.copies.append(copy)
-
-    def wait(self):
-        for copy in self.copies:
-            copy.wait()
-
-
-STEP = 2
-FIRST = 14
-
-
-def remain_blocks(t_ref, lt_ref, sec_ref, gt_ref, m_ref, own_ref, peer_ref, c_ref, buf, writer, start, stop):
-    blocks = lt_ref.shape[0]
-    c = -flat(c_ref)
-    for j in range(start, stop):
-        x = pick(t_ref, own_ref, peer_ref, j, blocks // 2)
-        cols = slice(j * SIDE, (j + 1) * SIDE)
-        grad = mm(gt_ref[...], x)
-        less = decoded(lt_ref[j], sec_ref[j], column(c, j))
-        for p in range(2):
-            at = slice(p * LANES, (p + 1) * LANES)
-            moved = decay_rate * m_ref[at, cols].astype(f32) + grad[at]
-            buf[at, cols] = (moved + less[p]).astype(bf16)
-        if (j + 1 - start) % STEP == 0 or j + 1 == stop:
-            writer.put(j - (j - start) % STEP, j + 1)
-
-
-def remain_kernel(stop, *refs):
-    *ins, out_ref, buf, sems = refs
-    writer = Writer(buf, out_ref, sems)
-    remain_blocks(*ins, buf, writer, 0, stop)
-    writer.wait()
-
-
-def remain(stop, t, lt, sec, gt, m, own, peer, c):
-    return call(
-        functools.partial(remain_kernel, stop),
-        "remain",
-        flops=2 * 10**9,
-        nbytes=8 * 10**6,
-        in_specs=[SCALAR] + whole(7),
-        out_specs=anywhere(1)[0],
-        out_shape=jax.ShapeDtypeStruct(m.shape, bf16),
-        scratch_shapes=[pltpu.VMEM(m.shape, bf16), pltpu.SemaphoreType.DMA((stop,))],
-    )(t, *vmem(lt, sec, gt, m, own, peer, c))
-
-
-def finish_kernel(start, *refs):
-    *ins, g_ref, w_ref, wp_ref, dep_ref, begun_ref, out_ref, in_ref, buf, in_buf, sems, in_sems = refs
-    t_ref = ins[0]
-    blocks = ins[1].shape[0]
-    writer = Writer(buf, out_ref, sems)
-    remain_blocks(*ins, buf, writer, start, blocks)
-    width = in_buf.shape[1]
-    g = jnp.concatenate([g_ref[...], wp_ref[:, width:].T], axis=1)
-    in_writer = Writer(in_buf, in_ref, in_sems)
-    for n in range(width // SIDE):
-        at = slice(n * SIDE, (n + 1) * SIDE)
-        mine, _ = halves(t_ref, width, n * SIDE, SIDE)
-        w = jnp.concatenate([w_ref[:, mine], wp_ref[:, at]], axis=0)
-        in_buf[:, at] = mm(g, w).astype(bf16)
-        if n % STEP == STEP - 1:
-            in_writer.put(n + 1 - STEP, n + 1)
-    writer.wait()
-    in_writer.wait()
-
-
-def finish(start, begun, t, lt, sec, gt, m, own, peer, c, g, w, wp, dep):
-    shape = (g.shape[0], w.shape[1] // 2)
-    return call(
-        functools.partial(finish_kernel, start),
-        "finish",
-        flops=10**9,
-        nbytes=8 * 10**6,
-        in_specs=[SCALAR] + whole(10) + anywhere(2),
-        out_specs=anywhere(2),
-        out_shape=[jax.ShapeDtypeStruct(m.shape, bf16), jax.ShapeDtypeStruct(shape, bf16)],
-        scratch_shapes=[
-            pltpu.VMEM(m.shape, bf16),
-            pltpu.VMEM(shape, bf16),
-            pltpu.SemaphoreType.DMA((lt.shape[0],)),
-            pltpu.SemaphoreType.DMA((shape[1] // SIDE,)),
-        ],
-        input_output_aliases={12: 0},
-    )(t, *vmem(lt, sec, gt, m, own, peer, c, g, w, wp), dep, begun)
-
-
-def update_kernel(scale, lt_ref, sec_ref, sum_ref, out_ref, mean_ref, buf, mean, sems):
-    blocks = lt_ref.shape[0]
-    mean[...] = sum_ref[...] * scale
-    writer = Writer(buf, out_ref, sems)
-    pooled = pltpu.make_async_copy(mean, mean_ref, sems.at[blocks])
-    pooled.start()
-    c = flat(mean)
-    for j in range(blocks):
-        out = decoded(lt_ref[j], sec_ref[j], column(c, j))
-        for p in range(2):
-            buf[p * LANES : (p + 1) * LANES, j * SIDE : (j + 1) * SIDE] = out[p].astype(bf16)
-        if (j + 1) % STEP == 0:
-            writer.put(j + 1 - STEP, j + 1)
-    writer.wait()
-    pooled.wait()
-
-
-def update(lt, sec, total, replicas, shape):
-    return call(
-        functools.partial(update_kernel, 1.0 / replicas),
-        "update",
-        flops=10**9,
-        nbytes=6 * 10**6,
-        in_specs=whole(3),
-        out_specs=anywhere(2),
-        out_shape=[jax.ShapeDtypeStruct(shape, bf16), jax.ShapeDtypeStruct(total.shape, f32)],
-        scratch_shapes=[
-            pltpu.VMEM(shape, bf16),
-            pltpu.VMEM(total.shape, f32),
-            pltpu.SemaphoreType.DMA((lt.shape[0] + 1,)),
-        ],
-    )(*vmem(lt, sec, total))
-
-
 def halves(t_ref, width, at, size):
     t = t_ref[0]
     mine = pl.ds(pl.multiple_of(t * width + at, LANES), size)
@@ -363,34 +234,196 @@
     return mine, theirs
 
 
-def keys_kernel(t_ref, own_ref, peer_ref, w_ref, gt_ref, dep_ref, out_ref, part_ref, sems):
+class Writer:
+    def __init__(self, sems):
+        self.sems, self.copies = sems, []
+
+    def put(self, src, dst):
+        copy = pltpu.make_async_copy(src, dst, self.sems.at[len(self.copies)])
+        copy.start()
+        self.copies.append(copy)
+
+    def wait(self):
+        for copy in self.copies:
+            copy.wait()
+
+
+STEP = 2
+HEAD = 6
+BODY = 12
+CARRY = 2
+
+
+def columns(start, stop):
+    return pl.ds(start * SIDE, (stop - start) * SIDE)
+
+
+def remain_block(refs, j, put):
+    t_ref, lt_ref, sec_ref, gt_ref, m_ref, own_ref, peer_ref, c_ref = refs
+    x = pick(t_ref, own_ref, peer_ref, j, lt_ref.shape[0] // 2)
+    cols = slice(j * SIDE, (j + 1) * SIDE)
+    grad = mm(gt_ref[...], x)
+    less = decoded(lt_ref[j], sec_ref[j], column(-flat(c_ref), j))
+    for p in range(2):
+        at = slice(p * LANES, (p + 1) * LANES)
+        moved = decay_rate * m_ref[at, cols].astype(f32) + grad[at]
+        put(at, (moved + less[p]).astype(bf16))
+
+
+def store_at(ref, n):
+    def put(at, value):
+        ref[at, n * SIDE : (n + 1) * SIDE] = value
+
+    return put
+
+
+def keys_kernel(*refs):
+    *ins, w_ref, out_ref, part_ref, head_ref = refs
+    t_ref, gt_ref, own_ref, peer_ref = ins[0], ins[3], ins[5], ins[6]
     width = own_ref.shape[1]
     mine, theirs = halves(t_ref, width, 0, width)
-    copies = [
-        pltpu.make_async_copy(w_ref.at[:, theirs], part_ref.at[:, :width], sems.at[0]),
-        pltpu.make_async_copy(gt_ref, part_ref.at[:, width:], sems.at[1]),
-    ]
-    for copy in copies:
-        copy.start()
-    out_ref[...] = (mm_t(own_ref[...], w_ref[:, mine]) + mm_t(peer_ref[...], w_ref[:, theirs])).astype(bf16)
-    for copy in copies:
-        copy.wait()
-
-
-def keys_of(t, own, peer, w, gt, dep):
+    away = w_ref[:, theirs]
+    part_ref[:, :width] = away
+    part_ref[:, width:] = gt_ref[...]
+    out_ref[...] = (mm_t(w_ref[:, mine], own_ref[...]) + mm_t(away, peer_ref[...])).T.astype(bf16)
+    for j in range(HEAD):
+        remain_block(ins, j, store_at(head_ref, j))
+
+
+def keys_of(t, lt, sec, gt, m, own, peer, c, w):
     return call(
         keys_kernel,
         "keys",
-        flops=2 * own.shape[0] * w.shape[0] * w.shape[1],
+        flops=10**9,
         nbytes=4 * 10**6,
-        in_specs=[SCALAR] + whole(4) + anywhere(1),
-        out_specs=whole(1) + anywhere(1),
+        in_specs=[SCALAR] + whole(8),
+        out_specs=whole(3),
         out_shape=[
-            jax.ShapeDtypeStruct((own.shape[0], w.shape[0]), bf16),
-            jax.ShapeDtypeStruct((w.shape[0], own.shape[1] + gt.shape[1]), bf16),
-        ],
-        scratch_shapes=[pltpu.SemaphoreType.DMA((2,))],
-    )(t, *vmem(own, peer, w, gt), dep)
+            VMEM((own.shape[0], w.shape[0]), bf16),
+            VMEM((w.shape[0], own.shape[1] + gt.shape[1]), bf16),
+            VMEM((m.shape[0], HEAD * SIDE), bf16),
+        ],
+    )(t, *vmem(lt, sec, gt, m, own, peer, c, w))
+
+
+def remain_kernel(*refs):
+    *ins, keys_ref, head_ref, keys_out, out_ref, carry_ref, buf, sems = refs
+    writer = Writer(sems)
+    writer.put(head_ref, out_ref.at[:, columns(0, HEAD)])
+    writer.put(keys_ref, keys_out)
+    stop = HEAD + BODY - CARRY
+    begun = HEAD
+    for j in range(HEAD, stop):
+        remain_block(ins, j, store_at(buf, j))
+        if (j + 1 - begun) == STEP or j + 1 == stop:
+            at = columns(begun, j + 1)
+            writer.put(buf.at[:, at], out_ref.at[:, at])
+            begun = j + 1
+    for n in range(CARRY):
+        remain_block(ins, stop + n, store_at(carry_ref, n))
+    writer.wait()
+
+
+def remain(t, lt, sec, gt, m, own, peer, c, keys, head):
+    return call(
+        remain_kernel,
+        "remain",
+        flops=2 * 10**10,
+        nbytes=8 * 10**6,
+        in_specs=[SCALAR] + whole(9),
+        out_specs=anywhere(2) + whole(1),
+        out_shape=[
+            jax.ShapeDtypeStruct(keys.shape, bf16),
+            jax.ShapeDtypeStruct(m.shape, bf16),
+            VMEM((m.shape[0], CARRY * SIDE), bf16),
+        ],
+        scratch_shapes=[pltpu.VMEM(m.shape, bf16), pltpu.SemaphoreType.DMA((BODY + 2,))],
+    )(t, *vmem(lt, sec, gt, m, own, peer, c, keys, head))
+
+
+def finish_kernel(*refs):
+    *ins, carry_ref, g_ref, w_ref, dep_ref, begun_ref, out_ref, part_ref, buf, sems = refs
+    t_ref = ins[0]
+    blocks = ins[1].shape[0]
+    start = HEAD + BODY
+    writer = Writer(sems)
+    writer.put(carry_ref, out_ref.at[:, columns(start - CARRY, start)])
+    begun = start
+    for j in range(start, blocks):
+        remain_block(ins, j, store_at(buf, j))
+        if (j + 1 - begun) == STEP or j + 1 == blocks:
+            at = columns(begun, j + 1)
+            writer.put(buf.at[:, at], out_ref.at[:, at])
+            begun = j + 1
+    width = part_ref.shape[1]
+    for n in range(width // SIDE):
+        mine, _ = halves(t_ref, width, n * SIDE, SIDE)
+        part_ref[:, n * SIDE : (n + 1) * SIDE] = mm(g_ref[...], w_ref[:, mine])
+    writer.wait()
+
+
+def finish(begun, t, lt, sec, gt, m, own, peer, c, carry, g, w, dep):
+    return call(
+        finish_kernel,
+        "finish",
+        flops=10**9,
+        nbytes=8 * 10**6,
+        in_specs=[SCALAR] + whole(10) + anywhere(2),
+        out_specs=anywhere(1) + whole(1),
+        out_shape=[jax.ShapeDtypeStruct(m.shape, bf16), VMEM((g.shape[0], w.shape[1] // 2), f32)],
+        scratch_shapes=[pltpu.VMEM(m.shape, bf16), pltpu.SemaphoreType.DMA((lt.shape[0],))],
+        input_output_aliases={12: 0},
+    )(t, *vmem(lt, sec, gt, m, own, peer, c, carry, g, w), dep, begun)
+
+
+def update_kernel(scale, lt_ref, sec_ref, sum_ref, part_ref, wp_ref, out_ref, mean_ref, in_ref, buf, mean, in_buf, sems):
+    blocks = lt_ref.shape[0]
+    mean[...] = sum_ref[...] * scale
+    writer = Writer(sems)
+    writer.put(mean, mean_ref)
+    c = flat(mean)
+    width = in_buf.shape[1]
+    g = wp_ref[:, width:].T
+    for n in range(width // SIDE):
+        at = slice(n * SIDE, (n + 1) * SIDE)
+        in_buf[:, at] = (part_ref[:, at] + mm(g, wp_ref[:, at])).astype(bf16)
+        if n % STEP == STEP - 1:
+            at = columns(n + 1 - STEP, n + 1)
+            writer.put(in_buf.at[:, at], in_ref.at[:, at])
+    begun = 0
+    for j in range(blocks):
+        out = decoded(lt_ref[j], sec_ref[j], column(c, j))
+        for p in range(2):
+            buf[p * LANES : (p + 1) * LANES, j * SIDE : (j + 1) * SIDE] = out[p].astype(bf16)
+        if j == 0 or (j + 1 - begun) == STEP or j + 1 == blocks:
+            at = columns(begun, j + 1)
+            writer.put(buf.at[:, at], out_ref.at[:, at])
+            begun = j + 1
+    writer.wait()
+
+
+def update(lt, sec, total, part, wp, replicas, shape):
+    blocks = lt.shape[0]
+    assert blocks * SIDE == 2 * part.shape[1]
+    return call(
+        functools.partial(update_kernel, 1.0 / replicas),
+        "update",
+        flops=10**9,
+        nbytes=6 * 10**6,
+        in_specs=whole(5),
+        out_specs=anywhere(3),
+        out_shape=[
+            jax.ShapeDtypeStruct(shape, bf16),
+            jax.ShapeDtypeStruct(total.shape, f32),
+            jax.ShapeDtypeStruct(part.shape, bf16),
+        ],
+        scratch_shapes=[
+            pltpu.VMEM(shape, bf16),
+            pltpu.VMEM(total.shape, f32),
+            pltpu.VMEM(part.shape, bf16),
+            pltpu.SemaphoreType.DMA((2 * blocks,)),
+        ],
+    )(*vmem(lt, sec, total, part, wp))
 
 
 def shards(tokens, cotangent, key_weight, momentum, indices):
@@ -405,26 +438,30 @@
     total = select(t, sel, sec, m_in, own, peer, idx.shape)
     mine = total
 
-    def exchange(x, step):
-        return lax.ppermute(x, "replica", [(i, i ^ step) for i in range(replicas)])
-
-    steps = [1 << k for k in range(replicas.bit_length() - 1)]
-    split_at = FIRST
-    got = exchange(total, steps[0])
-    keys, w_part = keys_of(t, own, peer, key_weight, gt, total)
-    total, keys, w_part = lax.optimization_barrier((total + got, keys, w_part))
+    rounds = replicas.bit_length() - 1
+
+    def exchange(x, n):
+        step = 1 << n
+        if rounds > 1 and n in (0, rounds - 1):
+            pairs = [(2 * r + c, 2 * (r ^ step) + 1 - c) for r in range(replicas) for c in range(2)]
+            return lax.ppermute(x, ("replica", "tensor"), pairs), lax.ppermute(x, "tensor", swap)
+        return lax.ppermute(x, "replica", [(r, r ^ step) for r in range(replicas)]), x
+
+    shared = (t, lt, sec, gt, m_in, own, peer, mine)
+    far, near = exchange(total, 0)
+    keys, w_part, head = keys_of(*shared, key_weight)
+    total, keys, w_part = lax.optimization_barrier((near + far, keys, w_part))
+    for n in range(1, rounds - 2):
+        far, near = exchange(total, n)
+        total = far + near
+    far, near = exchange(total, rounds - 2)
     w_peer = lax.ppermute(w_part, "tensor", swap)
-    got = exchange(total, steps[1])
-    begun = remain(split_at, t, lt, sec, gt, m_in, own, peer, mine)
-    total, begun, w_peer = lax.optimization_barrier((total + got, begun, w_peer))
-    got = exchange(total, steps[2])
-    remaining, input_grad = finish(
-        split_at, begun, t, lt, sec, gt, m_in, own, peer, mine, cotangent, key_weight, w_peer, total
-    )
-    total, input_grad = lax.optimization_barrier((total + got, input_grad))
-    for step in steps[3:]:
-        total = total + exchange(total, step)
-    new_update, pooled = update(lt, sec, total, replicas, m.shape)
+    keys, begun, carry = remain(*shared, keys, head)
+    begun, total = lax.optimization_barrier((begun, near + far))
+    far, near = exchange(total, rounds - 1)
+    remaining, part = finish(begun, *shared, carry, cotangent, key_weight, total)
+    remaining, total = lax.optimization_barrier((remaining, near + far))
+    new_update, pooled, input_grad = update(lt, sec, total, part, w_peer, replicas, m.shape)
     return (keys, input_grad, remaining[None], new_update, pooled.transpose(0, 2, 1))
 
 

time: 20 us -> 19.1 us (0.955)
  Pallas kernels: 11 us -> 9.98 us
    pallas_call x3, Pallas kernels: 5.68 us -> 4.42 us  [the longest x1 1.78 us: remain(): call(remain_kernel, 'remain', flops=2 * 10 ** 10, nbytes=8 * 10 ** 6, in_...]
    pallas_call x1, Pallas kernels: 2 us -> 2.29 us  [update(): call(functools.partial(update_kernel, 1.0 / replicas), 'update', flops=10...]
    ppermute x3 -> x5, starting transfers between devices: 7.18 us -> 7.29 us  [the longest x2 5.23 us: exchange(): lax.ppermute(x, ('replica', 'tensor'), pairs)]
  transfers between devices with their start and end apart: 5 -> 7, of which waited for: 0 -> 1; matrix products, arithmetic and copies ran while one was open for 0% -> 0% of each run, Pallas kernels for 40% -> 35%
where the time goes in v5:
time: 19.1 us; the launch traced here: 18.9 us
  Pallas kernels  9.98 us (52%)
  starting transfers between devices  8.01 us (42%)
  between operations  0.72 us (4%)
    ppermute x2, starting transfers between devices, exchange(): lax.ppermute(x, ('replica', 'tensor'), pairs)  5.23 us
    pallas_call x1, Pallas kernels, update(): call(functools.partial(update_kernel, 1.0 / replicas), 'update', flops=10...  2.29 us
    pallas_call x1, Pallas kernels, plan(): call(plan_kernel, 'plan', flops=2 * 10 ** 9, nbytes=4 * 10 ** 6, in_specs...  2.27 us
    pallas_call x1, Pallas kernels, remain(): call(remain_kernel, 'remain', flops=2 * 10 ** 10, nbytes=8 * 10 ** 6, in_...  1.78 us
    ppermute x1, starting transfers between devices, exchange(): lax.ppermute(x, 'replica', [(r, r ^ step) for r in range(replicas)])  1.75 us
    pallas_call x1, Pallas kernels, keys_of(): call(keys_kernel, 'keys', flops=10 ** 9, nbytes=4 * 10 ** 6, in_specs=[SC...  1.35 us
    pallas_call x1, Pallas kernels, finish(): call(finish_kernel, 'finish', flops=10 ** 9, nbytes=8 * 10 ** 6, in_specs...  1.29 us
    pallas_call x1, Pallas kernels, select(): call(select_kernel, 'select', flops=10 ** 9, nbytes=6 * 10 ** 6, in_specs...  0.99 us
  transfers between devices with their start and end apart: 7, of which 1 were waited for; matrix products, arithmetic and copies ran while one was open for 0% of the time, Pallas kernels for 35%

profile of v5, /device:TPU:0, one launch (start us, length us, event | category | flops | bytes accessed | tf_op | source)
XLA Modules:
  0.0 18.9 jit_solution(17005510453394483057)
XLA Ops:
  0.6 0.5 %collective-permute-start = (bf16[128,2560]{1,0:T(8,128)(2,1)}, bf16[128,2560]{1,0:T(8,128)(2,1)S(1)}, u32[]{:S(2)}, u32[]{:S(2)}) collective-permute-start(bf16[128,2560]{1,0:T(8,128)(2,1)} %x_hbm.1), channel_id=1, source_target_pairs={{0,1},{1,0},{2,3},{3,2},{4,5},{5,4},{6,7},{7,6},{8,9},{9,8},{10,11... | collective-permute-start | bytes 1966088 | tf_op jit(solution)/shard_map/ppermute | solution.py:433
  1.1 2.3 %plan.1 = (bf16[20,2,128,256]{3,2,1,0:T(8,128)(2,1)S(1)}, f32[20,128,128]{2,1,0:T(8,128)S(1)}, bf16[20,2,128,128]{3,2,1,0:T(8,128)(2,1)S(1)}, bf16[256,128]{1,0:...) custom-call(s32[4,8,80]{2,1,0:T(8,128)} %bitcast.7, f32[64,128]{1,0:T(8,128)} %constant.6.clone.tab_hbm, ...), custom_call_target="tpu_custom_call" | custom-call | flops 2000000000 | bytes 4000000 | tf_op jit(solution)/shard_map/plan/pallas_call | solution.py:147
  3.4 0.0 collective-permute-done.peer_ref.refs_6_
  3.4 0.0 copy-start
  3.5 1.0 %select.1.refs_7_ = f32[4,8,80]{2,1,0:T(8,128)S(1)} custom-call(s32[1]{0:T(128)} %bitcast.t_ref.refs_0_, bf16[20,2,128,256]{3,2,1,0:T(8,128)(2,1)S(1)} %get-tuple-element.34.sel_ref, f32[20,128,128]{2,1,0:T(8,128)S(1)} %get-tuple-element.30.sec_ref.refs_2_, bf16[256,5120]{1,0:T(8,128)(2,1)S(1)} %get-tuple-element.32.m_ref.refs_4_, ...), custom_call_target="tpu_custom_call" | custom-call | flops 1000000000 | bytes 6000000 | tf_op jit(solution)/shard_map/select/pallas_call | solution.py:201
  4.4 2.7 %collective-permute-start.2 = (f32[4,8,80]{2,1,0:T(8,128)S(1)}, f32[4,8,80]{2,1,0:T(8,128)S(1)}, u32[]{:S(2)}, u32[]{:S(2)}) collective-permute-start(f32[4,8,80]{2,1,0:T(8,128)S(1)} %select.1.refs_7_), channel_id=1, source_target_pairs={{0,3},{1,2},{2,1},{3,0},{4,7},{5,6},{6,5},{7,4},{8,11},{9,10},{10,... | collective-permute-start | bytes 30728 | tf_op jit(solution)/shard_map/ppermute | solution.py:447
  7.1 0.0 collective-permute-start.1
  7.2 0.0 copy-done
  7.2 1.3 %keys.1 = (bf16[128,256]{1,0:T(8,128)(2,1)S(1)}, bf16[256,2688]{1,0:T(8,128)(2,1)S(1)}, bf16[256,1536]{1,0:T(8,128)(2,1)S(1)}) custom-call(s32[1]{0:T(128)} %bitcast.t_ref.refs_0_, bf16[20,2,128,128]{3,2,1,0:T(8,128)(2,1)S(1)} %get-tuple-element.29.refs_1_.lt_ref, f32[20,128,128]{2,1,0:T(8,128)S(1)} %get-tuple-element.30.sec_ref.refs_2_, ...), custom_call_target="tpu_custom_call" | custom-call | flops 1000000000 | bytes 4000000 | tf_op jit(solution)/shard_map/keys/pallas_call | solution.py:294
  8.5 0.1 collective-permute-done.2
  8.6 0.0 collective-permute-done.1
  8.6 1.7 %collective-permute-start.3 = (f32[4,8,80]{2,1,0:T(8,128)S(1)}, f32[4,8,80]{2,1,0:T(8,128)S(1)}, u32[]{:S(2)}, u32[]{:S(2)}) collective-permute-start(f32[4,8,80]{2,1,0:T(8,128)S(1)} %add.9), channel_id=1, source_target_pairs={{0,4},{2,6},{4,0},{6,2},{8,12},{10,14},{12,8},{14,10},{1,5},{3,7},... | collective-permute-start | bytes 30728 | tf_op jit(solution)/shard_map/ppermute | solution.py:448
  10.3 0.2 %collective-permute-start.6 = (bf16[256,2688]{1,0:T(8,128)(2,1)S(1)}, bf16[256,2688]{1,0:T(8,128)(2,1)S(1)}, u32[]{:S(2)}, u32[]{:S(2)}) collective-permute-start(bf16[256,2688]{1,0:T(8,128)(2,1)S(1)} %get-tuple-element.48), channel_id=1, source_target_pairs={{0,1},{1,0},{2,3},{3,2},{4,5},{5,4},{6,7},{7,6},{8,9},{9,8},{10,11... | collective-permute-start | bytes 4128776 | tf_op jit(solution)/shard_map/ppermute | solution.py:458
  10.6 0.0 copy-start.1
  10.6 1.8 %remain.1 = (bf16[128,256]{1,0:T(8,128)(2,1)}, bf16[256,5120]{1,0:T(8,128)(2,1)}, bf16[256,512]{1,0:T(8,128)(2,1)S(1)}) custom-call(s32[1]{0:T(128)} %bitcast.t_ref.refs_0_, bf16[20,2,128,128]{3,2,1,0:T(8,128)(2,1)S(1)} %get-tuple-element.29.refs_1_.lt_ref, f32[20,128,128]{2,1,0:T(8,128)S(1)} %get-tuple-element.30.sec_ref.refs_2_, ...), custom_call_target="tpu_custom_call" | custom-call | flops 20000000000 | bytes 8000000 | tf_op jit(solution)/shard_map/remain/pallas_call | solution.py:328
  12.3 0.0 collective-permute-done.3
  12.4 2.5 %collective-permute-start.5 = (f32[4,8,80]{2,1,0:T(8,128)S(1)}, f32[4,8,80]{2,1,0:T(8,128)S(1)}, u32[]{:S(2)}, u32[]{:S(2)}) collective-permute-start(f32[4,8,80]{2,1,0:T(8,128)S(1)} %add.10.refs_11_), channel_id=1, source_target_pairs={{0,9},{1,8},{2,11},{3,10},{4,13},{5,12},{6,15},{7,14},{8,1},{9,0},... | collective-permute-start | bytes 30728 | tf_op jit(solution)/shard_map/ppermute | solution.py:447
  14.9 0.3 %collective-permute-start.4 = (f32[4,8,80]{2,1,0:T(8,128)S(1)}, f32[4,8,80]{2,1,0:T(8,128)S(1)}, u32[]{:S(2)}, u32[]{:S(2)}) collective-permute-start(f32[4,8,80]{2,1,0:T(8,128)S(1)} %add.10.refs_11_), channel_id=1, source_target_pairs={{0,1},{1,0},{2,3},{3,2},{4,5},{5,4},{6,7},{7,6},{8,9},{9,8},{10,11... | collective-permute-start | bytes 30728 | tf_op jit(solution)/shard_map/ppermute | solution.py:447
  15.2 0.0 copy-done.1
  15.2 1.3 %finish.1 = (bf16[256,5120]{1,0:T(8,128)(2,1)}, f32[128,2560]{1,0:T(8,128)S(1)}) custom-call(s32[1]{0:T(128)} %bitcast.t_ref.refs_0_, bf16[20,2,128,128]{3,2,1,0:T(8,128)(2,1)S(1)} %get-tuple-element.29.refs_1_.lt_ref, f32[20,128,128]{2,1,0:T(8,128)S(1)} %get-tuple-element.30.sec_ref.refs_2_, ...), custom_call_target="tpu_custom_call", output_to_operand_aliasing={{0}: (12, {})} | custom-call | flops 1000000000 | bytes 8000000 | tf_op jit(solution)/shard_map/finish/pallas_call | solution.py:366
  16.5 0.0 collective-permute-done.5
  16.5 0.0 collective-permute-done.4
  16.6 0.0 collective-permute-done.6.wp_ref
  16.6 2.3 %update.1 = (bf16[256,5120]{1,0:T(8,128)(2,1)}, f32[4,8,80]{2,1,0:T(8,128)}, bf16[128,2560]{1,0:T(8,128)(2,1)}) custom-call(bf16[20,2,128,128]{3,2,1,0:T(8,128)(2,1)S(1)} %get-tuple-element.29.refs_1_.lt_ref, f32[20,128,128]{2,1,0:T(8,128)S(1)} %get-tuple-element.30.sec_ref.refs_2_, f32[4,8,80]{2,1,0:T(8,128)S(1)} %add.11.sum_ref, ...), custom_call_target="tpu_custom_call" | custom-call | flops 1000000000 | bytes 6000000 | tf_op jit(solution)/shard_map/update/pallas_call | solution.py:408
  (3 shorter events, 0.0 us)
Async XLA Ops:
  0.6 2.8 %collective-permute-start = (bf16[128,2560]{1,0:T(8,128)(2,1)}, bf16[128,2560]{1,0:T(8,128)(2,1)S(1)}, u32[]{:S(2)}, u32[]{:S(2)}) collective-permute-start(bf16[128,2560]{1,0:T(8,128)(2,1)} %x_hbm.1), channel_id=1, source_target_pairs={{0,1},{1,0},{2,3},{3,2},{4,5},{5,4},{6,7},{7,6},{8,9},{9,8},{10,11... | collective-permute-start | bytes 1966088 | tf_op jit(solution)/shard_map/ppermute | solution.py:433
  3.4 3.7 %copy-start = (bf16[256,5120]{1,0:T(8,128)(2,1)S(1)}, bf16[256,5120]{1,0:T(8,128)(2,1)}, u32[]{:S(2)}) copy-start(bf16[256,5120]{1,0:T(8,128)(2,1)} %refs_10_.1) | copy-start | bytes 7864324
  4.4 4.1 %collective-permute-start.2 = (f32[4,8,80]{2,1,0:T(8,128)S(1)}, f32[4,8,80]{2,1,0:T(8,128)S(1)}, u32[]{:S(2)}, u32[]{:S(2)}) collective-permute-start(f32[4,8,80]{2,1,0:T(8,128)S(1)} %select.1.refs_7_), channel_id=1, source_target_pairs={{0,3},{1,2},{2,1},{3,0},{4,7},{5,6},{6,5},{7,4},{8,11},{9,10},{10,... | collective-permute-start | bytes 30728 | tf_op jit(solution)/shard_map/ppermute | solution.py:447
  7.1 1.4 %collective-permute-start.1 = (f32[4,8,80]{2,1,0:T(8,128)S(1)}, f32[4,8,80]{2,1,0:T(8,128)S(1)}, u32[]{:S(2)}, u32[]{:S(2)}) collective-permute-start(f32[4,8,80]{2,1,0:T(8,128)S(1)} %select.1.refs_7_), channel_id=1, source_target_pairs={{0,1},{1,0},{2,3},{3,2},{4,5},{5,4},{6,7},{7,6},{8,9},{9,8},{10,11... | collective-permute-start | bytes 30728 | tf_op jit(solution)/shard_map/ppermute | solution.py:447
  8.6 3.8 %collective-permute-start.3 = (f32[4,8,80]{2,1,0:T(8,128)S(1)}, f32[4,8,80]{2,1,0:T(8,128)S(1)}, u32[]{:S(2)}, u32[]{:S(2)}) collective-permute-start(f32[4,8,80]{2,1,0:T(8,128)S(1)} %add.9), channel_id=1, source_target_pairs={{0,4},{2,6},{4,0},{6,2},{8,12},{10,14},{12,8},{14,10},{1,5},{3,7},... | collective-permute-start | bytes 30728 | tf_op jit(solution)/shard_map/ppermute | solution.py:448
  10.3 6.2 %collective-permute-start.6 = (bf16[256,2688]{1,0:T(8,128)(2,1)S(1)}, bf16[256,2688]{1,0:T(8,128)(2,1)S(1)}, u32[]{:S(2)}, u32[]{:S(2)}) collective-permute-start(bf16[256,2688]{1,0:T(8,128)(2,1)S(1)} %get-tuple-element.48), channel_id=1, source_target_pairs={{0,1},{1,0},{2,3},{3,2},{4,5},{5,4},{6,7},{7,6},{8,9},{9,8},{10,11... | collective-permute-start | bytes 4128776 | tf_op jit(solution)/shard_map/ppermute | solution.py:458
  10.6 4.7 %copy-start.1 = (bf16[128,256]{1,0:T(8,128)(2,1)S(1)}, bf16[128,256]{1,0:T(8,128)(2,1)}, u32[]{:S(2)}) copy-start(bf16[128,256]{1,0:T(8,128)(2,1)} %refs_9_.1) | copy-start | bytes 196612
  12.4 4.1 %collective-permute-start.5 = (f32[4,8,80]{2,1,0:T(8,128)S(1)}, f32[4,8,80]{2,1,0:T(8,128)S(1)}, u32[]{:S(2)}, u32[]{:S(2)}) collective-permute-start(f32[4,8,80]{2,1,0:T(8,128)S(1)} %add.10.refs_11_), channel_id=1, source_target_pairs={{0,9},{1,8},{2,11},{3,10},{4,13},{5,12},{6,15},{7,14},{8,1},{9,0},... | collective-permute-start | bytes 30728 | tf_op jit(solution)/shard_map/ppermute | solution.py:447
  14.9 1.6 %collective-permute-start.4 = (f32[4,8,80]{2,1,0:T(8,128)S(1)}, f32[4,8,80]{2,1,0:T(8,128)S(1)}, u32[]{:S(2)}, u32[]{:S(2)}) collective-permute-start(f32[4,8,80]{2,1,0:T(8,128)S(1)} %add.10.refs_11_), channel_id=1, source_target_pairs={{0,1},{1,0},{2,3},{3,2},{4,5},{5,4},{6,7},{7,6},{8,9},{9,8},{10,11... | collective-permute-start | bytes 30728 | tf_op jit(solution)/shard_map/ppermute | solution.py:447

commit v6 on v5

--- a/solution.py
+++ b/solution.py
@@ -119,19 +119,22 @@
     hi, lo = [jnp.concatenate([part, part], axis=0) for part in (hi, lo)]
     row_tab = jnp.concatenate([hi, ghi, lo, glo], axis=1)
     none = jnp.zeros((half, LANES), bf16)
-    for j in range(0, blocks, 2):
-        cols = [column(z, k) for k in (j, j + 1)]
+    group = 10
+    for j in range(0, blocks, group):
+        cols = [column(z, k) for k in range(j, j + group)]
         one_b = [jnp.where((col & (SPAN - 1)) == lane_in, 1.0, 0.0).astype(bf16) for col in cols]
-        sec = mm(jnp.concatenate(one_b, axis=1), col_tab)
-        for k in range(2):
-            sec_ref[j + k] = jnp.where(mine, sec[:, k * LANES : (k + 1) * LANES], 0.0)
-            one = jnp.where((cols[k] >> 6) == place, 1.0, 0.0).astype(bf16)
-            one_a = jnp.concatenate(
-                [jnp.concatenate([one[:half], none], axis=1), jnp.concatenate([none, one[half:]], axis=1)], axis=0
-            )
-            rows = mm(one_a, row_tab).astype(bf16)
+        one_a = []
+        for col in cols:
+            one = jnp.where((col >> 6) == place, 1.0, 0.0).astype(bf16)
+            one_a.append(jnp.concatenate([one[:half], none], axis=1))
+            one_a.append(jnp.concatenate([none, one[half:]], axis=1))
+        pairs = [jnp.concatenate(one_b[k : k + 2], axis=1) for k in range(0, group, 2)]
+        sec = mm(jnp.concatenate(pairs, axis=0), col_tab)
+        rows = mm(jnp.concatenate(one_a, axis=0), row_tab).astype(bf16)
+        for k in range(group):
+            sec_ref[j + k] = jnp.where(mine, sec[k // 2 * kept : (k // 2 + 1) * kept, k % 2 * LANES : (k % 2 + 1) * LANES], 0.0)
             for p in range(2):
-                at = slice(p * half, (p + 1) * half)
+                at = slice(k * kept + p * half, k * kept + (p + 1) * half)
                 sel_ref[j + k, p, :half, :] = rows[at, :SIDE]
                 sel_ref[j + k, p, half:, :] = rows[at, SIDE:]
                 lt_ref[j + k, p] = jnp.concatenate([rows[at, :LANES], rows[at, SIDE : SIDE + LANES]], axis=0).T
@@ -395,7 +398,7 @@
         out = decoded(lt_ref[j], sec_ref[j], column(c, j))
         for p in range(2):
             buf[p * LANES : (p + 1) * LANES, j * SIDE : (j + 1) * SIDE] = out[p].astype(bf16)
-        if j == 0 or (j + 1 - begun) == STEP or j + 1 == blocks:
+        if j == 0 or (j + 1 - begun) == STEP or j + 2 >= blocks:
             at = columns(begun, j + 1)
             writer.put(buf.at[:, at], out_ref.at[:, at])
             begun = j + 1

time: 19.1 us -> 19.1 us (level)
  transfers between devices with their start and end apart: 7 -> 7, of which waited for: 1 -> 0; matrix products, arithmetic and copies ran while one was open for 0% -> 0% of each run, Pallas kernels for 35% -> 35%
where the time goes in v6:
time: 19.1 us; the launch traced here: 18.8 us
  Pallas kernels  9.92 us (52%)
  starting transfers between devices  8.07 us (42%)
  between operations  0.72 us (4%)
    ppermute x2, starting transfers between devices, exchange(): lax.ppermute(x, ('replica', 'tensor'), pairs)  5.26 us
    pallas_call x1, Pallas kernels, update(): call(functools.partial(update_kernel, 1.0 / replicas), 'update', flops=10...  2.29 us
    pallas_call x1, Pallas kernels, plan(): call(plan_kernel, 'plan', flops=2 * 10 ** 9, nbytes=4 * 10 ** 6, in_specs...  2.22 us
    pallas_call x1, Pallas kernels, remain(): call(remain_kernel, 'remain', flops=2 * 10 ** 10, nbytes=8 * 10 ** 6, in_...  1.78 us
    ppermute x1, starting transfers between devices, exchange(): lax.ppermute(x, 'replica', [(r, r ^ step) for r in range(replicas)])  1.78 us
    pallas_call x1, Pallas kernels, keys_of(): call(keys_kernel, 'keys', flops=10 ** 9, nbytes=4 * 10 ** 6, in_specs=[SC...  1.35 us
    pallas_call x1, Pallas kernels, finish(): call(finish_kernel, 'finish', flops=10 ** 9, nbytes=8 * 10 ** 6, in_specs...  1.29 us
    pallas_call x1, Pallas kernels, select(): call(select_kernel, 'select', flops=10 ** 9, nbytes=6 * 10 ** 6, in_specs...  0.99 us
  transfers between devices with their start and end apart: 7, of which 0 were waited for; matrix products, arithmetic and copies ran while one was open for 0% of the time, Pallas kernels for 35%

profile of v6, /device:TPU:0, one launch (start us, length us, event | category | flops | bytes accessed | tf_op | source)
XLA Modules:
  0.0 18.8 jit_solution(3706976987726017951)
XLA Ops:
  0.6 0.5 %collective-permute-start = (bf16[128,2560]{1,0:T(8,128)(2,1)}, bf16[128,2560]{1,0:T(8,128)(2,1)S(1)}, u32[]{:S(2)}, u32[]{:S(2)}) collective-permute-start(bf16[128,2560]{1,0:T(8,128)(2,1)} %x_hbm.1), channel_id=1, source_target_pairs={{0,1},{1,0},{2,3},{3,2},{4,5},{5,4},{6,7},{7,6},{8,9},{9,8},{10,11... | collective-permute-start | bytes 1966088 | tf_op jit(solution)/shard_map/ppermute | solution.py:436
  1.1 2.2 %plan.1 = (bf16[20,2,128,256]{3,2,1,0:T(8,128)(2,1)S(1)}, f32[20,128,128]{2,1,0:T(8,128)S(1)}, bf16[20,2,128,128]{3,2,1,0:T(8,128)(2,1)S(1)}, bf16[256,128]{1,0:...) custom-call(s32[4,8,80]{2,1,0:T(8,128)} %bitcast.7, f32[64,128]{1,0:T(8,128)} %constant.6.clone.tab_hbm, ...), custom_call_target="tpu_custom_call" | custom-call | flops 2000000000 | bytes 4000000 | tf_op jit(solution)/shard_map/plan/pallas_call | solution.py:150
  3.4 0.0 collective-permute-done.peer_ref.refs_6_
  3.4 0.0 copy-start
  3.4 1.0 %select.1.refs_7_ = f32[4,8,80]{2,1,0:T(8,128)S(1)} custom-call(s32[1]{0:T(128)} %bitcast.t_ref.refs_0_, bf16[20,2,128,256]{3,2,1,0:T(8,128)(2,1)S(1)} %get-tuple-element.34.sel_ref, f32[20,128,128]{2,1,0:T(8,128)S(1)} %get-tuple-element.30.sec_ref.refs_2_, bf16[256,5120]{1,0:T(8,128)(2,1)S(1)} %get-tuple-element.32.m_ref.refs_4_, ...), custom_call_target="tpu_custom_call" | custom-call | flops 1000000000 | bytes 6000000 | tf_op jit(solution)/shard_map/select/pallas_call | solution.py:204
  4.4 2.7 %collective-permute-start.2 = (f32[4,8,80]{2,1,0:T(8,128)S(1)}, f32[4,8,80]{2,1,0:T(8,128)S(1)}, u32[]{:S(2)}, u32[]{:S(2)}) collective-permute-start(f32[4,8,80]{2,1,0:T(8,128)S(1)} %select.1.refs_7_), channel_id=1, source_target_pairs={{0,3},{1,2},{2,1},{3,0},{4,7},{5,6},{6,5},{7,4},{8,11},{9,10},{10,... | collective-permute-start | bytes 30728 | tf_op jit(solution)/shard_map/ppermute | solution.py:450
  7.1 0.1 collective-permute-start.1
  7.1 0.0 copy-done
  7.1 1.3 %keys.1 = (bf16[128,256]{1,0:T(8,128)(2,1)S(1)}, bf16[256,2688]{1,0:T(8,128)(2,1)S(1)}, bf16[256,1536]{1,0:T(8,128)(2,1)S(1)}) custom-call(s32[1]{0:T(128)} %bitcast.t_ref.refs_0_, bf16[20,2,128,128]{3,2,1,0:T(8,128)(2,1)S(1)} %get-tuple-element.29.refs_1_.lt_ref, f32[20,128,128]{2,1,0:T(8,128)S(1)} %get-tuple-element.30.sec_ref.refs_2_, ...), custom_call_target="tpu_custom_call" | custom-call | flops 1000000000 | bytes 4000000 | tf_op jit(solution)/shard_map/keys/pallas_call | solution.py:297
  8.5 0.0 collective-permute-done.2
  8.5 0.0 collective-permute-done.1
  8.5 1.8 %collective-permute-start.3 = (f32[4,8,80]{2,1,0:T(8,128)S(1)}, f32[4,8,80]{2,1,0:T(8,128)S(1)}, u32[]{:S(2)}, u32[]{:S(2)}) collective-permute-start(f32[4,8,80]{2,1,0:T(8,128)S(1)} %add.9), channel_id=1, source_target_pairs={{0,4},{2,6},{4,0},{6,2},{8,12},{10,14},{12,8},{14,10},{1,5},{3,7},... | collective-permute-start | bytes 30728 | tf_op jit(solution)/shard_map/ppermute | solution.py:451
  10.3 0.2 collective-permute-start.6
  10.5 0.0 copy-start.1
  10.5 1.8 %remain.1 = (bf16[128,256]{1,0:T(8,128)(2,1)}, bf16[256,5120]{1,0:T(8,128)(2,1)}, bf16[256,512]{1,0:T(8,128)(2,1)S(1)}) custom-call(s32[1]{0:T(128)} %bitcast.t_ref.refs_0_, bf16[20,2,128,128]{3,2,1,0:T(8,128)(2,1)S(1)} %get-tuple-element.29.refs_1_.lt_ref, f32[20,128,128]{2,1,0:T(8,128)S(1)} %get-tuple-element.30.sec_ref.refs_2_, ...), custom_call_target="tpu_custom_call" | custom-call | flops 20000000000 | bytes 8000000 | tf_op jit(solution)/shard_map/remain/pallas_call | solution.py:331
  12.3 0.0 collective-permute-done.3
  12.3 2.6 %collective-permute-start.5 = (f32[4,8,80]{2,1,0:T(8,128)S(1)}, f32[4,8,80]{2,1,0:T(8,128)S(1)}, u32[]{:S(2)}, u32[]{:S(2)}) collective-permute-start(f32[4,8,80]{2,1,0:T(8,128)S(1)} %add.10.refs_11_), channel_id=1, source_target_pairs={{0,9},{1,8},{2,11},{3,10},{4,13},{5,12},{6,15},{7,14},{8,1},{9,0},... | collective-permute-start | bytes 30728 | tf_op jit(solution)/shard_map/ppermute | solution.py:450
  14.9 0.3 %collective-permute-start.4 = (f32[4,8,80]{2,1,0:T(8,128)S(1)}, f32[4,8,80]{2,1,0:T(8,128)S(1)}, u32[]{:S(2)}, u32[]{:S(2)}) collective-permute-start(f32[4,8,80]{2,1,0:T(8,128)S(1)} %add.10.refs_11_), channel_id=1, source_target_pairs={{0,1},{1,0},{2,3},{3,2},{4,5},{5,4},{6,7},{7,6},{8,9},{9,8},{10,11... | collective-permute-start | bytes 30728 | tf_op jit(solution)/shard_map/ppermute | solution.py:450
  15.2 0.0 copy-done.1
  15.2 1.3 %finish.1 = (bf16[256,5120]{1,0:T(8,128)(2,1)}, f32[128,2560]{1,0:T(8,128)S(1)}) custom-call(s32[1]{0:T(128)} %bitcast.t_ref.refs_0_, bf16[20,2,128,128]{3,2,1,0:T(8,128)(2,1)S(1)} %get-tuple-element.29.refs_1_.lt_ref, f32[20,128,128]{2,1,0:T(8,128)S(1)} %get-tuple-element.30.sec_ref.refs_2_, ...), custom_call_target="tpu_custom_call", output_to_operand_aliasing={{0}: (12, {})} | custom-call | flops 1000000000 | bytes 8000000 | tf_op jit(solution)/shard_map/finish/pallas_call | solution.py:369
  16.5 0.0 collective-permute-done.5
  16.5 0.0 collective-permute-done.4
  16.5 0.0 collective-permute-done.6.wp_ref
  16.5 2.3 %update.1 = (bf16[256,5120]{1,0:T(8,128)(2,1)}, f32[4,8,80]{2,1,0:T(8,128)}, bf16[128,2560]{1,0:T(8,128)(2,1)}) custom-call(bf16[20,2,128,128]{3,2,1,0:T(8,128)(2,1)S(1)} %get-tuple-element.29.refs_1_.lt_ref, f32[20,128,128]{2,1,0:T(8,128)S(1)} %get-tuple-element.30.sec_ref.refs_2_, f32[4,8,80]{2,1,0:T(8,128)S(1)} %add.11.sum_ref, ...), custom_call_target="tpu_custom_call" | custom-call | flops 1000000000 | bytes 6000000 | tf_op jit(solution)/shard_map/update/pallas_call | solution.py:411
  (3 shorter events, 0.0 us)
Async XLA Ops:
  0.6 2.8 %collective-permute-start = (bf16[128,2560]{1,0:T(8,128)(2,1)}, bf16[128,2560]{1,0:T(8,128)(2,1)S(1)}, u32[]{:S(2)}, u32[]{:S(2)}) collective-permute-start(bf16[128,2560]{1,0:T(8,128)(2,1)} %x_hbm.1), channel_id=1, source_target_pairs={{0,1},{1,0},{2,3},{3,2},{4,5},{5,4},{6,7},{7,6},{8,9},{9,8},{10,11... | collective-permute-start | bytes 1966088 | tf_op jit(solution)/shard_map/ppermute | solution.py:436
  3.4 3.8 %copy-start = (bf16[256,5120]{1,0:T(8,128)(2,1)S(1)}, bf16[256,5120]{1,0:T(8,128)(2,1)}, u32[]{:S(2)}) copy-start(bf16[256,5120]{1,0:T(8,128)(2,1)} %refs_10_.1) | copy-start | bytes 7864324
  4.4 4.1 %collective-permute-start.2 = (f32[4,8,80]{2,1,0:T(8,128)S(1)}, f32[4,8,80]{2,1,0:T(8,128)S(1)}, u32[]{:S(2)}, u32[]{:S(2)}) collective-permute-start(f32[4,8,80]{2,1,0:T(8,128)S(1)} %select.1.refs_7_), channel_id=1, source_target_pairs={{0,3},{1,2},{2,1},{3,0},{4,7},{5,6},{6,5},{7,4},{8,11},{9,10},{10,... | collective-permute-start | bytes 30728 | tf_op jit(solution)/shard_map/ppermute | solution.py:450
  7.1 1.4 %collective-permute-start.1 = (f32[4,8,80]{2,1,0:T(8,128)S(1)}, f32[4,8,80]{2,1,0:T(8,128)S(1)}, u32[]{:S(2)}, u32[]{:S(2)}) collective-permute-start(f32[4,8,80]{2,1,0:T(8,128)S(1)} %select.1.refs_7_), channel_id=1, source_target_pairs={{0,1},{1,0},{2,3},{3,2},{4,5},{5,4},{6,7},{7,6},{8,9},{9,8},{10,11... | collective-permute-start | bytes 30728 | tf_op jit(solution)/shard_map/ppermute | solution.py:450
  8.5 3.8 %collective-permute-start.3 = (f32[4,8,80]{2,1,0:T(8,128)S(1)}, f32[4,8,80]{2,1,0:T(8,128)S(1)}, u32[]{:S(2)}, u32[]{:S(2)}) collective-permute-start(f32[4,8,80]{2,1,0:T(8,128)S(1)} %add.9), channel_id=1, source_target_pairs={{0,4},{2,6},{4,0},{6,2},{8,12},{10,14},{12,8},{14,10},{1,5},{3,7},... | collective-permute-start | bytes 30728 | tf_op jit(solution)/shard_map/ppermute | solution.py:451
  10.3 6.2 %collective-permute-start.6 = (bf16[256,2688]{1,0:T(8,128)(2,1)S(1)}, bf16[256,2688]{1,0:T(8,128)(2,1)S(1)}, u32[]{:S(2)}, u32[]{:S(2)}) collective-permute-start(bf16[256,2688]{1,0:T(8,128)(2,1)S(1)} %get-tuple-element.48), channel_id=1, source_target_pairs={{0,1},{1,0},{2,3},{3,2},{4,5},{5,4},{6,7},{7,6},{8,9},{9,8},{10,11... | collective-permute-start | bytes 4128776 | tf_op jit(solution)/shard_map/ppermute | solution.py:461
  10.5 4.7 %copy-start.1 = (bf16[128,256]{1,0:T(8,128)(2,1)S(1)}, bf16[128,256]{1,0:T(8,128)(2,1)}, u32[]{:S(2)}) copy-start(bf16[128,256]{1,0:T(8,128)(2,1)} %refs_9_.1) | copy-start | bytes 196612
  12.3 4.2 %collective-permute-start.5 = (f32[4,8,80]{2,1,0:T(8,128)S(1)}, f32[4,8,80]{2,1,0:T(8,128)S(1)}, u32[]{:S(2)}, u32[]{:S(2)}) collective-permute-start(f32[4,8,80]{2,1,0:T(8,128)S(1)} %add.10.refs_11_), channel_id=1, source_target_pairs={{0,9},{1,8},{2,11},{3,10},{4,13},{5,12},{6,15},{7,14},{8,1},{9,0},... | collective-permute-start | bytes 30728 | tf_op jit(solution)/shard_map/ppermute | solution.py:450
  14.9 1.6 %collective-permute-start.4 = (f32[4,8,80]{2,1,0:T(8,128)S(1)}, f32[4,8,80]{2,1,0:T(8,128)S(1)}, u32[]{:S(2)}, u32[]{:S(2)}) collective-permute-start(f32[4,8,80]{2,1,0:T(8,128)S(1)} %add.10.refs_11_), channel_id=1, source_target_pairs={{0,1},{1,0},{2,3},{3,2},{4,5},{5,4},{6,7},{7,6},{8,9},{9,8},{10,11... | collective-permute-start | bytes 30728 | tf_op jit(solution)/shard_map/ppermute | solution.py:450

commit v7 on v6

--- a/solution.py
+++ b/solution.py
@@ -379,9 +379,9 @@
     )(t, *vmem(lt, sec, gt, m, own, peer, c, carry, g, w), dep, begun)
 
 
-def update_kernel(scale, lt_ref, sec_ref, sum_ref, part_ref, wp_ref, out_ref, mean_ref, in_ref, buf, mean, in_buf, sems):
+def update_kernel(scale, lt_ref, sec_ref, near_ref, far_ref, part_ref, wp_ref, out_ref, mean_ref, in_ref, buf, mean, in_buf, sems):
     blocks = lt_ref.shape[0]
-    mean[...] = sum_ref[...] * scale
+    mean[...] = (near_ref[...] + far_ref[...]) * scale
     writer = Writer(sems)
     writer.put(mean, mean_ref)
     c = flat(mean)
@@ -405,7 +405,7 @@
     writer.wait()
 
 
-def update(lt, sec, total, part, wp, replicas, shape):
+def update(lt, sec, near, far, part, wp, replicas, shape):
     blocks = lt.shape[0]
     assert blocks * SIDE == 2 * part.shape[1]
     return call(
@@ -413,20 +413,20 @@
         "update",
         flops=10**9,
         nbytes=6 * 10**6,
-        in_specs=whole(5),
+        in_specs=whole(6),
         out_specs=anywhere(3),
         out_shape=[
             jax.ShapeDtypeStruct(shape, bf16),
-            jax.ShapeDtypeStruct(total.shape, f32),
+            jax.ShapeDtypeStruct(near.shape, f32),
             jax.ShapeDtypeStruct(part.shape, bf16),
         ],
         scratch_shapes=[
             pltpu.VMEM(shape, bf16),
-            pltpu.VMEM(total.shape, f32),
+            pltpu.VMEM(near.shape, f32),
             pltpu.VMEM(part.shape, bf16),
             pltpu.SemaphoreType.DMA((2 * blocks,)),
         ],
-    )(*vmem(lt, sec, total, part, wp))
+    )(*vmem(lt, sec, near, far, part, wp))
 
 
 def shards(tokens, cotangent, key_weight, momentum, indices):
@@ -444,7 +444,7 @@
     rounds = replicas.bit_length() - 1
 
     def exchange(x, n):
-        step = 1 << n
+        step = 1 << ((n + 1) % rounds)
         if rounds > 1 and n in (0, rounds - 1):
             pairs = [(2 * r + c, 2 * (r ^ step) + 1 - c) for r in range(replicas) for c in range(2)]
             return lax.ppermute(x, ("replica", "tensor"), pairs), lax.ppermute(x, "tensor", swap)
@@ -463,8 +463,8 @@
     begun, total = lax.optimization_barrier((begun, near + far))
     far, near = exchange(total, rounds - 1)
     remaining, part = finish(begun, *shared, carry, cotangent, key_weight, total)
-    remaining, total = lax.optimization_barrier((remaining, near + far))
-    new_update, pooled, input_grad = update(lt, sec, total, part, w_peer, replicas, m.shape)
+    remaining, near, far = lax.optimization_barrier((remaining, near, far))
+    new_update, pooled, input_grad = update(lt, sec, near, far, part, w_peer, replicas, m.shape)
     return (keys, input_grad, remaining[None], new_update, pooled.transpose(0, 2, 1))
 
 

time: 19.1 us -> 19.1 us (level)
    ppermute x2, starting transfers between devices: 5.26 us -> 4.27 us  [exchange(): lax.ppermute(x, ('replica', 'tensor'), pairs)]
    ppermute x1, starting transfers between devices: 1.78 us -> 2.74 us  [exchange(): lax.ppermute(x, 'replica', [(r, r ^ step) for r in range(replicas)])]
    ppermute x2, waiting for transfers between devices: 0.04 us -> 0.26 us  [exchange(): lax.ppermute(x, ('replica', 'tensor'), pairs)]
  transfers between devices with their start and end apart: 7 -> 7, of which waited for: 0 -> 1; matrix products, arithmetic and copies ran while one was open for 0% -> 0% of each run, Pallas kernels for 35% -> 35%
where the time goes in v7:
time: 19.1 us; the launch traced here: 18.9 us
  Pallas kernels  9.93 us (52%)
  starting transfers between devices  7.94 us (42%)
  between operations  0.7 us (4%)
  waiting for transfers between devices  0.28 us (1%)
    ppermute x2, starting transfers between devices, exchange(): lax.ppermute(x, ('replica', 'tensor'), pairs)  4.27 us
    ppermute x1, starting transfers between devices, exchange(): lax.ppermute(x, 'replica', [(r, r ^ step) for r in range(replicas)])  2.74 us
    pallas_call x1, Pallas kernels, update(): call(functools.partial(update_kernel, 1.0 / replicas), 'update', flops=10...  2.29 us
    pallas_call x1, Pallas kernels, plan(): call(plan_kernel, 'plan', flops=2 * 10 ** 9, nbytes=4 * 10 ** 6, in_specs...  2.22 us
    pallas_call x1, Pallas kernels, remain(): call(remain_kernel, 'remain', flops=2 * 10 ** 10, nbytes=8 * 10 ** 6, in_...  1.78 us
    pallas_call x1, Pallas kernels, keys_of(): call(keys_kernel, 'keys', flops=10 ** 9, nbytes=4 * 10 ** 6, in_specs=[SC...  1.35 us
    pallas_call x1, Pallas kernels, finish(): call(finish_kernel, 'finish', flops=10 ** 9, nbytes=8 * 10 ** 6, in_specs...  1.29 us
    pallas_call x1, Pallas kernels, select(): call(select_kernel, 'select', flops=10 ** 9, nbytes=6 * 10 ** 6, in_specs...  0.99 us
  transfers between devices with their start and end apart: 7, of which 1 were waited for; matrix products, arithmetic and copies ran while one was open for 0% of the time, Pallas kernels for 35%

profile of v7, /device:TPU:0, one launch (start us, length us, event | category | flops | bytes accessed | tf_op | source)
XLA Modules:
  0.0 18.9 jit_solution(2099254088118595025)
XLA Ops:
  0.6 0.5 %collective-permute-start = (bf16[128,2560]{1,0:T(8,128)(2,1)}, bf16[128,2560]{1,0:T(8,128)(2,1)S(1)}, u32[]{:S(2)}, u32[]{:S(2)}) collective-permute-start(bf16[128,2560]{1,0:T(8,128)(2,1)} %x_hbm.1), channel_id=1, source_target_pairs={{0,1},{1,0},{2,3},{3,2},{4,5},{5,4},{6,7},{7,6},{8,9},{9,8},{10,11... | collective-permute-start | bytes 1966088 | tf_op jit(solution)/shard_map/ppermute | solution.py:436
  1.1 2.2 %plan.1 = (bf16[20,2,128,256]{3,2,1,0:T(8,128)(2,1)S(1)}, f32[20,128,128]{2,1,0:T(8,128)S(1)}, bf16[20,2,128,128]{3,2,1,0:T(8,128)(2,1)S(1)}, bf16[256,128]{1,0:...) custom-call(s32[4,8,80]{2,1,0:T(8,128)} %bitcast.7, f32[64,128]{1,0:T(8,128)} %constant.6.clone.tab_hbm, ...), custom_call_target="tpu_custom_call" | custom-call | flops 2000000000 | bytes 4000000 | tf_op jit(solution)/shard_map/plan/pallas_call | solution.py:150
  3.4 0.0 collective-permute-done.peer_ref.refs_6_
  3.4 0.0 copy-start
  3.4 1.0 %select.1.refs_7_ = f32[4,8,80]{2,1,0:T(8,128)S(1)} custom-call(s32[1]{0:T(128)} %bitcast.t_ref.refs_0_, bf16[20,2,128,256]{3,2,1,0:T(8,128)(2,1)S(1)} %get-tuple-element.35.sel_ref, f32[20,128,128]{2,1,0:T(8,128)S(1)} %get-tuple-element.31.sec_ref.refs_2_, bf16[256,5120]{1,0:T(8,128)(2,1)S(1)} %get-tuple-element.33.m_ref.refs_4_, ...), custom_call_target="tpu_custom_call" | custom-call | flops 1000000000 | bytes 6000000 | tf_op jit(solution)/shard_map/select/pallas_call | solution.py:204
  4.4 2.8 %collective-permute-start.2 = (f32[4,8,80]{2,1,0:T(8,128)S(1)}, f32[4,8,80]{2,1,0:T(8,128)S(1)}, u32[]{:S(2)}, u32[]{:S(2)}) collective-permute-start(f32[4,8,80]{2,1,0:T(8,128)S(1)} %select.1.refs_7_), channel_id=1, source_target_pairs={{0,5},{1,4},{2,7},{3,6},{4,1},{5,0},{6,3},{7,2},{8,13},{9,12},{10,... | collective-permute-start | bytes 30728 | tf_op jit(solution)/shard_map/ppermute | solution.py:450
  7.1 0.1 collective-permute-start.1
  7.2 0.0 copy-done
  7.2 1.3 %keys.1 = (bf16[128,256]{1,0:T(8,128)(2,1)S(1)}, bf16[256,2688]{1,0:T(8,128)(2,1)S(1)}, bf16[256,1536]{1,0:T(8,128)(2,1)S(1)}) custom-call(s32[1]{0:T(128)} %bitcast.t_ref.refs_0_, bf16[20,2,128,128]{3,2,1,0:T(8,128)(2,1)S(1)} %get-tuple-element.30.refs_1_.lt_ref, f32[20,128,128]{2,1,0:T(8,128)S(1)} %get-tuple-element.31.sec_ref.refs_2_, ...), custom_call_target="tpu_custom_call" | custom-call | flops 1000000000 | bytes 4000000 | tf_op jit(solution)/shard_map/keys/pallas_call | solution.py:297
  8.6 0.0 collective-permute-done.2
  8.6 0.0 collective-permute-done.1
  8.6 2.7 %collective-permute-start.3 = (f32[4,8,80]{2,1,0:T(8,128)S(1)}, f32[4,8,80]{2,1,0:T(8,128)S(1)}, u32[]{:S(2)}, u32[]{:S(2)}) collective-permute-start(f32[4,8,80]{2,1,0:T(8,128)S(1)} %add.6), channel_id=1, source_target_pairs={{0,8},{2,10},{4,12},{6,14},{8,0},{10,2},{12,4},{14,6},{1,9},{3,11}... | collective-permute-start | bytes 30728 | tf_op jit(solution)/shard_map/ppermute | solution.py:451
  11.3 0.2 collective-permute-start.6
  11.5 0.0 copy-start.1
  11.5 1.8 %remain.1 = (bf16[128,256]{1,0:T(8,128)(2,1)}, bf16[256,5120]{1,0:T(8,128)(2,1)}, bf16[256,512]{1,0:T(8,128)(2,1)S(1)}) custom-call(s32[1]{0:T(128)} %bitcast.t_ref.refs_0_, bf16[20,2,128,128]{3,2,1,0:T(8,128)(2,1)S(1)} %get-tuple-element.30.refs_1_.lt_ref, f32[20,128,128]{2,1,0:T(8,128)S(1)} %get-tuple-element.31.sec_ref.refs_2_, ...), custom_call_target="tpu_custom_call" | custom-call | flops 20000000000 | bytes 8000000 | tf_op jit(solution)/shard_map/remain/pallas_call | solution.py:331
  13.3 0.0 collective-permute-done.3
  13.3 1.5 %collective-permute-start.5 = (f32[4,8,80]{2,1,0:T(8,128)S(1)}, f32[4,8,80]{2,1,0:T(8,128)S(1)}, u32[]{:S(2)}, u32[]{:S(2)}) collective-permute-start(f32[4,8,80]{2,1,0:T(8,128)S(1)} %add.7.refs_11_), channel_id=1, source_target_pairs={{0,3},{1,2},{2,1},{3,0},{4,7},{5,6},{6,5},{7,4},{8,11},{9,10},{10,... | collective-permute-start | bytes 30728 | tf_op jit(solution)/shard_map/ppermute | solution.py:450
  14.9 0.2 collective-permute-start.4
  15.0 0.0 copy-done.1
  15.0 1.3 %finish.1 = (bf16[256,5120]{1,0:T(8,128)(2,1)}, f32[128,2560]{1,0:T(8,128)S(1)}) custom-call(s32[1]{0:T(128)} %bitcast.t_ref.refs_0_, bf16[20,2,128,128]{3,2,1,0:T(8,128)(2,1)S(1)} %get-tuple-element.30.refs_1_.lt_ref, f32[20,128,128]{2,1,0:T(8,128)S(1)} %get-tuple-element.31.sec_ref.refs_2_, ...), custom_call_target="tpu_custom_call", output_to_operand_aliasing={{0}: (12, {})} | custom-call | flops 1000000000 | bytes 8000000 | tf_op jit(solution)/shard_map/finish/pallas_call | solution.py:369
  16.3 0.2 %collective-permute-done.5.far_ref = f32[4,8,80]{2,1,0:T(8,128)S(1)} collective-permute-done((f32[4,8,80]{2,1,0:T(8,128)S(1)}, f32[4,8,80]{2,1,0:T(8,128)S(1)}, u32[]{:S(2)}, u32[]{:S(2)}) %collective-permute-start.5) | collective-permute-done | bytes 10272 | tf_op jit(solution)/shard_map/ppermute | solution.py:450
  16.6 0.0 collective-permute-done.4.near_ref
  16.6 0.0 collective-permute-done.6.wp_ref
  16.6 2.3 %update.1 = (bf16[256,5120]{1,0:T(8,128)(2,1)}, f32[4,8,80]{2,1,0:T(8,128)}, bf16[128,2560]{1,0:T(8,128)(2,1)}) custom-call(bf16[20,2,128,128]{3,2,1,0:T(8,128)(2,1)S(1)} %get-tuple-element.30.refs_1_.lt_ref, f32[20,128,128]{2,1,0:T(8,128)S(1)} %get-tuple-element.31.sec_ref.refs_2_, f32[4,8,80]{2,1,0:T(8,128)S(1)} %collective-permute-done.4.near_ref, ...), custom_call_target="tpu_custom_call" | custom-call | flops 1000000000 | bytes 6000000 | tf_op jit(solution)/shard_map/update/pallas_call | solution.py:411
  (2 shorter events, 0.0 us)
Async XLA Ops:
  0.6 2.8 %collective-permute-start = (bf16[128,2560]{1,0:T(8,128)(2,1)}, bf16[128,2560]{1,0:T(8,128)(2,1)S(1)}, u32[]{:S(2)}, u32[]{:S(2)}) collective-permute-start(bf16[128,2560]{1,0:T(8,128)(2,1)} %x_hbm.1), channel_id=1, source_target_pairs={{0,1},{1,0},{2,3},{3,2},{4,5},{5,4},{6,7},{7,6},{8,9},{9,8},{10,11... | collective-permute-start | bytes 1966088 | tf_op jit(solution)/shard_map/ppermute | solution.py:436
  3.4 3.8 %copy-start = (bf16[256,5120]{1,0:T(8,128)(2,1)S(1)}, bf16[256,5120]{1,0:T(8,128)(2,1)}, u32[]{:S(2)}) copy-start(bf16[256,5120]{1,0:T(8,128)(2,1)} %refs_10_.1) | copy-start | bytes 7864324
  4.4 4.2 %collective-permute-start.2 = (f32[4,8,80]{2,1,0:T(8,128)S(1)}, f32[4,8,80]{2,1,0:T(8,128)S(1)}, u32[]{:S(2)}, u32[]{:S(2)}) collective-permute-start(f32[4,8,80]{2,1,0:T(8,128)S(1)} %select.1.refs_7_), channel_id=1, source_target_pairs={{0,5},{1,4},{2,7},{3,6},{4,1},{5,0},{6,3},{7,2},{8,13},{9,12},{10,... | collective-permute-start | bytes 30728 | tf_op jit(solution)/shard_map/ppermute | solution.py:450
  7.1 1.4 %collective-permute-start.1 = (f32[4,8,80]{2,1,0:T(8,128)S(1)}, f32[4,8,80]{2,1,0:T(8,128)S(1)}, u32[]{:S(2)}, u32[]{:S(2)}) collective-permute-start(f32[4,8,80]{2,1,0:T(8,128)S(1)} %select.1.refs_7_), channel_id=1, source_target_pairs={{0,1},{1,0},{2,3},{3,2},{4,5},{5,4},{6,7},{7,6},{8,9},{9,8},{10,11... | collective-permute-start | bytes 30728 | tf_op jit(solution)/shard_map/ppermute | solution.py:450
  8.6 4.7 %collective-permute-start.3 = (f32[4,8,80]{2,1,0:T(8,128)S(1)}, f32[4,8,80]{2,1,0:T(8,128)S(1)}, u32[]{:S(2)}, u32[]{:S(2)}) collective-permute-start(f32[4,8,80]{2,1,0:T(8,128)S(1)} %add.6), channel_id=1, source_target_pairs={{0,8},{2,10},{4,12},{6,14},{8,0},{10,2},{12,4},{14,6},{1,9},{3,11}... | collective-permute-start | bytes 30728 | tf_op jit(solution)/shard_map/ppermute | solution.py:451
  11.3 5.2 %collective-permute-start.6 = (bf16[256,2688]{1,0:T(8,128)(2,1)S(1)}, bf16[256,2688]{1,0:T(8,128)(2,1)S(1)}, u32[]{:S(2)}, u32[]{:S(2)}) collective-permute-start(bf16[256,2688]{1,0:T(8,128)(2,1)S(1)} %get-tuple-element.50), channel_id=1, source_target_pairs={{0,1},{1,0},{2,3},{3,2},{4,5},{5,4},{6,7},{7,6},{8,9},{9,8},{10,11... | collective-permute-start | bytes 4128776 | tf_op jit(solution)/shard_map/ppermute | solution.py:461
  11.5 3.5 %copy-start.1 = (bf16[128,256]{1,0:T(8,128)(2,1)S(1)}, bf16[128,256]{1,0:T(8,128)(2,1)}, u32[]{:S(2)}) copy-start(bf16[128,256]{1,0:T(8,128)(2,1)} %refs_9_.1) | copy-start | bytes 196612
  13.3 3.2 %collective-permute-start.5 = (f32[4,8,80]{2,1,0:T(8,128)S(1)}, f32[4,8,80]{2,1,0:T(8,128)S(1)}, u32[]{:S(2)}, u32[]{:S(2)}) collective-permute-start(f32[4,8,80]{2,1,0:T(8,128)S(1)} %add.7.refs_11_), channel_id=1, source_target_pairs={{0,3},{1,2},{2,1},{3,0},{4,7},{5,6},{6,5},{7,4},{8,11},{9,10},{10,... | collective-permute-start | bytes 30728 | tf_op jit(solution)/shard_map/ppermute | solution.py:450
  14.9 1.7 %collective-permute-start.4 = (f32[4,8,80]{2,1,0:T(8,128)S(1)}, f32[4,8,80]{2,1,0:T(8,128)S(1)}, u32[]{:S(2)}, u32[]{:S(2)}) collective-permute-start(f32[4,8,80]{2,1,0:T(8,128)S(1)} %add.7.refs_11_), channel_id=1, source_target_pairs={{0,1},{1,0},{2,3},{3,2},{4,5},{5,4},{6,7},{7,6},{8,9},{9,8},{10,11... | collective-permute-start | bytes 30728 | tf_op jit(solution)/shard_map/ppermute | solution.py:450

commit v8 on v6

--- a/solution.py
+++ b/solution.py
@@ -251,7 +251,7 @@
             copy.wait()
 
 
-STEP = 2
+STEP = 1
 HEAD = 6
 BODY = 12
 CARRY = 2

time: 19.1 us -> 19 us (level)
  no operation moved by 1% of the time
where the time goes in v8:
time: 19 us; the launch traced here: 18.8 us
  Pallas kernels  9.88 us (52%)
  starting transfers between devices  8.07 us (42%)
  between operations  0.7 us (4%)
    ppermute x2, starting transfers between devices, exchange(): lax.ppermute(x, ('replica', 'tensor'), pairs)  5.27 us
    pallas_call x1, Pallas kernels, update(): call(functools.partial(update_kernel, 1.0 / replicas), 'update', flops=10...  2.28 us
    pallas_call x1, Pallas kernels, plan(): call(plan_kernel, 'plan', flops=2 * 10 ** 9, nbytes=4 * 10 ** 6, in_specs...  2.22 us
    pallas_call x1, Pallas kernels, remain(): call(remain_kernel, 'remain', flops=2 * 10 ** 10, nbytes=8 * 10 ** 6, in_...  1.8 us
    ppermute x1, starting transfers between devices, exchange(): lax.ppermute(x, 'replica', [(r, r ^ step) for r in range(replicas)])  1.78 us
    pallas_call x1, Pallas kernels, keys_of(): call(keys_kernel, 'keys', flops=10 ** 9, nbytes=4 * 10 ** 6, in_specs=[SC...  1.35 us
    pallas_call x1, Pallas kernels, finish(): call(finish_kernel, 'finish', flops=10 ** 9, nbytes=8 * 10 ** 6, in_specs...  1.23 us
    pallas_call x1, Pallas kernels, select(): call(select_kernel, 'select', flops=10 ** 9, nbytes=6 * 10 ** 6, in_specs...  0.99 us
  transfers between devices with their start and end apart: 7, of which 0 were waited for; matrix products, arithmetic and copies ran while one was open for 0% of the time, Pallas kernels for 35%

profile of v8, /device:TPU:0, one launch (start us, length us, event | category | flops | bytes accessed | tf_op | source)
XLA Modules:
  0.0 18.8 jit_solution(6719862207292096936)
XLA Ops:
  0.6 0.5 %collective-permute-start = (bf16[128,2560]{1,0:T(8,128)(2,1)}, bf16[128,2560]{1,0:T(8,128)(2,1)S(1)}, u32[]{:S(2)}, u32[]{:S(2)}) collective-permute-start(bf16[128,2560]{1,0:T(8,128)(2,1)} %x_hbm.1), channel_id=1, source_target_pairs={{0,1},{1,0},{2,3},{3,2},{4,5},{5,4},{6,7},{7,6},{8,9},{9,8},{10,11... | collective-permute-start | bytes 1966088 | tf_op jit(solution)/shard_map/ppermute | solution.py:436
  1.1 2.2 %plan.1 = (bf16[20,2,128,256]{3,2,1,0:T(8,128)(2,1)S(1)}, f32[20,128,128]{2,1,0:T(8,128)S(1)}, bf16[20,2,128,128]{3,2,1,0:T(8,128)(2,1)S(1)}, bf16[256,128]{1,0:...) custom-call(s32[4,8,80]{2,1,0:T(8,128)} %bitcast.7, f32[64,128]{1,0:T(8,128)} %constant.6.clone.tab_hbm, ...), custom_call_target="tpu_custom_call" | custom-call | flops 2000000000 | bytes 4000000 | tf_op jit(solution)/shard_map/plan/pallas_call | solution.py:150
  3.4 0.0 collective-permute-done.peer_ref.refs_6_
  3.4 0.0 copy-start
  3.4 1.0 %select.1.refs_7_ = f32[4,8,80]{2,1,0:T(8,128)S(1)} custom-call(s32[1]{0:T(128)} %bitcast.t_ref.refs_0_, bf16[20,2,128,256]{3,2,1,0:T(8,128)(2,1)S(1)} %get-tuple-element.34.sel_ref, f32[20,128,128]{2,1,0:T(8,128)S(1)} %get-tuple-element.30.sec_ref.refs_2_, bf16[256,5120]{1,0:T(8,128)(2,1)S(1)} %get-tuple-element.32.m_ref.refs_4_, ...), custom_call_target="tpu_custom_call" | custom-call | flops 1000000000 | bytes 6000000 | tf_op jit(solution)/shard_map/select/pallas_call | solution.py:204
  4.4 2.7 %collective-permute-start.2 = (f32[4,8,80]{2,1,0:T(8,128)S(1)}, f32[4,8,80]{2,1,0:T(8,128)S(1)}, u32[]{:S(2)}, u32[]{:S(2)}) collective-permute-start(f32[4,8,80]{2,1,0:T(8,128)S(1)} %select.1.refs_7_), channel_id=1, source_target_pairs={{0,3},{1,2},{2,1},{3,0},{4,7},{5,6},{6,5},{7,4},{8,11},{9,10},{10,... | collective-permute-start | bytes 30728 | tf_op jit(solution)/shard_map/ppermute | solution.py:450
  7.1 0.1 collective-permute-start.1
  7.1 0.0 copy-done
  7.1 1.3 %keys.1 = (bf16[128,256]{1,0:T(8,128)(2,1)S(1)}, bf16[256,2688]{1,0:T(8,128)(2,1)S(1)}, bf16[256,1536]{1,0:T(8,128)(2,1)S(1)}) custom-call(s32[1]{0:T(128)} %bitcast.t_ref.refs_0_, bf16[20,2,128,128]{3,2,1,0:T(8,128)(2,1)S(1)} %get-tuple-element.29.refs_1_.lt_ref, f32[20,128,128]{2,1,0:T(8,128)S(1)} %get-tuple-element.30.sec_ref.refs_2_, ...), custom_call_target="tpu_custom_call" | custom-call | flops 1000000000 | bytes 4000000 | tf_op jit(solution)/shard_map/keys/pallas_call | solution.py:297
  8.5 0.0 collective-permute-done.2
  8.5 0.0 collective-permute-done.1
  8.5 1.8 %collective-permute-start.3 = (f32[4,8,80]{2,1,0:T(8,128)S(1)}, f32[4,8,80]{2,1,0:T(8,128)S(1)}, u32[]{:S(2)}, u32[]{:S(2)}) collective-permute-start(f32[4,8,80]{2,1,0:T(8,128)S(1)} %add.9), channel_id=1, source_target_pairs={{0,4},{2,6},{4,0},{6,2},{8,12},{10,14},{12,8},{14,10},{1,5},{3,7},... | collective-permute-start | bytes 30728 | tf_op jit(solution)/shard_map/ppermute | solution.py:451
  10.3 0.2 collective-permute-start.6
  10.5 0.0 copy-start.1
  10.5 1.8 %remain.1 = (bf16[128,256]{1,0:T(8,128)(2,1)}, bf16[256,5120]{1,0:T(8,128)(2,1)}, bf16[256,512]{1,0:T(8,128)(2,1)S(1)}) custom-call(s32[1]{0:T(128)} %bitcast.t_ref.refs_0_, bf16[20,2,128,128]{3,2,1,0:T(8,128)(2,1)S(1)} %get-tuple-element.29.refs_1_.lt_ref, f32[20,128,128]{2,1,0:T(8,128)S(1)} %get-tuple-element.30.sec_ref.refs_2_, ...), custom_call_target="tpu_custom_call" | custom-call | flops 20000000000 | bytes 8000000 | tf_op jit(solution)/shard_map/remain/pallas_call | solution.py:331
  12.3 0.0 collective-permute-done.3
  12.3 2.6 %collective-permute-start.5 = (f32[4,8,80]{2,1,0:T(8,128)S(1)}, f32[4,8,80]{2,1,0:T(8,128)S(1)}, u32[]{:S(2)}, u32[]{:S(2)}) collective-permute-start(f32[4,8,80]{2,1,0:T(8,128)S(1)} %add.10.refs_11_), channel_id=1, source_target_pairs={{0,9},{1,8},{2,11},{3,10},{4,13},{5,12},{6,15},{7,14},{8,1},{9,0},... | collective-permute-start | bytes 30728 | tf_op jit(solution)/shard_map/ppermute | solution.py:450
  14.9 0.3 %collective-permute-start.4 = (f32[4,8,80]{2,1,0:T(8,128)S(1)}, f32[4,8,80]{2,1,0:T(8,128)S(1)}, u32[]{:S(2)}, u32[]{:S(2)}) collective-permute-start(f32[4,8,80]{2,1,0:T(8,128)S(1)} %add.10.refs_11_), channel_id=1, source_target_pairs={{0,1},{1,0},{2,3},{3,2},{4,5},{5,4},{6,7},{7,6},{8,9},{9,8},{10,11... | collective-permute-start | bytes 30728 | tf_op jit(solution)/shard_map/ppermute | solution.py:450
  15.2 0.0 copy-done.1
  15.2 1.2 %finish.1 = (bf16[256,5120]{1,0:T(8,128)(2,1)}, f32[128,2560]{1,0:T(8,128)S(1)}) custom-call(s32[1]{0:T(128)} %bitcast.t_ref.refs_0_, bf16[20,2,128,128]{3,2,1,0:T(8,128)(2,1)S(1)} %get-tuple-element.29.refs_1_.lt_ref, f32[20,128,128]{2,1,0:T(8,128)S(1)} %get-tuple-element.30.sec_ref.refs_2_, ...), custom_call_target="tpu_custom_call", output_to_operand_aliasing={{0}: (12, {})} | custom-call | flops 1000000000 | bytes 8000000 | tf_op jit(solution)/shard_map/finish/pallas_call | solution.py:369
  16.4 0.0 collective-permute-done.5
  16.5 0.0 collective-permute-done.4
  16.5 0.0 collective-permute-done.6.wp_ref
  16.5 2.3 %update.1 = (bf16[256,5120]{1,0:T(8,128)(2,1)}, f32[4,8,80]{2,1,0:T(8,128)}, bf16[128,2560]{1,0:T(8,128)(2,1)}) custom-call(bf16[20,2,128,128]{3,2,1,0:T(8,128)(2,1)S(1)} %get-tuple-element.29.refs_1_.lt_ref, f32[20,128,128]{2,1,0:T(8,128)S(1)} %get-tuple-element.30.sec_ref.refs_2_, f32[4,8,80]{2,1,0:T(8,128)S(1)} %add.11.sum_ref, ...), custom_call_target="tpu_custom_call" | custom-call | flops 1000000000 | bytes 6000000 | tf_op jit(solution)/shard_map/update/pallas_call | solution.py:411
  (3 shorter events, 0.0 us)
Async XLA Ops:
  0.6 2.8 %collective-permute-start = (bf16[128,2560]{1,0:T(8,128)(2,1)}, bf16[128,2560]{1,0:T(8,128)(2,1)S(1)}, u32[]{:S(2)}, u32[]{:S(2)}) collective-permute-start(bf16[128,2560]{1,0:T(8,128)(2,1)} %x_hbm.1), channel_id=1, source_target_pairs={{0,1},{1,0},{2,3},{3,2},{4,5},{5,4},{6,7},{7,6},{8,9},{9,8},{10,11... | collective-permute-start | bytes 1966088 | tf_op jit(solution)/shard_map/ppermute | solution.py:436
  3.4 3.8 %copy-start = (bf16[256,5120]{1,0:T(8,128)(2,1)S(1)}, bf16[256,5120]{1,0:T(8,128)(2,1)}, u32[]{:S(2)}) copy-start(bf16[256,5120]{1,0:T(8,128)(2,1)} %refs_10_.1) | copy-start | bytes 7864324
  4.4 4.1 %collective-permute-start.2 = (f32[4,8,80]{2,1,0:T(8,128)S(1)}, f32[4,8,80]{2,1,0:T(8,128)S(1)}, u32[]{:S(2)}, u32[]{:S(2)}) collective-permute-start(f32[4,8,80]{2,1,0:T(8,128)S(1)} %select.1.refs_7_), channel_id=1, source_target_pairs={{0,3},{1,2},{2,1},{3,0},{4,7},{5,6},{6,5},{7,4},{8,11},{9,10},{10,... | collective-permute-start | bytes 30728 | tf_op jit(solution)/shard_map/ppermute | solution.py:450
  7.1 1.4 %collective-permute-start.1 = (f32[4,8,80]{2,1,0:T(8,128)S(1)}, f32[4,8,80]{2,1,0:T(8,128)S(1)}, u32[]{:S(2)}, u32[]{:S(2)}) collective-permute-start(f32[4,8,80]{2,1,0:T(8,128)S(1)} %select.1.refs_7_), channel_id=1, source_target_pairs={{0,1},{1,0},{2,3},{3,2},{4,5},{5,4},{6,7},{7,6},{8,9},{9,8},{10,11... | collective-permute-start | bytes 30728 | tf_op jit(solution)/shard_map/ppermute | solution.py:450
  8.5 3.8 %collective-permute-start.3 = (f32[4,8,80]{2,1,0:T(8,128)S(1)}, f32[4,8,80]{2,1,0:T(8,128)S(1)}, u32[]{:S(2)}, u32[]{:S(2)}) collective-permute-start(f32[4,8,80]{2,1,0:T(8,128)S(1)} %add.9), channel_id=1, source_target_pairs={{0,4},{2,6},{4,0},{6,2},{8,12},{10,14},{12,8},{14,10},{1,5},{3,7},... | collective-permute-start | bytes 30728 | tf_op jit(solution)/shard_map/ppermute | solution.py:451
  10.3 6.2 %collective-permute-start.6 = (bf16[256,2688]{1,0:T(8,128)(2,1)S(1)}, bf16[256,2688]{1,0:T(8,128)(2,1)S(1)}, u32[]{:S(2)}, u32[]{:S(2)}) collective-permute-start(bf16[256,2688]{1,0:T(8,128)(2,1)S(1)} %get-tuple-element.48), channel_id=1, source_target_pairs={{0,1},{1,0},{2,3},{3,2},{4,5},{5,4},{6,7},{7,6},{8,9},{9,8},{10,11... | collective-permute-start | bytes 4128776 | tf_op jit(solution)/shard_map/ppermute | solution.py:461
  10.5 4.7 %copy-start.1 = (bf16[128,256]{1,0:T(8,128)(2,1)S(1)}, bf16[128,256]{1,0:T(8,128)(2,1)}, u32[]{:S(2)}) copy-start(bf16[128,256]{1,0:T(8,128)(2,1)} %refs_9_.1) | copy-start | bytes 196612
  12.3 4.1 %collective-permute-start.5 = (f32[4,8,80]{2,1,0:T(8,128)S(1)}, f32[4,8,80]{2,1,0:T(8,128)S(1)}, u32[]{:S(2)}, u32[]{:S(2)}) collective-permute-start(f32[4,8,80]{2,1,0:T(8,128)S(1)} %add.10.refs_11_), channel_id=1, source_target_pairs={{0,9},{1,8},{2,11},{3,10},{4,13},{5,12},{6,15},{7,14},{8,1},{9,0},... | collective-permute-start | bytes 30728 | tf_op jit(solution)/shard_map/ppermute | solution.py:450
  14.9 1.5 %collective-permute-start.4 = (f32[4,8,80]{2,1,0:T(8,128)S(1)}, f32[4,8,80]{2,1,0:T(8,128)S(1)}, u32[]{:S(2)}, u32[]{:S(2)}) collective-permute-start(f32[4,8,80]{2,1,0:T(8,128)S(1)} %add.10.refs_11_), channel_id=1, source_target_pairs={{0,1},{1,0},{2,3},{3,2},{4,5},{5,4},{6,7},{7,6},{8,9},{9,8},{10,11... | collective-permute-start | bytes 30728 | tf_op jit(solution)/shard_map/ppermute | solution.py:450

commit v9 on v7

--- a/solution.py
+++ b/solution.py
@@ -444,7 +444,7 @@
     rounds = replicas.bit_length() - 1
 
     def exchange(x, n):
-        step = 1 << ((n + 1) % rounds)
+        step = 1 << n
         if rounds > 1 and n in (0, rounds - 1):
             pairs = [(2 * r + c, 2 * (r ^ step) + 1 - c) for r in range(replicas) for c in range(2)]
             return lax.ppermute(x, ("replica", "tensor"), pairs), lax.ppermute(x, "tensor", swap)

time: 19.1 us -> 19.1 us (level)
    ppermute x2, starting transfers between devices: 4.27 us -> 5.26 us  [exchange(): lax.ppermute(x, ('replica', 'tensor'), pairs)]
    ppermute x1, starting transfers between devices: 2.74 us -> 1.78 us  [exchange(): lax.ppermute(x, 'replica', [(r, r ^ step) for r in range(replicas)])]
    ppermute x2, waiting for transfers between devices: 0.26 us -> 0.04 us  [exchange(): lax.ppermute(x, ('replica', 'tensor'), pairs)]
  transfers between devices with their start and end apart: 7 -> 7, of which waited for: 1 -> 0; matrix products, arithmetic and copies ran while one was open for 0% -> 0% of each run, Pallas kernels for 35% -> 35%
where the time goes in v9:
time: 19.1 us; the launch traced here: 18.8 us
  Pallas kernels  9.92 us (52%)
  starting transfers between devices  8.07 us (42%)
  between operations  0.71 us (4%)
    ppermute x2, starting transfers between devices, exchange(): lax.ppermute(x, ('replica', 'tensor'), pairs)  5.26 us
    pallas_call x1, Pallas kernels, update(): call(functools.partial(update_kernel, 1.0 / replicas), 'update', flops=10...  2.29 us
    pallas_call x1, Pallas kernels, plan(): call(plan_kernel, 'plan', flops=2 * 10 ** 9, nbytes=4 * 10 ** 6, in_specs...  2.22 us
    pallas_call x1, Pallas kernels, remain(): call(remain_kernel, 'remain', flops=2 * 10 ** 10, nbytes=8 * 10 ** 6, in_...  1.78 us
    ppermute x1, starting transfers between devices, exchange(): lax.ppermute(x, 'replica', [(r, r ^ step) for r in range(replicas)])  1.78 us
    pallas_call x1, Pallas kernels, keys_of(): call(keys_kernel, 'keys', flops=10 ** 9, nbytes=4 * 10 ** 6, in_specs=[SC...  1.35 us
    pallas_call x1, Pallas kernels, finish(): call(finish_kernel, 'finish', flops=10 ** 9, nbytes=8 * 10 ** 6, in_specs...  1.29 us
    pallas_call x1, Pallas kernels, select(): call(select_kernel, 'select', flops=10 ** 9, nbytes=6 * 10 ** 6, in_specs...  0.99 us
  transfers between devices with their start and end apart: 7, of which 0 were waited for; matrix products, arithmetic and copies ran while one was open for 0% of the time, Pallas kernels for 35%

profile of v9, /device:TPU:0, one launch (start us, length us, event | category | flops | bytes accessed | tf_op | source)
XLA Modules:
  0.0 18.8 jit_solution(4550184918024437090)
XLA Ops:
  0.6 0.5 %collective-permute-start = (bf16[128,2560]{1,0:T(8,128)(2,1)}, bf16[128,2560]{1,0:T(8,128)(2,1)S(1)}, u32[]{:S(2)}, u32[]{:S(2)}) collective-permute-start(bf16[128,2560]{1,0:T(8,128)(2,1)} %x_hbm.1), channel_id=1, source_target_pairs={{0,1},{1,0},{2,3},{3,2},{4,5},{5,4},{6,7},{7,6},{8,9},{9,8},{10,11... | collective-permute-start | bytes 1966088 | tf_op jit(solution)/shard_map/ppermute | solution.py:436
  1.1 2.2 %plan.1 = (bf16[20,2,128,256]{3,2,1,0:T(8,128)(2,1)S(1)}, f32[20,128,128]{2,1,0:T(8,128)S(1)}, bf16[20,2,128,128]{3,2,1,0:T(8,128)(2,1)S(1)}, bf16[256,128]{1,0:...) custom-call(s32[4,8,80]{2,1,0:T(8,128)} %bitcast.7, f32[64,128]{1,0:T(8,128)} %constant.6.clone.tab_hbm, ...), custom_call_target="tpu_custom_call" | custom-call | flops 2000000000 | bytes 4000000 | tf_op jit(solution)/shard_map/plan/pallas_call | solution.py:150
  3.4 0.0 collective-permute-done.peer_ref.refs_6_
  3.4 0.0 copy-start
  3.4 1.0 %select.1.refs_7_ = f32[4,8,80]{2,1,0:T(8,128)S(1)} custom-call(s32[1]{0:T(128)} %bitcast.t_ref.refs_0_, bf16[20,2,128,256]{3,2,1,0:T(8,128)(2,1)S(1)} %get-tuple-element.35.sel_ref, f32[20,128,128]{2,1,0:T(8,128)S(1)} %get-tuple-element.31.sec_ref.refs_2_, bf16[256,5120]{1,0:T(8,128)(2,1)S(1)} %get-tuple-element.33.m_ref.refs_4_, ...), custom_call_target="tpu_custom_call" | custom-call | flops 1000000000 | bytes 6000000 | tf_op jit(solution)/shard_map/select/pallas_call | solution.py:204
  4.4 2.7 %collective-permute-start.2 = (f32[4,8,80]{2,1,0:T(8,128)S(1)}, f32[4,8,80]{2,1,0:T(8,128)S(1)}, u32[]{:S(2)}, u32[]{:S(2)}) collective-permute-start(f32[4,8,80]{2,1,0:T(8,128)S(1)} %select.1.refs_7_), channel_id=1, source_target_pairs={{0,3},{1,2},{2,1},{3,0},{4,7},{5,6},{6,5},{7,4},{8,11},{9,10},{10,... | collective-permute-start | bytes 30728 | tf_op jit(solution)/shard_map/ppermute | solution.py:450
  7.1 0.1 collective-permute-start.1
  7.1 0.0 copy-done
  7.1 1.3 %keys.1 = (bf16[128,256]{1,0:T(8,128)(2,1)S(1)}, bf16[256,2688]{1,0:T(8,128)(2,1)S(1)}, bf16[256,1536]{1,0:T(8,128)(2,1)S(1)}) custom-call(s32[1]{0:T(128)} %bitcast.t_ref.refs_0_, bf16[20,2,128,128]{3,2,1,0:T(8,128)(2,1)S(1)} %get-tuple-element.30.refs_1_.lt_ref, f32[20,128,128]{2,1,0:T(8,128)S(1)} %get-tuple-element.31.sec_ref.refs_2_, ...), custom_call_target="tpu_custom_call" | custom-call | flops 1000000000 | bytes 4000000 | tf_op jit(solution)/shard_map/keys/pallas_call | solution.py:297
  8.5 0.0 collective-permute-done.2
  8.5 0.0 collective-permute-done.1
  8.5 1.8 %collective-permute-start.3 = (f32[4,8,80]{2,1,0:T(8,128)S(1)}, f32[4,8,80]{2,1,0:T(8,128)S(1)}, u32[]{:S(2)}, u32[]{:S(2)}) collective-permute-start(f32[4,8,80]{2,1,0:T(8,128)S(1)} %add.6), channel_id=1, source_target_pairs={{0,4},{2,6},{4,0},{6,2},{8,12},{10,14},{12,8},{14,10},{1,5},{3,7},... | collective-permute-start | bytes 30728 | tf_op jit(solution)/shard_map/ppermute | solution.py:451
  10.3 0.2 collective-permute-start.6
  10.5 0.0 copy-start.1
  10.5 1.8 %remain.1 = (bf16[128,256]{1,0:T(8,128)(2,1)}, bf16[256,5120]{1,0:T(8,128)(2,1)}, bf16[256,512]{1,0:T(8,128)(2,1)S(1)}) custom-call(s32[1]{0:T(128)} %bitcast.t_ref.refs_0_, bf16[20,2,128,128]{3,2,1,0:T(8,128)(2,1)S(1)} %get-tuple-element.30.refs_1_.lt_ref, f32[20,128,128]{2,1,0:T(8,128)S(1)} %get-tuple-element.31.sec_ref.refs_2_, ...), custom_call_target="tpu_custom_call" | custom-call | flops 20000000000 | bytes 8000000 | tf_op jit(solution)/shard_map/remain/pallas_call | solution.py:331
  12.3 0.0 collective-permute-done.3
  12.3 2.6 %collective-permute-start.5 = (f32[4,8,80]{2,1,0:T(8,128)S(1)}, f32[4,8,80]{2,1,0:T(8,128)S(1)}, u32[]{:S(2)}, u32[]{:S(2)}) collective-permute-start(f32[4,8,80]{2,1,0:T(8,128)S(1)} %add.7.refs_11_), channel_id=1, source_target_pairs={{0,9},{1,8},{2,11},{3,10},{4,13},{5,12},{6,15},{7,14},{8,1},{9,0},... | collective-permute-start | bytes 30728 | tf_op jit(solution)/shard_map/ppermute | solution.py:450
  14.9 0.3 %collective-permute-start.4 = (f32[4,8,80]{2,1,0:T(8,128)S(1)}, f32[4,8,80]{2,1,0:T(8,128)S(1)}, u32[]{:S(2)}, u32[]{:S(2)}) collective-permute-start(f32[4,8,80]{2,1,0:T(8,128)S(1)} %add.7.refs_11_), channel_id=1, source_target_pairs={{0,1},{1,0},{2,3},{3,2},{4,5},{5,4},{6,7},{7,6},{8,9},{9,8},{10,11... | collective-permute-start | bytes 30728 | tf_op jit(solution)/shard_map/ppermute | solution.py:450
  15.2 0.0 copy-done.1
  15.2 1.3 %finish.1 = (bf16[256,5120]{1,0:T(8,128)(2,1)}, f32[128,2560]{1,0:T(8,128)S(1)}) custom-call(s32[1]{0:T(128)} %bitcast.t_ref.refs_0_, bf16[20,2,128,128]{3,2,1,0:T(8,128)(2,1)S(1)} %get-tuple-element.30.refs_1_.lt_ref, f32[20,128,128]{2,1,0:T(8,128)S(1)} %get-tuple-element.31.sec_ref.refs_2_, ...), custom_call_target="tpu_custom_call", output_to_operand_aliasing={{0}: (12, {})} | custom-call | flops 1000000000 | bytes 8000000 | tf_op jit(solution)/shard_map/finish/pallas_call | solution.py:369
  16.5 0.0 collective-permute-done.5.far_ref
  16.5 0.0 collective-permute-done.4.near_ref
  16.5 0.0 collective-permute-done.6.wp_ref
  16.5 2.3 %update.1 = (bf16[256,5120]{1,0:T(8,128)(2,1)}, f32[4,8,80]{2,1,0:T(8,128)}, bf16[128,2560]{1,0:T(8,128)(2,1)}) custom-call(bf16[20,2,128,128]{3,2,1,0:T(8,128)(2,1)S(1)} %get-tuple-element.30.refs_1_.lt_ref, f32[20,128,128]{2,1,0:T(8,128)S(1)} %get-tuple-element.31.sec_ref.refs_2_, f32[4,8,80]{2,1,0:T(8,128)S(1)} %collective-permute-done.4.near_ref, ...), custom_call_target="tpu_custom_call" | custom-call | flops 1000000000 | bytes 6000000 | tf_op jit(solution)/shard_map/update/pallas_call | solution.py:411
  (2 shorter events, 0.0 us)
Async XLA Ops:
  0.6 2.8 %collective-permute-start = (bf16[128,2560]{1,0:T(8,128)(2,1)}, bf16[128,2560]{1,0:T(8,128)(2,1)S(1)}, u32[]{:S(2)}, u32[]{:S(2)}) collective-permute-start(bf16[128,2560]{1,0:T(8,128)(2,1)} %x_hbm.1), channel_id=1, source_target_pairs={{0,1},{1,0},{2,3},{3,2},{4,5},{5,4},{6,7},{7,6},{8,9},{9,8},{10,11... | collective-permute-start | bytes 1966088 | tf_op jit(solution)/shard_map/ppermute | solution.py:436
  3.4 3.8 %copy-start = (bf16[256,5120]{1,0:T(8,128)(2,1)S(1)}, bf16[256,5120]{1,0:T(8,128)(2,1)}, u32[]{:S(2)}) copy-start(bf16[256,5120]{1,0:T(8,128)(2,1)} %refs_10_.1) | copy-start | bytes 7864324
  4.4 4.1 %collective-permute-start.2 = (f32[4,8,80]{2,1,0:T(8,128)S(1)}, f32[4,8,80]{2,1,0:T(8,128)S(1)}, u32[]{:S(2)}, u32[]{:S(2)}) collective-permute-start(f32[4,8,80]{2,1,0:T(8,128)S(1)} %select.1.refs_7_), channel_id=1, source_target_pairs={{0,3},{1,2},{2,1},{3,0},{4,7},{5,6},{6,5},{7,4},{8,11},{9,10},{10,... | collective-permute-start | bytes 30728 | tf_op jit(solution)/shard_map/ppermute | solution.py:450
  7.1 1.4 %collective-permute-start.1 = (f32[4,8,80]{2,1,0:T(8,128)S(1)}, f32[4,8,80]{2,1,0:T(8,128)S(1)}, u32[]{:S(2)}, u32[]{:S(2)}) collective-permute-start(f32[4,8,80]{2,1,0:T(8,128)S(1)} %select.1.refs_7_), channel_id=1, source_target_pairs={{0,1},{1,0},{2,3},{3,2},{4,5},{5,4},{6,7},{7,6},{8,9},{9,8},{10,11... | collective-permute-start | bytes 30728 | tf_op jit(solution)/shard_map/ppermute | solution.py:450
  8.5 3.8 %collective-permute-start.3 = (f32[4,8,80]{2,1,0:T(8,128)S(1)}, f32[4,8,80]{2,1,0:T(8,128)S(1)}, u32[]{:S(2)}, u32[]{:S(2)}) collective-permute-start(f32[4,8,80]{2,1,0:T(8,128)S(1)} %add.6), channel_id=1, source_target_pairs={{0,4},{2,6},{4,0},{6,2},{8,12},{10,14},{12,8},{14,10},{1,5},{3,7},... | collective-permute-start | bytes 30728 | tf_op jit(solution)/shard_map/ppermute | solution.py:451
  10.3 6.2 %collective-permute-start.6 = (bf16[256,2688]{1,0:T(8,128)(2,1)S(1)}, bf16[256,2688]{1,0:T(8,128)(2,1)S(1)}, u32[]{:S(2)}, u32[]{:S(2)}) collective-permute-start(bf16[256,2688]{1,0:T(8,128)(2,1)S(1)} %get-tuple-element.50), channel_id=1, source_target_pairs={{0,1},{1,0},{2,3},{3,2},{4,5},{5,4},{6,7},{7,6},{8,9},{9,8},{10,11... | collective-permute-start | bytes 4128776 | tf_op jit(solution)/shard_map/ppermute | solution.py:461
  10.5 4.7 %copy-start.1 = (bf16[128,256]{1,0:T(8,128)(2,1)S(1)}, bf16[128,256]{1,0:T(8,128)(2,1)}, u32[]{:S(2)}) copy-start(bf16[128,256]{1,0:T(8,128)(2,1)} %refs_9_.1) | copy-start | bytes 196612
  12.3 4.2 %collective-permute-start.5 = (f32[4,8,80]{2,1,0:T(8,128)S(1)}, f32[4,8,80]{2,1,0:T(8,128)S(1)}, u32[]{:S(2)}, u32[]{:S(2)}) collective-permute-start(f32[4,8,80]{2,1,0:T(8,128)S(1)} %add.7.refs_11_), channel_id=1, source_target_pairs={{0,9},{1,8},{2,11},{3,10},{4,13},{5,12},{6,15},{7,14},{8,1},{9,0},... | collective-permute-start | bytes 30728 | tf_op jit(solution)/shard_map/ppermute | solution.py:450
  14.9 1.6 %collective-permute-start.4 = (f32[4,8,80]{2,1,0:T(8,128)S(1)}, f32[4,8,80]{2,1,0:T(8,128)S(1)}, u32[]{:S(2)}, u32[]{:S(2)}) collective-permute-start(f32[4,8,80]{2,1,0:T(8,128)S(1)} %add.7.refs_11_), channel_id=1, source_target_pairs={{0,1},{1,0},{2,3},{3,2},{4,5},{5,4},{6,7},{7,6},{8,9},{9,8},{10,11... | collective-permute-start | bytes 30728 | tf_op jit(solution)/shard_map/ppermute | solution.py:450
